TPU v7x, 32 devices: a whole 2x2x4 slice. The times are simulated.
32 devices in a mesh: groups: 2 (over y), src: 4 (over z), tgt: 2 (over x), dir: 2 (over core).
Axes of the slice: x: 2, y: 2, z: 4, core: 2. Of those that a mesh axis runs over, the one named last changes fastest.
Arguments:
- incident: bfloat16 [2, 64, 4096], P(None, 'dir', ('groups', 'src')), parts along dimension 2, may hold values from -6 to 6
- near_blocks: bfloat16 [8, 2, 56, 2, 128, 128], P(('groups', 'src'), 'tgt'), parts along dimension 0, may hold values from -0.25 to 0.25
- near_src: int32 [8, 2, 56], P(('groups', 'src'), 'tgt'), parts along dimension 0, may hold values from 0 to 3
- near_tgt: int32 [8, 2, 56], P(('groups', 'src'), 'tgt'), parts along dimension 0, may hold values from 0 to 15, as said below
- far_v: bfloat16 [8, 2, 32, 2, 32, 128], P(('groups', 'src'), 'tgt'), parts along dimension 0, may hold values from -0.5 to 0.5
- far_src: int32 [8, 2, 32], P(('groups', 'src'), 'tgt'), parts along dimension 0, may hold values from 0 to 3
- far_dst: int32 [8, 2, 32], P(('groups', 'src'), 'tgt'), parts along dimension 0, may hold values from 0 to 127, as said below
- far_u: bfloat16 [8, 2, 32, 2, 32, 128], P(('groups', 'src'), 'tgt'), parts along dimension 0, may hold values from -0.75 to 0.75
- far_tgt: int32 [8, 2, 32], P(('groups', 'src'), 'tgt'), parts along dimension 0, may hold values from 0 to 3
Outputs:
- potential: float32 [2, 64, 4096], P(None, 'dir', ('groups', 'src', 'tgt')), parts along dimension 2
There are 2 independent parts, one for each index of `groups`. A program takes and returns all parts, laid end to end along the dimension named above; each array names one. Nothing has to cross between parts.
Inputs may be any that keep to these rules, and one draw needn't show every extreme that they name: Near block (s, t, b) aims at owner near_tgt // 4. The near blocks of one device aimed at one owner other than s number at most 2 and reach at most 1 distinct target cluster; in every draw some owner receives exactly 2 near blocks from every device of every other owner. `far_dst`: value v names owner v // 32 and slot v % 32 at the same tgt index. Among the devices of one tgt index every value occurs exactly once; one device sends exactly 8 far blocks or none to each owner.
All inputs are finite; a program needn't handle non-finite values.
Results may differ from a plain program's by a relative error of at most 0.0025.
Values may be sent and summed in bfloat16 or wider, within the bound.
No kernel may reach another device: no remote copies, remote signals or barrier semaphores. Data moves between devices by JAX's collectives and lax.ppermute only.
A program may use at most 64 MiB of HBM per device.

v0:
```python
import jax
import jax.numpy as jnp
from jax import lax
from jax.sharding import PartitionSpec as P

PANEL = 128
CAP = 2


def complex_apply(operand, matrices, pattern):
    products = jnp.einsum(pattern, operand, matrices, preferred_element_type=jnp.float32)
    return jnp.stack(
        [products[:, 0, 0] - products[:, 1, 1], products[:, 1, 0] + products[:, 0, 1]], axis=1
    )


def place_rows(targets, owners, slot_depth):
    position = jnp.arange(targets.shape[0], dtype=jnp.int32)
    earlier = (targets[:, None] == targets[None, :]) & (position[:, None] < position[None, :])
    rank_in = jnp.sum(earlier.astype(jnp.int32), axis=0)
    slot_of = jnp.where(targets >= 0, targets * slot_depth + rank_in, -1)
    slot_hits = slot_of[None, :] == jnp.arange(owners * slot_depth, dtype=jnp.int32)[:, None]
    chosen = jnp.sum(slot_hits.astype(jnp.int32) * position[None, :], axis=1)
    return (chosen, jnp.any(slot_hits, axis=1))


def cluster_sum(labels, values, clusters):
    one_hot = (labels[None, :] == jnp.arange(clusters, dtype=jnp.int32)[:, None]).astype(
        jnp.float32
    )
    return jnp.einsum("lr,radp->adlp", one_hot, values, precision=lax.Precision.HIGHEST)


def body(incident, near_blocks, near_src, near_tgt, far_v, far_src, far_dst, far_u, far_tgt):
    owners = lax.axis_size("src")
    my_owner = lax.axis_index("src")
    half_dirs = incident.shape[1]
    own_clusters = incident.shape[2] // PANEL
    source = incident.reshape(2, half_dirs, own_clusters, PANEL)
    blocks = near_blocks.reshape((-1,) + near_blocks.shape[3:])
    near_from = near_src.reshape(-1)
    near_to = near_tgt.reshape(-1)
    picked = jnp.take(source, near_from, axis=2)
    partial_value = complex_apply(picked, blocks, "adbq,bcpq->bacdp")
    dest_owner = near_to // own_clusters
    local_cluster = near_to % own_clusters
    is_mine = dest_owner == my_owner
    remote = jnp.where(is_mine, -1, dest_owner)
    own_sum = cluster_sum(jnp.where(is_mine, local_cluster, -1), partial_value, own_clusters)
    chosen, filled = place_rows(remote, owners, CAP)
    outgoing = jnp.where(filled[:, None, None, None], partial_value[chosen], 0.0)
    labels = jnp.where(filled, local_cluster[chosen], -1)
    arrived, arrived_labels = (
        lax.all_to_all(
            outgoing.reshape(owners, CAP, 2, half_dirs, PANEL),
            "src",
            split_axis=0,
            concat_axis=0,
            tiled=True,
        ),
        lax.all_to_all(labels.reshape(owners, CAP), "src", split_axis=0, concat_axis=0, tiled=True),
    )
    arrived_rows = arrived.reshape((-1, 2, half_dirs, PANEL))
    near_in = cluster_sum(arrived_labels.reshape(-1), arrived_rows, own_clusters)
    far_count = far_v.shape[2]
    far_from = far_src.reshape(-1)
    far_factors = far_v.reshape((-1,) + far_v.shape[3:])
    coefficients = complex_apply(
        jnp.take(source, far_from, axis=2), far_factors, "adbq,bckq->bacdk"
    ).astype(jnp.bfloat16)
    routed = far_dst.reshape(-1)
    slot_depth = max(2, far_count // owners)
    chosen_far, filled_far = place_rows(routed // far_count, owners, slot_depth)
    outgoing_far = jnp.where(filled_far[:, None, None, None], coefficients[chosen_far], 0)
    slot_far = jnp.where(filled_far, routed[chosen_far] % far_count, -1)
    received, received_slot = (
        lax.all_to_all(
            outgoing_far.reshape((owners, slot_depth) + coefficients.shape[1:]),
            "src",
            split_axis=0,
            concat_axis=0,
            tiled=True,
        ),
        lax.all_to_all(
            slot_far.reshape(owners, slot_depth), "src", split_axis=0, concat_axis=0, tiled=True
        ),
    )
    received_slot = received_slot.reshape(-1)
    slot_match = received_slot[None, :] == jnp.arange(far_count, dtype=jnp.int32)[:, None]
    row_index = jnp.sum(
        slot_match.astype(jnp.int32) * jnp.arange(received_slot.shape[0], dtype=jnp.int32)[None, :],
        axis=1,
    )
    matched = jnp.take(received.reshape((-1,) + coefficients.shape[1:]), row_index, axis=0)
    potential = complex_apply(matched, far_u.reshape((-1,) + far_u.shape[3:]), "badk,bckp->bacdp")
    far_in = cluster_sum(far_tgt.reshape(-1), potential, own_clusters)
    cluster_total = own_sum + near_in + far_in
    result = lax.psum_scatter(cluster_total, "tgt", scatter_dimension=2, tiled=True)
    return result.reshape(2, half_dirs, -1)


def solution(mesh):
    placed = (
        P(None, "dir", ("groups", "src")),
        P(("groups", "src"), "tgt", None, None, None, None),
        P(("groups", "src"), "tgt", None),
        P(("groups", "src"), "tgt", None),
        P(("groups", "src"), "tgt", None, None, None, None),
        P(("groups", "src"), "tgt", None),
        P(("groups", "src"), "tgt", None),
        P(("groups", "src"), "tgt", None, None, None, None),
        P(("groups", "src"), "tgt", None),
    )
    return jax.shard_map(
        body,
        mesh=mesh,
        in_specs=placed,
        out_specs=P(None, "dir", ("groups", "src", "tgt")),
        check_vma=False,
    )
```

profile of v0, /device:TPU:0, one launch (start us, length us, event | category | flops | bytes accessed | tf_op | source)
XLA Modules:
  0.0 88.7 jit_solution(1472638785312227239)
XLA Ops:
  6.5 0.7 compare_select_fusion.9
  7.3 0.1 convert_reduce_fusion
  7.4 0.1 select_reduce_fusion.2
  7.5 0.1 fusion.46
  7.6 0.6 gather_fusion.2
  8.3 0.7 select_n.224
  8.9 6.3 %all-to-all-start.1 = ((s32[4,1,2]{2,1,0:T(1,128)}), s32[4,1,2]{2,1,0:T(1,128)S(1)}, u32[]{:S(2)}, u32[]{:S(2)}) async-start(s32[4,1,2]{2,1,0:T(1,128)} %bitcast.19), calls=%async_computation.1 | async-start | bytes 4096 | tf_op jit(solution)/shard_map/all_to_all | solution.py:61
  15.3 0.7 fusion.59
  15.9 0.7 compare_and_fusion.2
  16.6 0.8 copy_bitcast_fusion.1
  17.4 0.7 gather_fusion
  18.2 3.5 %fusion.2 = f32[56,2,2,32,128]{4,3,2,1,0:T(8,128)S(1)} fusion(bf16[1,1,56,2,128,128]{5,4,3,2,1,0:T(8,128)(2,1)} %param.10, bf16[56,2,32,128]{3,2,1,0:T(8,128)(2,1)S(1)} %gather_fusion, pred[56]{0:T(512)(128)(4,1)S(1)} %compare_and_fusion.2), kind=kOutput, calls=%fused_computation.9 | convolution fusion | flops 235339776 | bytes 8257592 | tf_op jit(solution)/shard_map/adbq,bcpq->bacdp/dot_general | solution.py:11
  21.7 0.2 fusion.18
  21.8 0.0 copy-start.2
  21.9 1.1 %fusion.20 = f32[56,1,32,128]{3,2,0,1:T(8,128)} fusion(f32[56,2,2,32,128]{4,3,2,1,0:T(8,128)S(1)} %fusion.2), kind=kLoop, calls=%fused_computation.25 | loop fusion | flops 229376 | bytes 2752512 | tf_op jit(solution)/shard_map/sub | solution.py:13
  23.0 0.1 broadcast_in_dim.100
  23.1 0.6 gather_fusion.4
  23.7 1.0 %convolution_bitcast_fusion.1 = f32[32,2,2,32,32]{4,3,2,1,0:T(8,128)S(1)} fusion(bf16[1,1,32,2,32,128]{5,4,3,2,1,0:T(8,128)(2,1)S(1)} %copy-done.2, bf16[32,2,32,128]{3,2,1,0:T(8,128)(2,1)S(1)} %gather_fusion.4, pred[32]{0:T(512)(128)(4,1)S(1)} %compare_and_fusion), kind=kOutput, calls=%fused_computation.14 | convolution fusion | flops 33816576 | bytes 1572896 | tf_op jit(solution)/shard_map/adbq,bckq->bacdk/dot_general | solution.py:11
  24.8 0.0 copy-start.1
  24.8 0.8 fusion.39
  25.6 0.8 fusion.40
  26.4 0.1 convert_reduce_fusion.1
  26.5 0.1 select_reduce_fusion.1
  26.6 0.1 fusion.44
  26.7 0.1 broadcast_in_dim.106
  26.8 0.1 reduce_or.22
  26.9 1.4 %pad_maximum_fusion = f32[56,2,32,128]{3,2,0,1:T(8,128)S(1)} fusion(f32[56,1,32,128]{3,2,0,1:T(8,128)S(1)} %fusion.18, f32[56,1,32,128]{3,2,0,1:T(8,128)} %fusion.20), kind=kLoop, calls=%fused_computation.10 | loop fusion | flops 458752 | bytes 3670016 | tf_op jit(solution)/shard_map/stack | solution.py:12
  28.2 1.3 %gather_fusion.1 = f32[8,2,32,128]{3,2,1,0:T(8,128)} fusion(f32[56,2,32,128]{3,2,0,1:T(8,128)S(1)} %pad_maximum_fusion, s32[1024]{0:T(1024)S(1)} %pad_clamp_fusion.3), kind=kCustom, calls=%fused_computation.1 | custom fusion | bytes 524320 | tf_op jit(solution)/shard_map/gather | solution.py:51
  29.5 1.1 %pad_maximum_fusion.2 = bf16[32,2,32,32]{3,2,0,1:T(8,128)(2,1)S(1)} fusion(bf16[32,1,32,32]{3,2,0,1:T(8,128)(2,1)} %fusion.40, bf16[32,1,32,32]{3,2,0,1:T(8,128)(2,1)} %fusion.39), kind=kLoop, calls=%fused_computation.42 | loop fusion | flops 65536 | bytes 262144 | tf_op jit(solution)/shard_map/stack | solution.py:12
  30.7 0.6 gather_fusion.5
  31.3 0.1 broadcast_select_fusion
  31.4 1.2 %reshape.635 = bf16[4,2,8192]{2,1,0:T(2,128)(2,1)} reshape(bf16[4,8,2,32,32]{4,3,2,1,0:T(8,128)(2,1)S(1)} %broadcast_select_fusion) | data formatting | bytes 262144
  32.6 0.7 gather_fusion.3
  33.3 0.1 gather.35
  33.4 1.7 %broadcast_select_fusion.1 = f32[4,2,2,32,128]{4,3,2,1,0:T(8,128)} fusion(f32[4,2,2,32,128]{4,3,2,1,0:T(8,128)} %bitcast.177, pred[4,2]{1,0:T(4,128)(4,1)S(1)} %broadcast_in_dim.100), kind=kLoop, calls=%fused_computation.57 | loop fusion | flops 65536 | bytes 524296 | tf_op jit(solution)/shard_map/jit(_where)/select_n | solution.py:51
  35.1 0.6 fusion.48
  35.7 5.1 %all-to-all-start.2 = ((s32[4,1,8]{2,1,0:T(1,128)}), s32[4,1,8]{2,1,0:T(1,128)S(1)}, u32[]{:S(2)}, u32[]{:S(2)}) async-start(s32[4,1,8]{2,1,0:T(1,128)} %bitcast.25), calls=%async_computation.2 | async-start | bytes 4096 | tf_op jit(solution)/shard_map/all_to_all | solution.py:84
  40.8 0.6 broadcast.502
  41.4 0.6 reduce.7
  42.0 0.1 eq.141
  42.1 4.2 %all-to-all-done.2 = s32[4,1,8]{2,1,0:T(1,128)S(1)} async-done(((s32[4,1,8]{2,1,0:T(1,128)}), s32[4,1,8]{2,1,0:T(1,128)S(1)}, u32[]{:S(2)}, u32[]{:S(2)}) %all-to-all-start.2) | async-done | bytes 160 | tf_op jit(solution)/shard_map/all_to_all | solution.py:84
  46.3 3.3 %all-to-all-start.3 = ((bf16[4,2,8192]{2,1,0:T(2,128)(2,1)}), bf16[4,2,8192]{2,1,0:T(2,128)(2,1)S(1)}, u32[]{:S(2)}, u32[]{:S(2)}) async-start(bf16[4,2,8192]{2,1,0:T(2,128)(2,1)} %reshape.635), calls=%async_computation.3 | async-start | bytes 262144 | tf_op jit(solution)/shard_map/all_to_all | solution.py:77
  49.6 0.6 reduce.6
  50.3 0.1 eq.150
  50.4 0.1 select_reduce_fusion
  50.5 5.0 %all-to-all-done.3 = bf16[4,2,8192]{2,1,0:T(2,128)(2,1)S(1)} async-done(((bf16[4,2,8192]{2,1,0:T(2,128)(2,1)}), bf16[4,2,8192]{2,1,0:T(2,128)(2,1)S(1)}, u32[]{:S(2)}, u32[]{:S(2)}) %all-to-all-start.3) | async-done | bytes 131104 | tf_op jit(solution)/shard_map/all_to_all | solution.py:77
  55.5 4.0 %all-to-all-start = ((f32[4,2,2,32,128]{4,3,2,1,0:T(8,128)}), f32[4,2,2,32,128]{4,3,2,1,0:T(8,128)}, u32[]{:S(2)}, u32[]{:S(2)}) async-start(f32[4,2,2,32,128]{4,3,2,1,0:T(8,128)} %broadcast_select_fusion.1), calls=%async_computation | async-start | bytes 524288 | tf_op jit(solution)/shard_map/all_to_all | solution.py:54
  59.6 0.0 reduce-scatter.2.cloned.1.call-start
  59.6 0.3 reshape.636
  59.9 0.6 gather_fusion.6
  60.5 0.5 convolution_bitcast_fusion
  61.0 0.1 fusion.24
  61.1 0.1 fusion.26
  61.2 0.1 pad_maximum_fusion.1
  61.3 0.5 copy-done.3
  61.8 1.0 %fusion.16 = f32[2,32,128,4]{2,3,1,0:T(4,128)S(1)} fusion(f32[32,2,32,128]{3,2,0,1:T(8,128)S(1)} %pad_maximum_fusion.1, s32[32]{0:T(128)S(1)} %bitcast.179), kind=kOutput, calls=%fused_computation.19 | convolution fusion | flops 12583040 | bytes 1179776 | tf_op jit(solution)/shard_map/lr,radp->adlp/dot_general | solution.py:31
  62.8 3.6 %all-to-all-done = f32[4,2,2,32,128]{4,3,2,1,0:T(8,128)} async-done(((f32[4,2,2,32,128]{4,3,2,1,0:T(8,128)}), f32[4,2,2,32,128]{4,3,2,1,0:T(8,128)}, u32[]{:S(2)}, u32[]{:S(2)}) %all-to-all-start) | async-done | bytes 262176 | tf_op jit(solution)/shard_map/all_to_all | solution.py:54
  66.4 1.2 %copy.72 = f32[4,2,2,32,128]{4,1,0,3,2:T(2,128)S(1)} copy(f32[4,2,2,32,128]{4,3,2,1,0:T(8,128)} %all-to-all-done) | data formatting | bytes 524288 | tf_op jit(solution)/shard_map/all_to_all | solution.py:54
  67.6 0.2 fusion.52
  67.8 1.7 %fusion.13 = f32[2,32,4,128]{3,2,1,0:T(4,128)S(1)} fusion(f32[2,32,128,4]{2,3,1,0:T(4,128)S(1)} %fusion.16, f32[2,32,128,4]{2,3,1,0:T(4,128)S(1)} %fusion.52, f32[56,2,32,128]{3,2,0,1:T(8,128)S(1)} %pad_maximum_fusion, s32[56]{0:T(128)S(1)} %get-tuple-element.5), kind=kOutput, calls=%fused_computation.17 | convolution fusion | flops 22085856 | bytes 2228448 | tf_op jit(solution)/shard_map/lr,radp->adlp/dot_general | solution.py:31
  69.5 0.6 copy.81
  70.2 0.0 reduce-scatter.2.cloned.1.call-update
  70.2 10.2 %reduce-scatter.2.cloned.1.call-done = f32[2,32,2,128]{3,1,0,2:T(8,128)} async-done(((f32[2,32,4,128]{3,1,0,2:T(8,128)}), f32[2,32,2,128]{3,1,0,2:T(8,128)}) %reduce-scatter.2.cloned.1.call-update) | async-done | bytes 65552 | tf_op jit(solution)/shard_map/reduce_scatter | solution.py:98
  80.4 1.5 %copy_bitcast_fusion = f32[2,32,256]{2,1,0:T(8,128)} fusion(f32[2,32,2,128]{3,1,0,2:T(8,128)} %reduce-scatter.2.cloned.1.call-done), kind=kLoop, calls=%fused_computation.58 | loop fusion | bytes 131072 | tf_op jit(solution)/shard_map/reshape | solution.py:99
  (24 shorter events, 0.1 us)
Async XLA Ops:
  6.5 54.0 %copy-start = (bf16[1,1,32,2,32,128]{5,4,3,2,1,0:T(8,128)(2,1)S(1)}, bf16[1,1,32,2,32,128]{5,4,3,2,1,0:T(8,128)(2,1)}, u32[]{:S(2)}) copy-start(bf16[1,1,32,2,32,128]{5,4,3,2,1,0:T(8,128)(2,1)} %param.16) | copy-start | bytes 1572868
  8.9 26.8 %all-to-all-start.1 = ((s32[4,1,2]{2,1,0:T(1,128)}), s32[4,1,2]{2,1,0:T(1,128)S(1)}, u32[]{:S(2)}, u32[]{:S(2)}) async-start(s32[4,1,2]{2,1,0:T(1,128)} %bitcast.19), calls=%async_computation.1 | async-start | bytes 4096 | tf_op jit(solution)/shard_map/all_to_all | solution.py:61
  21.7 1.4 %copy-start.4 = (s32[1,1,32]{2,1,0:T(1,128)S(1)}, s32[1,1,32]{2,1,0:T(1,128)}, u32[]{:S(2)}) copy-start(s32[1,1,32]{2,1,0:T(1,128)} %param.14) | copy-start | bytes 388
  21.8 1.9 %copy-start.2 = (bf16[1,1,32,2,32,128]{5,4,3,2,1,0:T(8,128)(2,1)S(1)}, bf16[1,1,32,2,32,128]{5,4,3,2,1,0:T(8,128)(2,1)}, u32[]{:S(2)}) copy-start(bf16[1,1,32,2,32,128]{5,4,3,2,1,0:T(8,128)(2,1)} %param.13) | copy-start | bytes 1572868
  24.8 1.6 %copy-start.1 = (s32[1,1,32]{2,1,0:T(1,128)S(1)}, s32[1,1,32]{2,1,0:T(1,128)}, u32[]{:S(2)}) copy-start(s32[1,1,32]{2,1,0:T(1,128)} %param.15) | copy-start | bytes 388
  35.7 10.6 %all-to-all-start.2 = ((s32[4,1,8]{2,1,0:T(1,128)}), s32[4,1,8]{2,1,0:T(1,128)S(1)}, u32[]{:S(2)}, u32[]{:S(2)}) async-start(s32[4,1,8]{2,1,0:T(1,128)} %bitcast.25), calls=%async_computation.2 | async-start | bytes 4096 | tf_op jit(solution)/shard_map/all_to_all | solution.py:84
  46.3 9.2 %all-to-all-start.3 = ((bf16[4,2,8192]{2,1,0:T(2,128)(2,1)}), bf16[4,2,8192]{2,1,0:T(2,128)(2,1)S(1)}, u32[]{:S(2)}, u32[]{:S(2)}) async-start(bf16[4,2,8192]{2,1,0:T(2,128)(2,1)} %reshape.635), calls=%async_computation.3 | async-start | bytes 262144 | tf_op jit(solution)/shard_map/all_to_all | solution.py:77
  55.5 10.9 %all-to-all-start = ((f32[4,2,2,32,128]{4,3,2,1,0:T(8,128)}), f32[4,2,2,32,128]{4,3,2,1,0:T(8,128)}, u32[]{:S(2)}, u32[]{:S(2)}) async-start(f32[4,2,2,32,128]{4,3,2,1,0:T(8,128)} %broadcast_select_fusion.1), calls=%async_computation | async-start | bytes 524288 | tf_op jit(solution)/shard_map/all_to_all | solution.py:54
  59.6 20.9 %reduce-scatter.2.cloned.1.call-start = ((), (), s32[]{:S(2)}) async-start(), calls=%async_computation.5 | async-start | bytes 196608 | tf_op jit(solution)/shard_map/reduce_scatter | solution.py:98
  61.1 0.7 copy-start.3
Sparse Core Ops, SparseCore 0:
  70.3 10.0 reduce-scatter.1
where the time goes:
time: 89.4 us; the launch traced here: 88.7 us
  waiting for transfers between devices  23 us (26%)
  starting transfers between devices  18.8 us (21%)
  between operations  13.7 us (15%)
  local copies, waits for them, and re-layouts  13.1 us (15%)
  other arithmetic  12.2 us (14%)
  matrix products  7.98 us (9%)
    reduce_scatter x1, waiting for transfers between devices, body(): lax.psum_scatter(cluster_total, 'tgt', scatter_dimension=2, tiled=True)  10.2 us
    all_to_all x1, starting transfers between devices, body(): lax.all_to_all(labels.reshape(owners, CAP), 'src', split_axis=0, concat_a...  6.32 us
    all_to_all x1, starting transfers between devices, body(): lax.all_to_all(slot_far.reshape(owners, slot_depth), 'src', split_axis=0,...  5.09 us
    all_to_all x1, waiting for transfers between devices, body(): lax.all_to_all(outgoing_far.reshape((owners, slot_depth) + coefficients.s...  5.01 us
    dot_general x3, matrix products, complex_apply(): jnp.einsum(pattern, operand, matrices, preferred_element_type=jnp.float32)  4.97 us
    all_to_all x1, waiting for transfers between devices, body(): lax.all_to_all(slot_far.reshape(owners, slot_depth), 'src', split_axis=0,...  4.17 us
    all_to_all x1, starting transfers between devices, body(): lax.all_to_all(outgoing.reshape(owners, CAP, 2, half_dirs, PANEL), 'src',...  4.04 us
    all_to_all x1, waiting for transfers between devices, body(): lax.all_to_all(outgoing.reshape(owners, CAP, 2, half_dirs, PANEL), 'src',...  3.57 us
  transfers between devices with their start and end apart: 5, of which 4 were waited for; matrix products, arithmetic and copies ran while one was open for 28% of the time, Pallas kernels for 0%

commit v1 on v0

v1 whole, which is shorter than its diff:
```python
import functools

import jax
import jax.numpy as jnp
from jax import lax
from jax.experimental import pallas as pl
from jax.experimental.pallas import tpu as pltpu
from jax.sharding import PartitionSpec as P

PANEL = 128
LANES = 128
LABEL_ROWS = 16
LIMIT = 24 << 20
VMEM = pl.BlockSpec(memory_space=pltpu.VMEM)
SMEM = pl.BlockSpec(memory_space=pltpu.SMEM)
PARAMS = pltpu.CompilerParams(vmem_limit_bytes=LIMIT)


def div_by(value, size):
    if size & (size - 1) == 0:
        return lax.shift_right_logical(value, jnp.int32(size.bit_length() - 1))
    return lax.div(value, jnp.int32(size))


def ahead_of(owner, me, owners):
    ahead = owner - me
    return jnp.where(ahead < 0, ahead + owners, ahead)


def dot_nt(left, right):
    return lax.dot_general(left, right, (((1,), (1,)), ((), ())), preferred_element_type=jnp.float32)


def dot_nn(left, right):
    return jnp.dot(left, right, preferred_element_type=jnp.float32)


def coeff_kernel(owners, depth, far_src, far_dst, incident, far_v, field, labels, *rest):
    outs, (ordered, source_of) = rest[:owners], rest[owners:]
    me = lax.axis_index("src")
    clusters = incident.shape[2] // PANEL
    half = incident.shape[1]
    rows = 2 * half
    blocks, rank = far_v.shape[2], far_v.shape[4]
    per_chunk = LANES // rank
    lane = lax.broadcasted_iota(jnp.int32, (1, LANES), 1)
    for s in range(clusters):
        real, imag = (incident[c, :, s * PANEL:(s + 1) * PANEL] for c in range(2))
        field[s * rows:s * rows + half, :] = jnp.concatenate([real, -imag], axis=1)
        field[s * rows + half:(s + 1) * rows, :] = jnp.concatenate([imag, real], axis=1)
    if owners * depth != blocks:
        ordered[...] = jnp.zeros_like(ordered)
        for place in range(owners * depth):
            source_of[place] = 0
    counts = [jnp.int32(0)] * owners
    label_row = jnp.full((1, LANES), -1, jnp.int32)
    for f in range(blocks):
        routed = far_dst[0, 0, f]
        owner = div_by(routed, blocks)
        slot = routed - owner * blocks
        ahead = ahead_of(owner, me, owners)
        taken = jnp.int32(0)
        for k in range(owners):
            taken = jnp.where(ahead == k, counts[k], taken)
            counts[k] = jnp.where(ahead == k, counts[k] + 1, counts[k])
        place = ahead * depth + taken
        at = pl.ds(pl.multiple_of(place * rank, rank), rank)
        ordered[at, 0:PANEL] = far_v[0, 0, f, 0]
        ordered[at, PANEL:2 * PANEL] = far_v[0, 0, f, 1]
        source_of[place] = far_src[0, 0, f]
        label_row = jnp.where(lane == place, slot, label_row)
    labels[...] = jnp.broadcast_to(label_row, (8, LANES))
    group = lane // rank
    everything = field[...]
    for chunk in range(owners * depth // per_chunk):
        source = jnp.zeros((1, LANES), jnp.int32)
        for at in range(per_chunk):
            source = jnp.where(group == at, source_of[chunk * per_chunk + at], source)
        product = dot_nt(everything, ordered[chunk * LANES:(chunk + 1) * LANES, :])
        chosen = product[0:rows]
        for s in range(1, clusters):
            chosen = jnp.where(source == s, product[s * rows:(s + 1) * rows], chosen)
        chunks = depth // per_chunk
        at = chunk % chunks
        outs[chunk // chunks][at * rows:(at + 1) * rows, :] = chosen.astype(jnp.bfloat16)


def near_out_kernel(owners, near_src, near_tgt, near_row, field, labels, near_blocks, *rest):
    coeffs, outs = rest[:owners - 1], rest[owners - 1:]
    me = lax.axis_index("src")
    rows = outs[0].shape[0] - LABEL_ROWS - coeffs[0].shape[0]
    clusters = field.shape[0] // rows
    count = near_row.shape[2]
    targets = near_row[0]
    position = lax.broadcasted_iota(jnp.int32, targets.shape, 1)
    lane = lax.broadcasted_iota(jnp.int32, (1, LANES), 1)
    near_labels = jnp.full((1, LANES), -1, jnp.int32)
    for k in range(1, owners):
        owner = me + k
        owner = jnp.where(owner >= owners, owner - owners, owner)
        low = owner * clusters
        aimed = (targets >= low) & (targets < low + clusters)
        first = jnp.min(jnp.where(aimed, position, count))
        last = jnp.max(jnp.where(aimed, position, -1))
        filled = last >= 0
        first = jnp.minimum(first, count - 1)
        final = jnp.maximum(last, 0)
        cluster = jnp.where(filled, near_tgt[0, 0, first] - low, -1)
        near_labels = jnp.where(lane == k, cluster, near_labels)
        total = None
        for at, used in ((first, filled), (final, last > first)):
            source = pl.ds(pl.multiple_of(near_src[0, 0, at] * rows, rows), rows)
            matrix = jnp.concatenate([near_blocks[0, 0, at, 0], near_blocks[0, 0, at, 1]], axis=1)
            part = jnp.where(used, dot_nt(field[source, :], matrix), 0.0)
            total = part if total is None else total + part
        depth_rows = coeffs[k - 1].shape[0]
        outs[k - 1][0:depth_rows, :] = coeffs[k - 1][...]
        outs[k - 1][depth_rows:depth_rows + rows, :] = total.astype(jnp.bfloat16)
    far_part = labels[0:8, :].astype(jnp.float32)
    near_part = jnp.broadcast_to(near_labels, (8, LANES)).astype(jnp.float32)
    label_tile = jnp.concatenate([far_part, near_part], axis=0).astype(jnp.bfloat16)
    for k in range(1, owners):
        outs[k - 1][outs[k - 1].shape[0] - LABEL_ROWS:, :] = label_tile


def near_own_kernel(near_src, near_tgt, field, near_blocks, total):
    me = lax.axis_index("src")
    clusters = total.shape[0] - 1
    rows = total.shape[1]
    total[...] = jnp.zeros_like(total)
    for b in range(near_blocks.shape[2]):
        target = near_tgt[0, 0, b] - me * clusters
        target = jnp.where((target >= 0) & (target < clusters), target, clusters)
        source = pl.ds(pl.multiple_of(near_src[0, 0, b] * rows, rows), rows)
        matrix = jnp.concatenate([near_blocks[0, 0, b, 0], near_blocks[0, 0, b, 1]], axis=1)
        total[target] += dot_nt(field[source, :], matrix)


def pick(vector, where):
    return jnp.sum(jnp.where(where, vector, 0))


def target_kernel(owners, depth, used, sharers, steps, far_tgt, labels, own_coeffs, far_u, total, *rest):
    messages = rest[:owners - 1]
    outs = rest[owners - 1:owners - 1 + len(steps)]
    right = rest[owners - 1 + len(steps)]
    clusters = total.shape[0] - 1
    rows = total.shape[1]
    half = rows // 2
    share = clusters // sharers
    blocks, rank = far_u.shape[2], far_u.shape[4]
    chunks = depth * rank // LANES
    me = lax.axis_index("tgt")
    lane = lax.broadcasted_iota(jnp.int32, (1, LANES), 1)
    bases = []
    for step in steps:
        holder = me + step
        holder = jnp.where(holder >= sharers, holder - sharers, holder)
        bases.append(holder * share)
    width = share * PANEL
    sums = [jnp.concatenate([total[base + c] for c in range(share)], axis=1) for base in bases]
    for k in range(owners):
        if k == 0:
            far_labels = labels[0:1, :]
            coeffs = own_coeffs
        else:
            message = messages[k - 1]
            tile = message[message.shape[0] - LABEL_ROWS:, :].astype(jnp.float32)
            far_labels = tile[0:1].astype(jnp.int32)
            near_label = pick(tile[8:9].astype(jnp.int32), lane == k)
            coeffs = message
            near = message[chunks * rows:(chunks + 1) * rows, :].astype(jnp.float32)
            for i, base in enumerate(bases):
                sums[i] = sums[i] + jnp.concatenate(
                    [jnp.where(near_label == base + c, near, 0.0) for c in range(share)], axis=1)
        values = jnp.concatenate([coeffs[c * rows:(c + 1) * rows, :] for c in range(chunks)], axis=1)
        crossed = jnp.concatenate([-values[half:rows], values[0:half]], axis=0)
        spread = depth * rank
        for r in range(depth):
            if r < used:
                slot = pick(far_labels, lane == k * depth + r)
                known = slot >= 0
                slot = jnp.maximum(slot, 0)
                cluster = jnp.where(known, far_tgt[0, 0, slot], -1)
            for part in range(2):
                at = (k * 2 + part) * spread + r * rank
                for i, base in enumerate(bases):
                    for c in range(share):
                        to = i * width + c * PANEL
                        if r < used:
                            factor = far_u[0, 0, slot, part]
                            factor = jnp.where(cluster == base + c, factor, jnp.zeros_like(factor))
                        else:
                            factor = jnp.zeros((rank, PANEL), jnp.bfloat16)
                        right[at:at + rank, to:to + PANEL] = factor
        for part, left in enumerate((values, crossed)):
            at = (k * 2 + part) * spread
            product = dot_nn(left, right[at:at + spread, :])
            for i in range(len(bases)):
                sums[i] = sums[i] + product[:, i * width:(i + 1) * width]
    for i, out in enumerate(outs):
        out[...] = sums[i].astype(out.dtype).reshape(out.shape)


def body(incident, near_blocks, near_src, near_tgt, far_v, far_src, far_dst, far_u, far_tgt):
    owners = lax.axis_size("src")
    sharers = lax.axis_size("tgt")
    half = incident.shape[1]
    rows = 2 * half
    clusters = incident.shape[2] // PANEL
    share = clusters // sharers
    blocks, rank = far_v.shape[2], far_v.shape[4]
    used = max(2, blocks // owners)
    per_chunk = LANES // rank
    depth = -(-used // per_chunk) * per_chunk
    chunks = depth // per_chunk
    bf16, f32, i32 = jnp.bfloat16, jnp.float32, jnp.int32

    def shape(dims, dtype):
        return jax.ShapeDtypeStruct(dims, dtype)

    field, labels, *coeffs = pl.pallas_call(
        functools.partial(coeff_kernel, owners, depth),
        out_shape=[shape((clusters * rows, 2 * PANEL), bf16), shape((8, LANES), i32)]
        + [shape((chunks * rows, LANES), bf16)] * owners,
        in_specs=[SMEM, SMEM, VMEM, VMEM],
        out_specs=[VMEM] * (2 + owners),
        scratch_shapes=[
            pltpu.VMEM((owners * depth * rank, 2 * PANEL), bf16),
            pltpu.SMEM((owners * depth,), i32),
        ],
        compiler_params=PARAMS,
        name="coefficients",
    )(far_src, far_dst, incident, far_v)
    messages = pl.pallas_call(
        functools.partial(near_out_kernel, owners),
        out_shape=[shape(((chunks + 1) * rows + LABEL_ROWS, LANES), bf16)] * (owners - 1),
        in_specs=[SMEM, SMEM] + [VMEM] * (3 + owners),
        out_specs=[VMEM] * (owners - 1),
        compiler_params=PARAMS,
        name="near_out",
    )(near_src, near_tgt, near_tgt, field, labels, near_blocks, *coeffs[1:])
    arrived = [
        lax.ppermute(message, "src", [(s, (s + k) % owners) for s in range(owners)])
        for k, message in enumerate(messages, 1)
    ]
    total = pl.pallas_call(
        near_own_kernel,
        out_shape=shape((clusters + 1, rows, PANEL), f32),
        in_specs=[SMEM, SMEM, VMEM, VMEM],
        out_specs=VMEM,
        compiler_params=PARAMS,
        cost_estimate=pl.CostEstimate(flops=2 * 56 * 256 * 128 * 64 * 8, bytes_accessed=4 << 20, transcendentals=0),
        name="near_own",
    )(near_src, near_tgt, field, near_blocks)

    def target(steps, dtype, dims):
        return pl.pallas_call(
            functools.partial(target_kernel, owners, depth, used, sharers, steps),
            out_shape=[shape(dims, dtype)] * len(steps),
            in_specs=[SMEM] + [VMEM] * (4 + owners - 1),
            out_specs=[VMEM] * len(steps),
            scratch_shapes=[pltpu.VMEM((owners * 2 * depth * rank, len(steps) * share * PANEL), bf16)],
            compiler_params=PARAMS,
            name="target_other" if steps[0] else "target_mine",
        )(far_tgt, labels, coeffs[0], far_u, total, *arrived)

    result = None
    if sharers > 1:
        others = target(tuple(range(1, sharers)), bf16, (rows, share * PANEL))
        received = [
            lax.ppermute(other, "tgt", [(t, (t + k) % sharers) for t in range(sharers)])
            for k, other in enumerate(others, 1)
        ]
    else:
        received = []
    (result,) = target((0,), f32, (2, half, share * PANEL))
    for other in received:
        result = result + other.astype(f32).reshape(result.shape)
    return result


def solution(mesh):
    placed = (
        P(None, "dir", ("groups", "src")),
        P(("groups", "src"), "tgt", None, None, None, None),
        P(("groups", "src"), "tgt", None),
        P(("groups", "src"), "tgt", None),
        P(("groups", "src"), "tgt", None, None, None, None),
        P(("groups", "src"), "tgt", None),
        P(("groups", "src"), "tgt", None),
        P(("groups", "src"), "tgt", None, None, None, None),
        P(("groups", "src"), "tgt", None),
    )
    return jax.shard_map(
        body,
        mesh=mesh,
        in_specs=placed,
        out_specs=P(None, "dir", ("groups", "src", "tgt")),
        check_vma=False,
    )
```

time: 89.4 us -> 24.9 us (0.28)
  waiting for transfers between devices: 23 us -> 2.17 us
  between operations: 13.7 us -> 0.07 us
  other arithmetic: 12.2 us -> 0.64 us
  starting transfers between devices: 18.8 us -> 8.71 us
  matrix products: 7.98 us -> 0 us
  local copies, waits for them, and re-layouts: 13.1 us -> 6.55 us
  Pallas kernels: 0 us -> 6.45 us
    all_to_all x4 -> x0, starting transfers between devices: 18.8 us -> none  [the longest x1 6.32 us: body(): lax.all_to_all(labels.reshape(owners, CAP), 'src', split_axis=0, concat_a...]
    all_to_all x4 -> x0, waiting for transfers between devices: 12.8 us -> none  [the longest x1 5.01 us: body(): lax.all_to_all(outgoing_far.reshape((owners, slot_depth) + coefficients.s...]
    reduce_scatter x1 -> x0, waiting for transfers between devices: 10.2 us -> none  [body(): lax.psum_scatter(cluster_total, 'tgt', scatter_dimension=2, tiled=True)]
    ppermute x0 -> x4, starting transfers between devices: none -> 8.71 us  [the longest x3 7.02 us: body(): lax.ppermute(message, 'src', [(s, (s + k) % owners) for s in range(owners)])]
    dot_general x6 -> x0, matrix products: 7.98 us -> none  [the longest x3 4.97 us: complex_apply(): jnp.einsum(pattern, operand, matrices, preferred_element_type=jnp.float32)]
    pallas_call x0 -> x5, Pallas kernels: none -> 6.45 us  [the longest x2 2.3 us: target(): pl.pallas_call(functools.partial(target_kernel, owners, depth, used, shar...]
    gather x8 -> x0, local copies, waits for them, and re-layouts: 5.35 us -> none  [the longest x1 1.26 us: body(): partial_value[chosen]]
    unnamed x12 -> x22, local copies, waits for them, and re-layouts: 1.94 us -> 6.55 us
  transfers between devices with their start and end apart: 5 -> 4, of which waited for: 4 -> 3; matrix products, arithmetic and copies ran while one was open for 28% -> 0% of each run, Pallas kernels for 0% -> 12%
where the time goes in v1:
time: 24.9 us; the launch traced here: 24.6 us
  starting transfers between devices  8.71 us (35%)
  local copies, waits for them, and re-layouts  6.55 us (26%)
  Pallas kernels  6.45 us (26%)
  waiting for transfers between devices  2.17 us (9%)
  other arithmetic  0.64 us (3%)
    ppermute x3, starting transfers between devices, body(): lax.ppermute(message, 'src', [(s, (s + k) % owners) for s in range(owners)])  7.02 us
    unnamed x22, local copies, waits for them, and re-layouts  6.55 us
    pallas_call x2, Pallas kernels, target(): pl.pallas_call(functools.partial(target_kernel, owners, depth, used, shar...  2.3 us
    pallas_call x1, Pallas kernels, body(): pl.pallas_call(near_own_kernel, out_shape=shape((clusters + 1, rows, PANE...  1.86 us
    ppermute x1, starting transfers between devices, body(): lax.ppermute(other, 'tgt', [(t, (t + k) % sharers) for t in range(sharers)])  1.69 us
    pallas_call x1, Pallas kernels, body(): pl.pallas_call(functools.partial(coeff_kernel, owners, depth), out_shape=...  1.27 us
    ppermute x1, waiting for transfers between devices, body(): lax.ppermute(other, 'tgt', [(t, (t + k) % sharers) for t in range(sharers)])  1.13 us
    ppermute x3, waiting for transfers between devices, body(): lax.ppermute(message, 'src', [(s, (s + k) % owners) for s in range(owners)])  1.04 us
  transfers between devices with their start and end apart: 4, of which 3 were waited for; matrix products, arithmetic and copies ran while one was open for 0% of the time, Pallas kernels for 12%

profile of v1, /device:TPU:0, one launch (start us, length us, event | category | flops | bytes accessed | tf_op | source)
XLA Modules:
  0.0 24.6 jit_solution(14210484368245239688)
XLA Ops:
  0.0 0.0 copy-start.3
  0.0 1.0 %copy-done.3 = bf16[1,1,32,2,32,128]{5,4,3,2,1,0:T(8,128)(2,1)S(1)} copy-done((bf16[1,1,32,2,32,128]{5,4,3,2,1,0:T(8,128)(2,1)S(1)}, bf16[1,1,32,2,32,128]{5,4,3,2,1,0:T(8,128)(2,1)}, u32[]{:S(2)}) %copy-start.3) | copy-done | bytes 524312
  1.0 0.0 copy-start.4
  1.0 0.8 %copy-done.4 = bf16[2,32,512]{2,1,0:T(8,128)(2,1)S(1)} copy-done((bf16[2,32,512]{2,1,0:T(8,128)(2,1)S(1)}, bf16[2,32,512]{2,1,0:T(8,128)(2,1)}, u32[]{:S(2)}) %copy-start.4) | copy-done | bytes 65560
  1.9 0.0 copy-start.8
  1.9 0.7 %copy-done.8 = s32[1,1,32]{2,1,0:T(1,128)S(1)} copy-done((s32[1,1,32]{2,1,0:T(1,128)S(1)}, s32[1,1,32]{2,1,0:T(1,128)}, u32[]{:S(2)}) %copy-start.8) | copy-done | bytes 152
  2.5 0.0 copy-start.9
  2.5 0.7 %copy-done.9 = s32[1,1,32]{2,1,0:T(1,128)S(1)} copy-done((s32[1,1,32]{2,1,0:T(1,128)S(1)}, s32[1,1,32]{2,1,0:T(1,128)}, u32[]{:S(2)}) %copy-start.9) | copy-done | bytes 152
  3.2 0.0 copy-start.7
  3.2 1.3 %coefficients.1 = (bf16[256,256]{1,0:T(8,128)(2,1)S(1)}, s32[8,128]{1,0:T(8,128)S(1)}, bf16[128,128]{1,0:T(8,128)(2,1)S(1)}, bf16[128,128]{1,0:T(8,128)(2,1)S(1)...) custom-call(s32[1,1,32]{2,1,0:T(1,128)S(1)} %copy-done.8, s32[1,1,32]{2,1,0:T(1,128)S(1)} %copy-done.9, ...), custom_call_target="tpu_custom_call" | custom-call | tf_op jit(solution)/shard_map/coefficients/pallas_call | solution.py:222
  4.5 0.0 copy-start
  4.5 2.0 %copy-done = bf16[1,1,56,2,128,128]{5,4,3,2,1,0:T(8,128)(2,1)S(1)} copy-done((bf16[1,1,56,2,128,128]{5,4,3,2,1,0:T(8,128)(2,1)S(1)}, bf16[1,1,56,2,128,128]{5,4,3,2,1,0:T(8,128)(2,1)}, u32[]{:S(2)}) %copy-start) | copy-done | bytes 3670040
  6.5 0.0 copy-start.6
  6.5 0.7 %copy-done.6 = s32[1,1,56]{2,1,0:T(1,128)S(1)} copy-done((s32[1,1,56]{2,1,0:T(1,128)S(1)}, s32[1,1,56]{2,1,0:T(1,128)}, u32[]{:S(2)}) %copy-start.6) | copy-done | bytes 248
  7.2 0.0 copy-start.10
  7.2 0.7 %copy-done.10 = s32[1,1,56]{2,1,0:T(1,128)S(1)} copy-done((s32[1,1,56]{2,1,0:T(1,128)S(1)}, s32[1,1,56]{2,1,0:T(1,128)}, u32[]{:S(2)}) %copy-start.10) | copy-done | bytes 248
  7.8 0.0 copy-start.1
  7.8 1.0 %near_out.1 = (bf16[208,128]{1,0:T(8,128)(2,1)S(1)}, bf16[208,128]{1,0:T(8,128)(2,1)S(1)}, bf16[208,128]{1,0:T(8,128)(2,1)S(1)}) custom-call(s32[1,1,56]{2,1,0:T(1,128)S(1)} %copy-done.10, s32[1,1,56]{2,1,0:T(1,128)S(1)} %copy-done.6, s32[1,1,56]{2,1,0:T(1,128)S(1)} %copy-done.6, bf16[256,256]{1,0:T(8,128)(2,1)S(1)} %get-tuple-element.16.field, ...), custom_call_target="tpu_custom_call" | custom-call | tf_op jit(solution)/shard_map/near_out/pallas_call | solution.py:235
  8.9 0.0 copy-start.2
  8.9 0.0 copy-start.5
  8.9 3.1 %collective-permute-start = (bf16[208,128]{1,0:T(8,128)(2,1)S(1)}, bf16[208,128]{1,0:T(8,128)(2,1)S(1)}, u32[]{:S(2)}, u32[]{:S(2)}) collective-permute-start(bf16[208,128]{1,0:T(8,128)(2,1)S(1)} %get-tuple-element.20), channel_id=1, source_target_pairs={{0,4},{4,8},{8,12},{12,0},{1,5},{5,9},{9,13},{13,1},{2,6},{6,10},{... | collective-permute-start | bytes 159752 | tf_op jit(solution)/shard_map/ppermute | solution.py:244
  12.0 2.6 %collective-permute-start.1 = (bf16[208,128]{1,0:T(8,128)(2,1)S(1)}, bf16[208,128]{1,0:T(8,128)(2,1)S(1)}, u32[]{:S(2)}, u32[]{:S(2)}) collective-permute-start(bf16[208,128]{1,0:T(8,128)(2,1)S(1)} %get-tuple-element.21), channel_id=1, source_target_pairs={{0,8},{4,12},{8,0},{12,4},{1,9},{5,13},{9,1},{13,5},{2,10},{6,14},... | collective-permute-start | bytes 159752 | tf_op jit(solution)/shard_map/ppermute | solution.py:244
  14.5 1.4 %collective-permute-start.2 = (bf16[208,128]{1,0:T(8,128)(2,1)S(1)}, bf16[208,128]{1,0:T(8,128)(2,1)S(1)}, u32[]{:S(2)}, u32[]{:S(2)}) collective-permute-start(bf16[208,128]{1,0:T(8,128)(2,1)S(1)} %get-tuple-element.22), channel_id=1, source_target_pairs={{0,12},{4,0},{8,4},{12,8},{1,13},{5,1},{9,5},{13,9},{2,14},{6,2},{... | collective-permute-start | bytes 159752 | tf_op jit(solution)/shard_map/ppermute | solution.py:244
  15.9 0.0 copy-done.7
  15.9 0.0 copy-done.1
  15.9 1.9 %near_own.1.total = f32[5,64,128]{2,1,0:T(8,128)S(1)} custom-call(s32[1,1,56]{2,1,0:T(1,128)S(1)} %copy-done.10, s32[1,1,56]{2,1,0:T(1,128)S(1)} %copy-done.7, bf16[256,256]{1,0:T(8,128)(2,1)S(1)} %get-tuple-element.16.field, bf16[1,1,56,2,128,128]{5,4,3,2,1,0:T(8,128)(2,1)S(1)} %copy-done.1), custom_call_target="tpu_custom_call" | custom-call | flops 1879048192 | bytes 4194304 | tf_op jit(solution)/shard_map/near_own/pallas_call | solution.py:247
  17.8 0.0 collective-permute-done.rest_0_
  17.8 0.6 %collective-permute-done.1.rest_1_ = bf16[208,128]{1,0:T(8,128)(2,1)S(1)} collective-permute-done((bf16[208,128]{1,0:T(8,128)(2,1)S(1)}, bf16[208,128]{1,0:T(8,128)(2,1)S(1)}, u32[]{:S(2)}, u32[]{:S(2)}) %collective-permute-start.1) | collective-permute-done | bytes 53280 | tf_op jit(solution)/shard_map/ppermute | solution.py:244
  18.4 0.4 %collective-permute-done.2.rest_2_ = bf16[208,128]{1,0:T(8,128)(2,1)S(1)} collective-permute-done((bf16[208,128]{1,0:T(8,128)(2,1)S(1)}, bf16[208,128]{1,0:T(8,128)(2,1)S(1)}, u32[]{:S(2)}, u32[]{:S(2)}) %collective-permute-start.2) | collective-permute-done | bytes 53280 | tf_op jit(solution)/shard_map/ppermute | solution.py:244
  18.8 0.0 copy-done.2
  18.8 0.0 copy-done.5
  18.8 1.1 %target_other.1 = bf16[64,256]{1,0:T(8,128)(2,1)S(1)} custom-call(s32[1,1,32]{2,1,0:T(1,128)S(1)} %copy-done.5, s32[8,128]{1,0:T(8,128)S(1)} %get-tuple-element.14.labels, bf16[128,128]{1,0:T(8,128)(2,1)S(1)} %get-tuple-element.15.own_coeffs, bf16[1,1,32,2,32,128]{5,4,3,2,1,0:T(8,128)(2,1)S(1)} %copy-done.2, f32[5,64,128]{2,1,0:T(8,128)S(1)} %near_own.1.total, ...), custom_call_target="tpu_custom_call" | custom-call | tf_op jit(solution)/shard_map/target_other/pallas_call | solution.py:258
  20.0 1.7 %collective-permute-start.3 = (bf16[64,256]{1,0:T(8,128)(2,1)S(1)}, bf16[64,256]{1,0:T(8,128)(2,1)S(1)}, u32[]{:S(2)}, u32[]{:S(2)}) collective-permute-start(bf16[64,256]{1,0:T(8,128)(2,1)S(1)} %target_other.1), channel_id=1, source_target_pairs={{0,2},{2,0},{1,3},{3,1},{4,6},{6,4},{5,7},{7,5},{8,10},{10,8},{9,1... | collective-permute-start | bytes 98312 | tf_op jit(solution)/shard_map/ppermute | solution.py:272
  21.7 1.1 %target_mine.1 = f32[2,32,256]{2,1,0:T(8,128)S(1)} custom-call(s32[1,1,32]{2,1,0:T(1,128)S(1)} %copy-done.5, s32[8,128]{1,0:T(8,128)S(1)} %get-tuple-element.14.labels, bf16[128,128]{1,0:T(8,128)(2,1)S(1)} %get-tuple-element.15.own_coeffs, bf16[1,1,32,2,32,128]{5,4,3,2,1,0:T(8,128)(2,1)S(1)} %copy-done.2, f32[5,64,128]{2,1,0:T(8,128)S(1)} %near_own.1.total, ...), custom_call_target="tpu_custom_call" | custom-call | tf_op jit(solution)/shard_map/target_mine/pallas_call | solution.py:258
  22.8 1.1 %collective-permute-done.3 = bf16[64,256]{1,0:T(8,128)(2,1)S(1)} collective-permute-done((bf16[64,256]{1,0:T(8,128)(2,1)S(1)}, bf16[64,256]{1,0:T(8,128)(2,1)S(1)}, u32[]{:S(2)}, u32[]{:S(2)}) %collective-permute-start.3) | collective-permute-done | bytes 32800 | tf_op jit(solution)/shard_map/ppermute | solution.py:272
  24.0 0.6 %convert_add_fusion = f32[2,32,256]{2,1,0:T(8,128)} fusion(f32[2,32,256]{2,1,0:T(8,128)S(1)} %target_mine.1, bf16[2,32,256]{2,1,0:T(8,128)(2,1)S(1)} %bitcast.2), kind=kLoop, calls=%fused_computation | loop fusion | flops 32768 | bytes 163840 | tf_op jit(solution)/shard_map/add | solution.py:279
Async XLA Ops:
  0.0 1.0 %copy-start.3 = (bf16[1,1,32,2,32,128]{5,4,3,2,1,0:T(8,128)(2,1)S(1)}, bf16[1,1,32,2,32,128]{5,4,3,2,1,0:T(8,128)(2,1)}, u32[]{:S(2)}) copy-start(bf16[1,1,32,2,32,128]{5,4,3,2,1,0:T(8,128)(2,1)} %far_v.1) | copy-start | bytes 1572868
  1.0 0.8 %copy-start.4 = (bf16[2,32,512]{2,1,0:T(8,128)(2,1)S(1)}, bf16[2,32,512]{2,1,0:T(8,128)(2,1)}, u32[]{:S(2)}) copy-start(bf16[2,32,512]{2,1,0:T(8,128)(2,1)} %incident.1) | copy-start | bytes 196612
  1.9 0.7 %copy-start.8 = (s32[1,1,32]{2,1,0:T(1,128)S(1)}, s32[1,1,32]{2,1,0:T(1,128)}, u32[]{:S(2)}) copy-start(s32[1,1,32]{2,1,0:T(1,128)} %far_src.1) | copy-start | bytes 388
  2.5 0.7 %copy-start.9 = (s32[1,1,32]{2,1,0:T(1,128)S(1)}, s32[1,1,32]{2,1,0:T(1,128)}, u32[]{:S(2)}) copy-start(s32[1,1,32]{2,1,0:T(1,128)} %far_dst.1) | copy-start | bytes 388
  3.2 12.7 %copy-start.7 = (s32[1,1,56]{2,1,0:T(1,128)S(1)}, s32[1,1,56]{2,1,0:T(1,128)}, u32[]{:S(2)}) copy-start(s32[1,1,56]{2,1,0:T(1,128)} %near_row.1) | copy-start | bytes 676
  4.5 2.0 %copy-start = (bf16[1,1,56,2,128,128]{5,4,3,2,1,0:T(8,128)(2,1)S(1)}, bf16[1,1,56,2,128,128]{5,4,3,2,1,0:T(8,128)(2,1)}, u32[]{:S(2)}) copy-start(bf16[1,1,56,2,128,128]{5,4,3,2,1,0:T(8,128)(2,1)} %near_blocks.3) | copy-start | bytes 11010052
  6.5 0.7 %copy-start.6 = (s32[1,1,56]{2,1,0:T(1,128)S(1)}, s32[1,1,56]{2,1,0:T(1,128)}, u32[]{:S(2)}) copy-start(s32[1,1,56]{2,1,0:T(1,128)} %near_row.1) | copy-start | bytes 676
  7.2 0.7 %copy-start.10 = (s32[1,1,56]{2,1,0:T(1,128)S(1)}, s32[1,1,56]{2,1,0:T(1,128)}, u32[]{:S(2)}) copy-start(s32[1,1,56]{2,1,0:T(1,128)} %near_src.3) | copy-start | bytes 676
  7.8 8.1 %copy-start.1 = (bf16[1,1,56,2,128,128]{5,4,3,2,1,0:T(8,128)(2,1)S(1)}, bf16[1,1,56,2,128,128]{5,4,3,2,1,0:T(8,128)(2,1)}, u32[]{:S(2)}) copy-start(bf16[1,1,56,2,128,128]{5,4,3,2,1,0:T(8,128)(2,1)} %near_blocks.3) | copy-start | bytes 11010052
  8.9 10.0 %copy-start.2 = (bf16[1,1,32,2,32,128]{5,4,3,2,1,0:T(8,128)(2,1)S(1)}, bf16[1,1,32,2,32,128]{5,4,3,2,1,0:T(8,128)(2,1)}, u32[]{:S(2)}) copy-start(bf16[1,1,32,2,32,128]{5,4,3,2,1,0:T(8,128)(2,1)} %far_u.3) | copy-start | bytes 1572868
  8.9 9.9 %copy-start.5 = (s32[1,1,32]{2,1,0:T(1,128)S(1)}, s32[1,1,32]{2,1,0:T(1,128)}, u32[]{:S(2)}) copy-start(s32[1,1,32]{2,1,0:T(1,128)} %far_tgt.3) | copy-start | bytes 388
  8.9 8.9 %collective-permute-start = (bf16[208,128]{1,0:T(8,128)(2,1)S(1)}, bf16[208,128]{1,0:T(8,128)(2,1)S(1)}, u32[]{:S(2)}, u32[]{:S(2)}) collective-permute-start(bf16[208,128]{1,0:T(8,128)(2,1)S(1)} %get-tuple-element.20), channel_id=1, source_target_pairs={{0,4},{4,8},{8,12},{12,0},{1,5},{5,9},{9,13},{13,1},{2,6},{6,10},{... | collective-permute-start | bytes 159752 | tf_op jit(solution)/shard_map/ppermute | solution.py:244
  12.0 6.4 %collective-permute-start.1 = (bf16[208,128]{1,0:T(8,128)(2,1)S(1)}, bf16[208,128]{1,0:T(8,128)(2,1)S(1)}, u32[]{:S(2)}, u32[]{:S(2)}) collective-permute-start(bf16[208,128]{1,0:T(8,128)(2,1)S(1)} %get-tuple-element.21), channel_id=1, source_target_pairs={{0,8},{4,12},{8,0},{12,4},{1,9},{5,13},{9,1},{13,5},{2,10},{6,14},... | collective-permute-start | bytes 159752 | tf_op jit(solution)/shard_map/ppermute | solution.py:244
  14.5 4.3 %collective-permute-start.2 = (bf16[208,128]{1,0:T(8,128)(2,1)S(1)}, bf16[208,128]{1,0:T(8,128)(2,1)S(1)}, u32[]{:S(2)}, u32[]{:S(2)}) collective-permute-start(bf16[208,128]{1,0:T(8,128)(2,1)S(1)} %get-tuple-element.22), channel_id=1, source_target_pairs={{0,12},{4,0},{8,4},{12,8},{1,13},{5,1},{9,5},{13,9},{2,14},{6,2},{... | collective-permute-start | bytes 159752 | tf_op jit(solution)/shard_map/ppermute | solution.py:244
  20.0 4.0 %collective-permute-start.3 = (bf16[64,256]{1,0:T(8,128)(2,1)S(1)}, bf16[64,256]{1,0:T(8,128)(2,1)S(1)}, u32[]{:S(2)}, u32[]{:S(2)}) collective-permute-start(bf16[64,256]{1,0:T(8,128)(2,1)S(1)} %target_other.1), channel_id=1, source_target_pairs={{0,2},{2,0},{1,3},{3,1},{4,6},{6,4},{5,7},{7,5},{8,10},{10,8},{9,1... | collective-permute-start | bytes 98312 | tf_op jit(solution)/shard_map/ppermute | solution.py:272

commit v2 on v0

v2 whole, which is shorter than its diff:
```python
import functools

import jax
import jax.numpy as jnp
from jax import lax
from jax.experimental import pallas as pl
from jax.experimental.pallas import tpu as pltpu
from jax.sharding import PartitionSpec as P

PANEL = 128
LANES = 128
LABEL_ROWS = 16
PACK = 4
BASE = 64
LIMIT = 24 << 20
VMEM = pl.BlockSpec(memory_space=pltpu.VMEM)
SMEM = pl.BlockSpec(memory_space=pltpu.SMEM)
HBM = pl.BlockSpec(memory_space=pltpu.HBM)
PARAMS = pltpu.CompilerParams(vmem_limit_bytes=LIMIT)


def div_by(value, size):
    if size & (size - 1) == 0:
        return lax.shift_right_logical(value, jnp.int32(size.bit_length() - 1))
    return lax.div(value, jnp.int32(size))


def wrap(value, size):
    if size & (size - 1) == 0:
        return value & (size - 1)
    return jnp.where(value < 0, value + size, jnp.where(value >= size, value - size, value))


def dot_nt(left, right):
    return lax.dot_general(left, right, (((1,), (1,)), ((), ())), preferred_element_type=jnp.float32)


def dot_nn(left, right):
    return jnp.dot(left, right, preferred_element_type=jnp.float32)


def send_kernel(owners, depth, far_src, far_dst, near_src, near_tgt, incident, far_v, near_blocks,
                field, labels, own_coeffs, *rest):
    messages, rest = rest[:owners - 1], rest[owners - 1:]
    (src_f, dst_f, src_n, tgt_n, tgt_row, waves, factors, picked, ordered, source_of, counts,
     sems, pick_sems) = rest
    me = lax.axis_index("src")
    half = waves.shape[1]
    rows = 2 * half
    clusters = waves.shape[2] // PANEL
    blocks, rank = factors.shape[2], factors.shape[4]
    count = tgt_row.shape[2]
    per_chunk = LANES // rank
    chunks = depth // per_chunk
    lane = lax.broadcasted_iota(jnp.int32, (1, LANES), 1)

    loads = [
        pltpu.make_async_copy(a, b, sems.at[i])
        for i, (a, b) in enumerate((
            (near_tgt, tgt_row), (near_tgt, tgt_n), (near_src, src_n), (far_dst, dst_f), (far_src, src_f),
            (incident, waves), (far_v, factors)))
    ]
    for load in loads:
        load.start()
    row_in, tgt_in, near_in, dst_in, far_in, waves_in, factors_in = loads

    row_in.wait()
    targets = tgt_row[0]
    position = lax.broadcasted_iota(jnp.int32, targets.shape, 1)
    chosen_near = []
    for k in range(1, owners):
        low = wrap(me + k, owners) * clusters
        aimed = (targets >= low) & (targets < low + clusters)
        first = jnp.min(jnp.where(aimed, position, count - 1))
        last = jnp.max(jnp.where(aimed, position, -1))
        final = jnp.maximum(last, 0)
        chosen_near.append((low, first, final, last >= 0, last > first))
        for i, at in enumerate((first, final)):
            pltpu.make_async_copy(
                near_blocks.at[0, 0, at], picked.at[2 * (k - 1) + i], pick_sems.at[2 * (k - 1) + i]).start()

    waves_in.wait()
    for s in range(clusters):
        real, imag = (waves[c, :, s * PANEL:(s + 1) * PANEL] for c in range(2))
        field[s * rows:s * rows + half, :] = jnp.concatenate([real, -imag], axis=1)
        field[s * rows + half:(s + 1) * rows, :] = jnp.concatenate([imag, real], axis=1)

    dst_in.wait()
    far_in.wait()
    packed = owners * 8 <= 32
    if owners * depth != blocks:
        ordered[...] = jnp.zeros_like(ordered)
        for place in range(owners * depth):
            source_of[place] = 0
    if not packed:
        for k in range(owners):
            counts[k] = 0
    so_far = jnp.int32(0)
    label_row = jnp.zeros((1, LANES), jnp.int32)
    factors_in.wait()
    for f in range(blocks):
        routed = dst_f[0, 0, f]
        owner = div_by(routed, blocks)
        slot = routed - owner * blocks
        ahead = wrap(owner - me, owners)
        if packed:
            shift = ahead * 8
            taken = lax.shift_right_logical(so_far, shift) & 255
            so_far = so_far + lax.shift_left(jnp.int32(1), shift)
        else:
            taken = counts[ahead]
            counts[ahead] = taken + 1
        place = ahead * depth + taken
        at = pl.ds(pl.multiple_of(place * rank, rank), rank)
        ordered[at, 0:PANEL] = factors[0, 0, f, 0]
        ordered[at, PANEL:2 * PANEL] = factors[0, 0, f, 1]
        source_of[place] = src_f[0, 0, f]
        label_row = jnp.where(lane == place, slot + 1, label_row)
    far_labels = jnp.broadcast_to(label_row, (8, LANES)).astype(jnp.float32)
    labels[...] = far_labels

    group = lane // rank
    everything = field[...]
    for k in range(owners):
        out = own_coeffs if k == 0 else messages[k - 1]
        product = dot_nt(everything, ordered[k * chunks * LANES:(k + 1) * chunks * LANES, :])
        for chunk in range(chunks):
            source = jnp.zeros((1, LANES), jnp.int32)
            for at in range(per_chunk):
                source = jnp.where(group == at, source_of[k * depth + chunk * per_chunk + at], source)
            part = product[:, chunk * LANES:(chunk + 1) * LANES]
            chosen = part[0:rows]
            for s in range(1, clusters):
                chosen = jnp.where(source == s, part[s * rows:(s + 1) * rows], chosen)
            out[chunk * rows:(chunk + 1) * rows, :] = chosen.astype(jnp.bfloat16)

    tgt_in.wait()
    near_in.wait()
    near_labels = jnp.zeros((1, LANES), jnp.int32)
    for k, (low, first, final, any_, two) in enumerate(chosen_near, 1):
        near_labels = jnp.where(lane == k, jnp.where(any_, tgt_n[0, 0, first] - low + 1, 0), near_labels)
        total = jnp.zeros((rows, PANEL), jnp.float32)
        for i, (at, used) in enumerate(((first, any_), (final, two))):
            pltpu.make_async_copy(
                near_blocks.at[0, 0, at], picked.at[2 * (k - 1) + i], pick_sems.at[2 * (k - 1) + i]).wait()
            source = pl.ds(pl.multiple_of(src_n[0, 0, at] * rows, rows), rows)
            matrix = jnp.concatenate([picked[2 * (k - 1) + i, 0], picked[2 * (k - 1) + i, 1]], axis=1)
            total = total + jnp.where(used, dot_nt(field[source, :], matrix), 0.0)
        messages[k - 1][chunks * rows:(chunks + 1) * rows, :] = total.astype(jnp.bfloat16)
    near_tile = jnp.broadcast_to(near_labels, (8, LANES)).astype(jnp.float32)
    tile = jnp.concatenate([far_labels, near_tile], axis=0).astype(jnp.bfloat16)
    for message in messages:
        message[(chunks + 1) * rows:, :] = tile


def read_labels(depth, used, k, far_tile, near_tile):
    lane = lax.broadcasted_iota(jnp.int32, (8, LANES), 1) - k * depth
    line = lax.broadcasted_iota(jnp.int32, (8, LANES), 0)
    weight = jnp.zeros((8, LANES), jnp.float32)
    for r in range(used):
        weight = jnp.where((lane == r) & (line == r // PACK), float(BASE ** (r % PACK)), weight)
    lines = -(-used // PACK)
    values = far_tile * weight
    if near_tile is not None:
        values = values + jnp.where((lane == k - k * depth) & (line == lines), near_tile, 0.0)
    sums = jnp.sum(values, axis=1, keepdims=True).astype(jnp.int32)
    slots = []
    for r in range(used):
        if r % PACK == 0:
            word = sums[r // PACK, 0]
        slots.append(lax.shift_right_logical(word, jnp.int32((r % PACK) * (BASE.bit_length() - 1))) & (BASE - 1))
    return slots, (sums[lines, 0] if near_tile is not None else None)


def far_operands(depth, chunks, rows, coeffs):
    half = rows // 2
    values = jnp.concatenate([coeffs[c * rows:(c + 1) * rows, :] for c in range(chunks)], axis=1)
    crossed = jnp.concatenate([-values[half:rows], values[0:half]], axis=0)
    return jnp.concatenate([values, crossed], axis=1)


def far_matrix(depth, holder, slots, spread):
    slots = slots + [0] * (depth - len(slots))
    return jnp.concatenate([spread[holder, slot, part] for part in range(2) for slot in slots], axis=0)


def own_kernel(depth, used, near_src, near_tgt, far_tgt, field, labels, own_coeffs, far_u, near_blocks,
               total, spread, sums):
    me = lax.axis_index("src")
    sharers, rows, width = total.shape
    clusters = sums.shape[0] - 1
    share = clusters // sharers
    blocks, rank = far_u.shape[2], far_u.shape[4]
    chunks = depth * rank // LANES
    sums[...] = jnp.zeros_like(sums)
    for b in range(near_blocks.shape[2]):
        target = near_tgt[0, 0, b] - me * clusters
        target = jnp.where((target >= 0) & (target < clusters), target, clusters)
        source = pl.ds(pl.multiple_of(near_src[0, 0, b] * rows, rows), rows)
        matrix = jnp.concatenate([near_blocks[0, 0, b, 0], near_blocks[0, 0, b, 1]], axis=1)
        sums[target] += dot_nt(field[source, :], matrix)
    zero = jnp.zeros((rank, PANEL), jnp.bfloat16)
    for holder in range(sharers):
        for part in range(2):
            spread[holder, 0, part] = jnp.zeros((rank, width), jnp.bfloat16)
    for slot in range(blocks):
        cluster = far_tgt[0, 0, slot]
        for part in range(2):
            factor = far_u[0, 0, slot, part]
            for c in range(clusters):
                to = (c % share) * PANEL
                spread[c // share, slot + 1, part, :, to:to + PANEL] = jnp.where(cluster == c, factor, zero)
    slots, _ = read_labels(depth, used, 0, labels[...], None)
    left = far_operands(depth, chunks, rows, own_coeffs)
    for holder in range(sharers):
        near = jnp.concatenate([sums[holder * share + c] for c in range(share)], axis=1)
        total[holder] = near + dot_nn(left, far_matrix(depth, holder, slots, spread))


def target_kernel(owners, depth, used, steps, total, spread, *rest):
    messages, outs = rest[:owners - 1], rest[owners - 1:]
    sharers, rows, width = total.shape
    share = width // PANEL
    chunks = depth * spread.shape[3] // LANES
    me = lax.axis_index("tgt")
    holders = [wrap(me + step, sharers) for step in steps]
    sums = [total[holder] for holder in holders]
    read = []
    for k, message in enumerate(messages, 1):
        tile = message[(chunks + 1) * rows:, :].astype(jnp.float32)
        read.append(read_labels(depth, used, k, tile[0:8], tile[8:16]))
    for message, (slots, label) in zip(messages, read):
        near = message[chunks * rows:(chunks + 1) * rows, :].astype(jnp.float32)
        left = far_operands(depth, chunks, rows, message)
        for i, holder in enumerate(holders):
            part = [jnp.where(label == holder * share + c + 1, near, 0.0) for c in range(share)]
            sums[i] = sums[i] + jnp.concatenate(part, axis=1)
            sums[i] = sums[i] + dot_nn(left, far_matrix(depth, holder, slots, spread))
    for out, value in zip(outs, sums):
        out[...] = value.astype(out.dtype).reshape(out.shape)


def body(incident, near_blocks, near_src, near_tgt, far_v, far_src, far_dst, far_u, far_tgt):
    owners = lax.axis_size("src")
    sharers = lax.axis_size("tgt")
    half = incident.shape[1]
    rows = 2 * half
    clusters = incident.shape[2] // PANEL
    width = clusters // sharers * PANEL
    blocks, rank = far_v.shape[2], far_v.shape[4]
    used = max(2, blocks // owners)
    per_chunk = LANES // rank
    depth = -(-used // per_chunk) * per_chunk
    chunks = depth // per_chunk
    bf16, f32, i32 = jnp.bfloat16, jnp.float32, jnp.int32
    shape = jax.ShapeDtypeStruct

    field, labels, own_coeffs, *messages = pl.pallas_call(
        functools.partial(send_kernel, owners, depth),
        out_shape=[shape((clusters * rows, 2 * PANEL), bf16), shape((8, LANES), f32), shape((chunks * rows, LANES), bf16)]
        + [shape(((chunks + 1) * rows + LABEL_ROWS, LANES), bf16)] * (owners - 1),
        in_specs=[HBM] * 7,
        out_specs=[VMEM] * (2 + owners),
        scratch_shapes=[
            pltpu.SMEM(far_src.shape, i32), pltpu.SMEM(far_dst.shape, i32),
            pltpu.SMEM(near_src.shape, i32), pltpu.SMEM(near_tgt.shape, i32),
            pltpu.VMEM(near_tgt.shape, i32),
            pltpu.VMEM(incident.shape, bf16),
            pltpu.VMEM(far_v.shape, bf16),
            pltpu.VMEM((2 * (owners - 1),) + near_blocks.shape[3:], bf16),
            pltpu.VMEM((owners * depth * rank, 2 * PANEL), bf16),
            pltpu.SMEM((owners * depth,), i32),
            pltpu.SMEM((owners,), i32),
            pltpu.SemaphoreType.DMA((7,)),
            pltpu.SemaphoreType.DMA((2 * (owners - 1),)),
        ],
        compiler_params=PARAMS,
        name="send",
    )(far_src, far_dst, near_src, near_tgt, incident, far_v, near_blocks)
    arrived = [
        lax.ppermute(message, "src", [(s, (s + k) % owners) for s in range(owners)])
        for k, message in enumerate(messages, 1)
    ]
    near_count = near_blocks.shape[2]
    total, spread = pl.pallas_call(
        functools.partial(own_kernel, depth, used),
        out_shape=[shape((sharers, rows, width), f32), shape((sharers, blocks + 1, 2, rank, width), bf16)],
        in_specs=[SMEM] * 3 + [VMEM] * 5,
        out_specs=[VMEM] * 2,
        scratch_shapes=[pltpu.VMEM((clusters + 1, rows, PANEL), f32)],
        compiler_params=PARAMS,
        cost_estimate=pl.CostEstimate(
            flops=64 * near_count * rows * PANEL * PANEL, bytes_accessed=near_count * 4 * PANEL * PANEL, transcendentals=0),
        name="own",
    )(near_src, near_tgt, far_tgt, field, labels, own_coeffs, far_u, near_blocks)

    def target(steps, dtype, dims, name):
        return pl.pallas_call(
            functools.partial(target_kernel, owners, depth, used, steps),
            out_shape=[shape(dims, dtype)] * len(steps),
            in_specs=[VMEM] * (2 + owners - 1),
            out_specs=[VMEM] * len(steps),
            compiler_params=PARAMS,
            name=name,
        )(total, spread, *arrived)

    received = []
    if sharers > 1:
        others = target(tuple(range(1, sharers)), bf16, (rows, width), "target_others")
        received = [
            lax.ppermute(other, "tgt", [(t, (t + k) % sharers) for t in range(sharers)])
            for k, other in enumerate(others, 1)
        ]
    (result,) = target((0,), f32, (2, half, width), "target_mine")
    for other in received:
        result = result + other.astype(f32).reshape(result.shape)
    return result


def solution(mesh):
    placed = (
        P(None, "dir", ("groups", "src")),
        P(("groups", "src"), "tgt", None, None, None, None),
        P(("groups", "src"), "tgt", None),
        P(("groups", "src"), "tgt", None),
        P(("groups", "src"), "tgt", None, None, None, None),
        P(("groups", "src"), "tgt", None),
        P(("groups", "src"), "tgt", None),
        P(("groups", "src"), "tgt", None, None, None, None),
        P(("groups", "src"), "tgt", None),
    )
    return jax.shard_map(
        body,
        mesh=mesh,
        in_specs=placed,
        out_specs=P(None, "dir", ("groups", "src", "tgt")),
        check_vma=False,
    )
```

time: 89.4 us -> 24.7 us (0.28)
  waiting for transfers between devices: 23 us -> 2.46 us
  between operations: 13.7 us -> 0.05 us
  other arithmetic: 12.2 us -> 0.64 us
  starting transfers between devices: 18.8 us -> 8.7 us
  matrix products: 7.98 us -> 0 us
  local copies, waits for them, and re-layouts: 13.1 us -> 6.55 us
  Pallas kernels: 0 us -> 6.01 us
    all_to_all x4 -> x0, starting transfers between devices: 18.8 us -> none  [the longest x1 6.32 us: body(): lax.all_to_all(labels.reshape(owners, CAP), 'src', split_axis=0, concat_a...]
    all_to_all x4 -> x0, waiting for transfers between devices: 12.8 us -> none  [the longest x1 5.01 us: body(): lax.all_to_all(outgoing_far.reshape((owners, slot_depth) + coefficients.s...]
    reduce_scatter x1 -> x0, waiting for transfers between devices: 10.2 us -> none  [body(): lax.psum_scatter(cluster_total, 'tgt', scatter_dimension=2, tiled=True)]
    ppermute x0 -> x4, starting transfers between devices: none -> 8.7 us  [the longest x3 7.01 us: body(): lax.ppermute(message, 'src', [(s, (s + k) % owners) for s in range(owners)])]
    dot_general x6 -> x0, matrix products: 7.98 us -> none  [the longest x3 4.97 us: complex_apply(): jnp.einsum(pattern, operand, matrices, preferred_element_type=jnp.float32)]
    pallas_call x0 -> x4, Pallas kernels: none -> 6.01 us  [the longest x1 2.91 us: body(): pl.pallas_call(functools.partial(send_kernel, owners, depth), out_shape=[...]
    gather x8 -> x0, local copies, waits for them, and re-layouts: 5.35 us -> none  [the longest x1 1.26 us: body(): partial_value[chosen]]
    unnamed x12 -> x20, local copies, waits for them, and re-layouts: 1.94 us -> 6.55 us
  transfers between devices with their start and end apart: 5 -> 4, of which waited for: 4 -> 3; matrix products, arithmetic and copies ran while one was open for 28% -> 0% of each run, Pallas kernels for 0% -> 11%
where the time goes in v2:
time: 24.7 us; the launch traced here: 24.4 us
  starting transfers between devices  8.7 us (35%)
  local copies, waits for them, and re-layouts  6.55 us (27%)
  Pallas kernels  6.01 us (24%)
  waiting for transfers between devices  2.46 us (10%)
  other arithmetic  0.64 us (3%)
    ppermute x3, starting transfers between devices, body(): lax.ppermute(message, 'src', [(s, (s + k) % owners) for s in range(owners)])  7.01 us
    unnamed x20, local copies, waits for them, and re-layouts  6.55 us
    pallas_call x1, Pallas kernels, body(): pl.pallas_call(functools.partial(send_kernel, owners, depth), out_shape=[...  2.91 us
    pallas_call x1, Pallas kernels, body(): pl.pallas_call(functools.partial(own_kernel, depth, used), out_shape=[sha...  2.34 us
    ppermute x1, waiting for transfers between devices, body(): lax.ppermute(other, 'tgt', [(t, (t + k) % sharers) for t in range(sharers)])  1.9 us
    ppermute x1, starting transfers between devices, body(): lax.ppermute(other, 'tgt', [(t, (t + k) % sharers) for t in range(sharers)])  1.69 us
    pallas_call x2, Pallas kernels, target(): pl.pallas_call(functools.partial(target_kernel, owners, depth, used, step...  0.76 us
    add x1, other arithmetic, body(): result = result + other.astype(f32).reshape(result.shape)  0.64 us
  transfers between devices with their start and end apart: 4, of which 3 were waited for; matrix products, arithmetic and copies ran while one was open for 0% of the time, Pallas kernels for 11%

profile of v2, /device:TPU:0, one launch (start us, length us, event | category | flops | bytes accessed | tf_op | source)
XLA Modules:
  0.0 24.4 jit_solution(4326665061787604030)
XLA Ops:
  0.0 0.0 copy-start
  0.0 2.0 %copy-done = bf16[1,1,56,2,128,128]{5,4,3,2,1,0:T(8,128)(2,1)S(1)} copy-done((bf16[1,1,56,2,128,128]{5,4,3,2,1,0:T(8,128)(2,1)S(1)}, bf16[1,1,56,2,128,128]{5,4,3,2,1,0:T(8,128)(2,1)}, u32[]{:S(2)}) %copy-start) | copy-done | bytes 3670040
  2.0 0.0 copy-start.2
  2.0 1.0 %copy-done.2 = bf16[1,1,32,2,32,128]{5,4,3,2,1,0:T(8,128)(2,1)S(1)} copy-done((bf16[1,1,32,2,32,128]{5,4,3,2,1,0:T(8,128)(2,1)S(1)}, bf16[1,1,32,2,32,128]{5,4,3,2,1,0:T(8,128)(2,1)}, u32[]{:S(2)}) %copy-start.2) | copy-done | bytes 524312
  3.1 0.0 copy-start.3
  3.1 0.8 %copy-done.3 = bf16[2,32,512]{2,1,0:T(8,128)(2,1)S(1)} copy-done((bf16[2,32,512]{2,1,0:T(8,128)(2,1)S(1)}, bf16[2,32,512]{2,1,0:T(8,128)(2,1)}, u32[]{:S(2)}) %copy-start.3) | copy-done | bytes 65560
  3.9 0.0 copy-start.4
  3.9 0.7 %copy-done.4 = s32[1,1,32]{2,1,0:T(1,128)S(1)} copy-done((s32[1,1,32]{2,1,0:T(1,128)S(1)}, s32[1,1,32]{2,1,0:T(1,128)}, u32[]{:S(2)}) %copy-start.4) | copy-done | bytes 152
  4.6 0.0 copy-start.5
  4.6 0.7 %copy-done.5 = s32[1,1,32]{2,1,0:T(1,128)S(1)} copy-done((s32[1,1,32]{2,1,0:T(1,128)S(1)}, s32[1,1,32]{2,1,0:T(1,128)}, u32[]{:S(2)}) %copy-start.5) | copy-done | bytes 152
  5.2 0.0 copy-start.6
  5.2 0.7 %copy-done.6 = s32[1,1,56]{2,1,0:T(1,128)S(1)} copy-done((s32[1,1,56]{2,1,0:T(1,128)S(1)}, s32[1,1,56]{2,1,0:T(1,128)}, u32[]{:S(2)}) %copy-start.6) | copy-done | bytes 248
  5.9 0.0 copy-start.7
  5.9 0.7 %copy-done.7 = s32[1,1,56]{2,1,0:T(1,128)S(1)} copy-done((s32[1,1,56]{2,1,0:T(1,128)S(1)}, s32[1,1,56]{2,1,0:T(1,128)}, u32[]{:S(2)}) %copy-start.7) | copy-done | bytes 248
  6.5 0.0 copy-start.1
  6.5 0.0 copy-start.8
  6.5 0.0 copy-start.9
  6.6 2.9 %send.1 = (bf16[256,256]{1,0:T(8,128)(2,1)S(1)}, f32[8,128]{1,0:T(8,128)S(1)}, bf16[128,128]{1,0:T(8,128)(2,1)S(1)}, bf16[208,128]{1,0:T(8,128)(2,1)S(1)}, bf16[...) custom-call(s32[1,1,32]{2,1,0:T(1,128)S(1)} %copy-done.4, s32[1,1,32]{2,1,0:T(1,128)S(1)} %copy-done.5, ...), custom_call_target="tpu_custom_call" | custom-call | tf_op jit(solution)/shard_map/send/pallas_call | solution.py:258
  9.5 3.1 %collective-permute-start = (bf16[208,128]{1,0:T(8,128)(2,1)S(1)}, bf16[208,128]{1,0:T(8,128)(2,1)S(1)}, u32[]{:S(2)}, u32[]{:S(2)}) collective-permute-start(bf16[208,128]{1,0:T(8,128)(2,1)S(1)} %get-tuple-element.18), channel_id=1, source_target_pairs={{0,4},{4,8},{8,12},{12,0},{1,5},{5,9},{9,13},{13,1},{2,6},{6,10},{... | collective-permute-start | bytes 159752 | tf_op jit(solution)/shard_map/ppermute | solution.py:281
  12.5 2.6 %collective-permute-start.1 = (bf16[208,128]{1,0:T(8,128)(2,1)S(1)}, bf16[208,128]{1,0:T(8,128)(2,1)S(1)}, u32[]{:S(2)}, u32[]{:S(2)}) collective-permute-start(bf16[208,128]{1,0:T(8,128)(2,1)S(1)} %get-tuple-element.19), channel_id=1, source_target_pairs={{0,8},{4,12},{8,0},{12,4},{1,9},{5,13},{9,1},{13,5},{2,10},{6,14},... | collective-permute-start | bytes 159752 | tf_op jit(solution)/shard_map/ppermute | solution.py:281
  15.1 1.3 %collective-permute-start.2 = (bf16[208,128]{1,0:T(8,128)(2,1)S(1)}, bf16[208,128]{1,0:T(8,128)(2,1)S(1)}, u32[]{:S(2)}, u32[]{:S(2)}) collective-permute-start(bf16[208,128]{1,0:T(8,128)(2,1)S(1)} %get-tuple-element.20), channel_id=1, source_target_pairs={{0,12},{4,0},{8,4},{12,8},{1,13},{5,1},{9,5},{13,9},{2,14},{6,2},{... | collective-permute-start | bytes 159752 | tf_op jit(solution)/shard_map/ppermute | solution.py:281
  16.5 0.0 copy-done.1
  16.5 0.0 copy-done.8
  16.5 0.0 copy-done.9
  16.5 2.3 %own.1 = (f32[2,64,256]{2,1,0:T(8,128)S(1)}, bf16[2,33,2,32,256]{4,3,2,1,0:T(8,128)(2,1)S(1)}) custom-call(s32[1,1,56]{2,1,0:T(1,128)S(1)} %copy-done.6, s32[1,1,56]{2,1,0:T(1,128)S(1)} %copy-done.7, s32[1,1,32]{2,1,0:T(1,128)S(1)} %copy-done.9, bf16[256,256]{1,0:T(8,128)(2,1)S(1)} %get-tuple-element.13.field, f32[8,128]{1,0:T(8,128)S(1)} %get-tuple-element.14.labels, ...), custom_call_target="tpu_custom_call" | custom-call | flops 3758096384 | bytes 3670016 | tf_op jit(solution)/shard_map/own/pallas_call | solution.py:285
  18.8 0.0 collective-permute-done.rest_0_
  18.8 0.1 collective-permute-done.1.rest_1_
  19.0 0.4 %collective-permute-done.2.rest_2_ = bf16[208,128]{1,0:T(8,128)(2,1)S(1)} collective-permute-done((bf16[208,128]{1,0:T(8,128)(2,1)S(1)}, bf16[208,128]{1,0:T(8,128)(2,1)S(1)}, u32[]{:S(2)}, u32[]{:S(2)}) %collective-permute-start.2) | collective-permute-done | bytes 53280 | tf_op jit(solution)/shard_map/ppermute | solution.py:281
  19.4 0.4 %target_others.1 = bf16[64,256]{1,0:T(8,128)(2,1)S(1)} custom-call(f32[2,64,256]{2,1,0:T(8,128)S(1)} %get-tuple-element.16.total, bf16[2,33,2,32,256]{4,3,2,1,0:T(8,128)(2,1)S(1)} %get-tuple-element.17.spread, bf16[208,128]{1,0:T(8,128)(2,1)S(1)} %collective-permute-done.rest_0_, bf16[208,128]{1,0:T(8,128)(2,1)S(1)} %collective-permute-done.1.rest_1_, ...), custom_call_target="tpu_custom_call" | custom-call | tf_op jit(solution)/shard_map/target_others/pallas_call | solution.py:298
  19.8 1.7 %collective-permute-start.3 = (bf16[64,256]{1,0:T(8,128)(2,1)S(1)}, bf16[64,256]{1,0:T(8,128)(2,1)S(1)}, u32[]{:S(2)}, u32[]{:S(2)}) collective-permute-start(bf16[64,256]{1,0:T(8,128)(2,1)S(1)} %target_others.1), channel_id=1, source_target_pairs={{0,2},{2,0},{1,3},{3,1},{4,6},{6,4},{5,7},{7,5},{8,10},{10,8},{9,1... | collective-permute-start | bytes 98312 | tf_op jit(solution)/shard_map/ppermute | solution.py:311
  21.5 0.4 %target_mine.1 = f32[2,32,256]{2,1,0:T(8,128)S(1)} custom-call(f32[2,64,256]{2,1,0:T(8,128)S(1)} %get-tuple-element.16.total, bf16[2,33,2,32,256]{4,3,2,1,0:T(8,128)(2,1)S(1)} %get-tuple-element.17.spread, bf16[208,128]{1,0:T(8,128)(2,1)S(1)} %collective-permute-done.rest_0_, bf16[208,128]{1,0:T(8,128)(2,1)S(1)} %collective-permute-done.1.rest_1_, ...), custom_call_target="tpu_custom_call" | custom-call | tf_op jit(solution)/shard_map/target_mine/pallas_call | solution.py:298
  21.9 1.9 %collective-permute-done.3 = bf16[64,256]{1,0:T(8,128)(2,1)S(1)} collective-permute-done((bf16[64,256]{1,0:T(8,128)(2,1)S(1)}, bf16[64,256]{1,0:T(8,128)(2,1)S(1)}, u32[]{:S(2)}, u32[]{:S(2)}) %collective-permute-start.3) | collective-permute-done | bytes 32800 | tf_op jit(solution)/shard_map/ppermute | solution.py:311
  23.8 0.6 %convert_add_fusion = f32[2,32,256]{2,1,0:T(8,128)} fusion(f32[2,32,256]{2,1,0:T(8,128)S(1)} %target_mine.1, bf16[2,32,256]{2,1,0:T(8,128)(2,1)S(1)} %bitcast.2), kind=kLoop, calls=%fused_computation | loop fusion | flops 32768 | bytes 163840 | tf_op jit(solution)/shard_map/add | solution.py:316
Async XLA Ops:
  0.0 2.0 %copy-start = (bf16[1,1,56,2,128,128]{5,4,3,2,1,0:T(8,128)(2,1)S(1)}, bf16[1,1,56,2,128,128]{5,4,3,2,1,0:T(8,128)(2,1)}, u32[]{:S(2)}) copy-start(bf16[1,1,56,2,128,128]{5,4,3,2,1,0:T(8,128)(2,1)} %near_blocks.3) | copy-start | bytes 11010052
  2.0 1.0 %copy-start.2 = (bf16[1,1,32,2,32,128]{5,4,3,2,1,0:T(8,128)(2,1)S(1)}, bf16[1,1,32,2,32,128]{5,4,3,2,1,0:T(8,128)(2,1)}, u32[]{:S(2)}) copy-start(bf16[1,1,32,2,32,128]{5,4,3,2,1,0:T(8,128)(2,1)} %far_v.1) | copy-start | bytes 1572868
  3.1 0.8 %copy-start.3 = (bf16[2,32,512]{2,1,0:T(8,128)(2,1)S(1)}, bf16[2,32,512]{2,1,0:T(8,128)(2,1)}, u32[]{:S(2)}) copy-start(bf16[2,32,512]{2,1,0:T(8,128)(2,1)} %incident.1) | copy-start | bytes 196612
  3.9 0.7 %copy-start.4 = (s32[1,1,32]{2,1,0:T(1,128)S(1)}, s32[1,1,32]{2,1,0:T(1,128)}, u32[]{:S(2)}) copy-start(s32[1,1,32]{2,1,0:T(1,128)} %far_src.1) | copy-start | bytes 388
  4.6 0.7 %copy-start.5 = (s32[1,1,32]{2,1,0:T(1,128)S(1)}, s32[1,1,32]{2,1,0:T(1,128)}, u32[]{:S(2)}) copy-start(s32[1,1,32]{2,1,0:T(1,128)} %far_dst.1) | copy-start | bytes 388
  5.2 0.7 %copy-start.6 = (s32[1,1,56]{2,1,0:T(1,128)S(1)}, s32[1,1,56]{2,1,0:T(1,128)}, u32[]{:S(2)}) copy-start(s32[1,1,56]{2,1,0:T(1,128)} %near_src.3) | copy-start | bytes 676
  5.9 0.7 %copy-start.7 = (s32[1,1,56]{2,1,0:T(1,128)S(1)}, s32[1,1,56]{2,1,0:T(1,128)}, u32[]{:S(2)}) copy-start(s32[1,1,56]{2,1,0:T(1,128)} %near_tgt.3) | copy-start | bytes 676
  6.5 9.9 %copy-start.1 = (bf16[1,1,56,2,128,128]{5,4,3,2,1,0:T(8,128)(2,1)S(1)}, bf16[1,1,56,2,128,128]{5,4,3,2,1,0:T(8,128)(2,1)}, u32[]{:S(2)}) copy-start(bf16[1,1,56,2,128,128]{5,4,3,2,1,0:T(8,128)(2,1)} %near_blocks.3) | copy-start | bytes 11010052
  6.5 9.9 %copy-start.8 = (bf16[1,1,32,2,32,128]{5,4,3,2,1,0:T(8,128)(2,1)S(1)}, bf16[1,1,32,2,32,128]{5,4,3,2,1,0:T(8,128)(2,1)}, u32[]{:S(2)}) copy-start(bf16[1,1,32,2,32,128]{5,4,3,2,1,0:T(8,128)(2,1)} %far_u.1) | copy-start | bytes 1572868
  6.5 9.9 %copy-start.9 = (s32[1,1,32]{2,1,0:T(1,128)S(1)}, s32[1,1,32]{2,1,0:T(1,128)}, u32[]{:S(2)}) copy-start(s32[1,1,32]{2,1,0:T(1,128)} %far_tgt.1) | copy-start | bytes 388
  9.5 9.4 %collective-permute-start = (bf16[208,128]{1,0:T(8,128)(2,1)S(1)}, bf16[208,128]{1,0:T(8,128)(2,1)S(1)}, u32[]{:S(2)}, u32[]{:S(2)}) collective-permute-start(bf16[208,128]{1,0:T(8,128)(2,1)S(1)} %get-tuple-element.18), channel_id=1, source_target_pairs={{0,4},{4,8},{8,12},{12,0},{1,5},{5,9},{9,13},{13,1},{2,6},{6,10},{... | collective-permute-start | bytes 159752 | tf_op jit(solution)/shard_map/ppermute | solution.py:281
  12.5 6.4 %collective-permute-start.1 = (bf16[208,128]{1,0:T(8,128)(2,1)S(1)}, bf16[208,128]{1,0:T(8,128)(2,1)S(1)}, u32[]{:S(2)}, u32[]{:S(2)}) collective-permute-start(bf16[208,128]{1,0:T(8,128)(2,1)S(1)} %get-tuple-element.19), channel_id=1, source_target_pairs={{0,8},{4,12},{8,0},{12,4},{1,9},{5,13},{9,1},{13,5},{2,10},{6,14},... | collective-permute-start | bytes 159752 | tf_op jit(solution)/shard_map/ppermute | solution.py:281
  15.1 4.3 %collective-permute-start.2 = (bf16[208,128]{1,0:T(8,128)(2,1)S(1)}, bf16[208,128]{1,0:T(8,128)(2,1)S(1)}, u32[]{:S(2)}, u32[]{:S(2)}) collective-permute-start(bf16[208,128]{1,0:T(8,128)(2,1)S(1)} %get-tuple-element.20), channel_id=1, source_target_pairs={{0,12},{4,0},{8,4},{12,8},{1,13},{5,1},{9,5},{13,9},{2,14},{6,2},{... | collective-permute-start | bytes 159752 | tf_op jit(solution)/shard_map/ppermute | solution.py:281
  19.8 4.0 %collective-permute-start.3 = (bf16[64,256]{1,0:T(8,128)(2,1)S(1)}, bf16[64,256]{1,0:T(8,128)(2,1)S(1)}, u32[]{:S(2)}, u32[]{:S(2)}) collective-permute-start(bf16[64,256]{1,0:T(8,128)(2,1)S(1)} %target_others.1), channel_id=1, source_target_pairs={{0,2},{2,0},{1,3},{3,1},{4,6},{6,4},{5,7},{7,5},{8,10},{10,8},{9,1... | collective-permute-start | bytes 98312 | tf_op jit(solution)/shard_map/ppermute | solution.py:311

commit v3 on v2

--- a/solution.py
+++ b/solution.py
@@ -276,7 +276,8 @@
         ],
         compiler_params=PARAMS,
         name="send",
-    )(far_src, far_dst, near_src, near_tgt, incident, far_v, near_blocks)
+    )(*(pltpu.with_memory_space_constraint(array, pltpu.HBM)
+        for array in (far_src, far_dst, near_src, near_tgt, incident, far_v, near_blocks)))
     arrived = [
         lax.ppermute(message, "src", [(s, (s + k) % owners) for s in range(owners)])
         for k, message in enumerate(messages, 1)

time: 24.7 us -> 18.6 us (0.75)
  local copies, waits for them, and re-layouts: 6.55 us -> 0.02 us
  Pallas kernels: 6.01 us -> 6.56 us
    unnamed x20 -> x10, local copies, waits for them, and re-layouts: 6.55 us -> 0.02 us
    pallas_call x1, Pallas kernels: 2.91 us -> 3.47 us  [body(): pl.pallas_call(functools.partial(send_kernel, owners, depth), out_shape=[...]
  transfers between devices with their start and end apart: 4 -> 4, of which waited for: 3 -> 3; matrix products, arithmetic and copies ran while one was open for 0% -> 0% of each run, Pallas kernels for 11% -> 15%
where the time goes in v3:
time: 18.6 us; the launch traced here: 18.4 us
  starting transfers between devices  8.71 us (47%)
  Pallas kernels  6.56 us (35%)
  waiting for transfers between devices  2.45 us (13%)
  other arithmetic  0.64 us (3%)
    ppermute x3, starting transfers between devices, body(): lax.ppermute(message, 'src', [(s, (s + k) % owners) for s in range(owners)])  7.01 us
    pallas_call x1, Pallas kernels, body(): pl.pallas_call(functools.partial(send_kernel, owners, depth), out_shape=[...  3.47 us
    pallas_call x1, Pallas kernels, body(): pl.pallas_call(functools.partial(own_kernel, depth, used), out_shape=[sha...  2.33 us
    ppermute x1, waiting for transfers between devices, body(): lax.ppermute(other, 'tgt', [(t, (t + k) % sharers) for t in range(sharers)])  1.9 us
    ppermute x1, starting transfers between devices, body(): lax.ppermute(other, 'tgt', [(t, (t + k) % sharers) for t in range(sharers)])  1.69 us
    pallas_call x2, Pallas kernels, target(): pl.pallas_call(functools.partial(target_kernel, owners, depth, used, step...  0.76 us
    add x1, other arithmetic, body(): result = result + other.astype(f32).reshape(result.shape)  0.64 us
    ppermute x3, waiting for transfers between devices, body(): lax.ppermute(message, 'src', [(s, (s + k) % owners) for s in range(owners)])  0.54 us
  transfers between devices with their start and end apart: 4, of which 3 were waited for; matrix products, arithmetic and copies ran while one was open for 0% of the time, Pallas kernels for 15%

profile of v3, /device:TPU:0, one launch (start us, length us, event | category | flops | bytes accessed | tf_op | source)
XLA Modules:
  0.0 18.4 jit_solution(7662189297058655785)
XLA Ops:
  0.0 0.0 copy-start.2
  0.0 0.0 copy-start.1
  0.0 0.0 copy-start
  0.0 0.0 copy-start.4
  0.0 0.0 copy-start.3
  0.0 3.5 %send.1 = (bf16[256,256]{1,0:T(8,128)(2,1)S(1)}, f32[8,128]{1,0:T(8,128)S(1)}, bf16[128,128]{1,0:T(8,128)(2,1)S(1)}, bf16[208,128]{1,0:T(8,128)(2,1)S(1)}, bf16[...) custom-call(s32[1,1,32]{2,1,0:T(1,128)} %far_src.1, s32[1,1,32]{2,1,0:T(1,128)} %far_dst.1, s32[1,1,56]{2,1,0:T(1,128)} %near_src.3, ...), custom_call_target="tpu_custom_call" | custom-call | tf_op jit(solution)/shard_map/send/pallas_call | solution.py:258
  3.5 3.1 %collective-permute-start = (bf16[208,128]{1,0:T(8,128)(2,1)S(1)}, bf16[208,128]{1,0:T(8,128)(2,1)S(1)}, u32[]{:S(2)}, u32[]{:S(2)}) collective-permute-start(bf16[208,128]{1,0:T(8,128)(2,1)S(1)} %get-tuple-element.18), channel_id=1, source_target_pairs={{0,4},{4,8},{8,12},{12,0},{1,5},{5,9},{9,13},{13,1},{2,6},{6,10},{... | collective-permute-start | bytes 159752 | tf_op jit(solution)/shard_map/ppermute | solution.py:282
  6.6 2.6 %collective-permute-start.1 = (bf16[208,128]{1,0:T(8,128)(2,1)S(1)}, bf16[208,128]{1,0:T(8,128)(2,1)S(1)}, u32[]{:S(2)}, u32[]{:S(2)}) collective-permute-start(bf16[208,128]{1,0:T(8,128)(2,1)S(1)} %get-tuple-element.19), channel_id=1, source_target_pairs={{0,8},{4,12},{8,0},{12,4},{1,9},{5,13},{9,1},{13,5},{2,10},{6,14},... | collective-permute-start | bytes 159752 | tf_op jit(solution)/shard_map/ppermute | solution.py:282
  9.2 1.3 %collective-permute-start.2 = (bf16[208,128]{1,0:T(8,128)(2,1)S(1)}, bf16[208,128]{1,0:T(8,128)(2,1)S(1)}, u32[]{:S(2)}, u32[]{:S(2)}) collective-permute-start(bf16[208,128]{1,0:T(8,128)(2,1)S(1)} %get-tuple-element.20), channel_id=1, source_target_pairs={{0,12},{4,0},{8,4},{12,8},{1,13},{5,1},{9,5},{13,9},{2,14},{6,2},{... | collective-permute-start | bytes 159752 | tf_op jit(solution)/shard_map/ppermute | solution.py:282
  10.5 0.0 copy-done.2
  10.5 0.0 copy-done.1
  10.5 0.0 copy-done
  10.5 0.0 copy-done.4
  10.5 0.0 copy-done.3
  10.5 2.3 %own.1 = (f32[2,64,256]{2,1,0:T(8,128)S(1)}, bf16[2,33,2,32,256]{4,3,2,1,0:T(8,128)(2,1)S(1)}) custom-call(s32[1,1,56]{2,1,0:T(1,128)S(1)} %copy-done.1, s32[1,1,56]{2,1,0:T(1,128)S(1)} %copy-done.2, s32[1,1,32]{2,1,0:T(1,128)S(1)} %copy-done.4, bf16[256,256]{1,0:T(8,128)(2,1)S(1)} %get-tuple-element.13.field, f32[8,128]{1,0:T(8,128)S(1)} %get-tuple-element.14.labels, ...), custom_call_target="tpu_custom_call" | custom-call | flops 3758096384 | bytes 3670016 | tf_op jit(solution)/shard_map/own/pallas_call | solution.py:286
  12.9 0.0 collective-permute-done.rest_0_
  12.9 0.1 collective-permute-done.1.rest_1_
  13.0 0.4 %collective-permute-done.2.rest_2_ = bf16[208,128]{1,0:T(8,128)(2,1)S(1)} collective-permute-done((bf16[208,128]{1,0:T(8,128)(2,1)S(1)}, bf16[208,128]{1,0:T(8,128)(2,1)S(1)}, u32[]{:S(2)}, u32[]{:S(2)}) %collective-permute-start.2) | collective-permute-done | bytes 53280 | tf_op jit(solution)/shard_map/ppermute | solution.py:282
  13.4 0.4 %target_others.1 = bf16[64,256]{1,0:T(8,128)(2,1)S(1)} custom-call(f32[2,64,256]{2,1,0:T(8,128)S(1)} %get-tuple-element.16.total, bf16[2,33,2,32,256]{4,3,2,1,0:T(8,128)(2,1)S(1)} %get-tuple-element.17.spread, bf16[208,128]{1,0:T(8,128)(2,1)S(1)} %collective-permute-done.rest_0_, bf16[208,128]{1,0:T(8,128)(2,1)S(1)} %collective-permute-done.1.rest_1_, ...), custom_call_target="tpu_custom_call" | custom-call | tf_op jit(solution)/shard_map/target_others/pallas_call | solution.py:299
  13.8 1.7 %collective-permute-start.3 = (bf16[64,256]{1,0:T(8,128)(2,1)S(1)}, bf16[64,256]{1,0:T(8,128)(2,1)S(1)}, u32[]{:S(2)}, u32[]{:S(2)}) collective-permute-start(bf16[64,256]{1,0:T(8,128)(2,1)S(1)} %target_others.1), channel_id=1, source_target_pairs={{0,2},{2,0},{1,3},{3,1},{4,6},{6,4},{5,7},{7,5},{8,10},{10,8},{9,1... | collective-permute-start | bytes 98312 | tf_op jit(solution)/shard_map/ppermute | solution.py:312
  15.5 0.4 %target_mine.1 = f32[2,32,256]{2,1,0:T(8,128)S(1)} custom-call(f32[2,64,256]{2,1,0:T(8,128)S(1)} %get-tuple-element.16.total, bf16[2,33,2,32,256]{4,3,2,1,0:T(8,128)(2,1)S(1)} %get-tuple-element.17.spread, bf16[208,128]{1,0:T(8,128)(2,1)S(1)} %collective-permute-done.rest_0_, bf16[208,128]{1,0:T(8,128)(2,1)S(1)} %collective-permute-done.1.rest_1_, ...), custom_call_target="tpu_custom_call" | custom-call | tf_op jit(solution)/shard_map/target_mine/pallas_call | solution.py:299
  15.9 1.9 %collective-permute-done.3 = bf16[64,256]{1,0:T(8,128)(2,1)S(1)} collective-permute-done((bf16[64,256]{1,0:T(8,128)(2,1)S(1)}, bf16[64,256]{1,0:T(8,128)(2,1)S(1)}, u32[]{:S(2)}, u32[]{:S(2)}) %collective-permute-start.3) | collective-permute-done | bytes 32800 | tf_op jit(solution)/shard_map/ppermute | solution.py:312
  17.8 0.6 %convert_add_fusion = f32[2,32,256]{2,1,0:T(8,128)} fusion(f32[2,32,256]{2,1,0:T(8,128)S(1)} %target_mine.1, bf16[2,32,256]{2,1,0:T(8,128)(2,1)S(1)} %bitcast.2), kind=kLoop, calls=%fused_computation | loop fusion | flops 32768 | bytes 163840 | tf_op jit(solution)/shard_map/add | solution.py:317
Async XLA Ops:
  0.0 10.5 %copy-start.2 = (s32[1,1,56]{2,1,0:T(1,128)S(1)}, s32[1,1,56]{2,1,0:T(1,128)}, u32[]{:S(2)}) copy-start(s32[1,1,56]{2,1,0:T(1,128)} %near_tgt.3) | copy-start | bytes 676
  0.0 10.5 %copy-start.1 = (s32[1,1,56]{2,1,0:T(1,128)S(1)}, s32[1,1,56]{2,1,0:T(1,128)}, u32[]{:S(2)}) copy-start(s32[1,1,56]{2,1,0:T(1,128)} %near_src.3) | copy-start | bytes 676
  0.0 10.5 %copy-start = (bf16[1,1,56,2,128,128]{5,4,3,2,1,0:T(8,128)(2,1)S(1)}, bf16[1,1,56,2,128,128]{5,4,3,2,1,0:T(8,128)(2,1)}, u32[]{:S(2)}) copy-start(bf16[1,1,56,2,128,128]{5,4,3,2,1,0:T(8,128)(2,1)} %near_blocks.3) | copy-start | bytes 11010052
  0.0 10.5 %copy-start.4 = (s32[1,1,32]{2,1,0:T(1,128)S(1)}, s32[1,1,32]{2,1,0:T(1,128)}, u32[]{:S(2)}) copy-start(s32[1,1,32]{2,1,0:T(1,128)} %far_tgt.1) | copy-start | bytes 388
  0.0 10.5 %copy-start.3 = (bf16[1,1,32,2,32,128]{5,4,3,2,1,0:T(8,128)(2,1)S(1)}, bf16[1,1,32,2,32,128]{5,4,3,2,1,0:T(8,128)(2,1)}, u32[]{:S(2)}) copy-start(bf16[1,1,32,2,32,128]{5,4,3,2,1,0:T(8,128)(2,1)} %far_u.1) | copy-start | bytes 1572868
  3.5 9.4 %collective-permute-start = (bf16[208,128]{1,0:T(8,128)(2,1)S(1)}, bf16[208,128]{1,0:T(8,128)(2,1)S(1)}, u32[]{:S(2)}, u32[]{:S(2)}) collective-permute-start(bf16[208,128]{1,0:T(8,128)(2,1)S(1)} %get-tuple-element.18), channel_id=1, source_target_pairs={{0,4},{4,8},{8,12},{12,0},{1,5},{5,9},{9,13},{13,1},{2,6},{6,10},{... | collective-permute-start | bytes 159752 | tf_op jit(solution)/shard_map/ppermute | solution.py:282
  6.6 6.4 %collective-permute-start.1 = (bf16[208,128]{1,0:T(8,128)(2,1)S(1)}, bf16[208,128]{1,0:T(8,128)(2,1)S(1)}, u32[]{:S(2)}, u32[]{:S(2)}) collective-permute-start(bf16[208,128]{1,0:T(8,128)(2,1)S(1)} %get-tuple-element.19), channel_id=1, source_target_pairs={{0,8},{4,12},{8,0},{12,4},{1,9},{5,13},{9,1},{13,5},{2,10},{6,14},... | collective-permute-start | bytes 159752 | tf_op jit(solution)/shard_map/ppermute | solution.py:282
  9.2 4.3 %collective-permute-start.2 = (bf16[208,128]{1,0:T(8,128)(2,1)S(1)}, bf16[208,128]{1,0:T(8,128)(2,1)S(1)}, u32[]{:S(2)}, u32[]{:S(2)}) collective-permute-start(bf16[208,128]{1,0:T(8,128)(2,1)S(1)} %get-tuple-element.20), channel_id=1, source_target_pairs={{0,12},{4,0},{8,4},{12,8},{1,13},{5,1},{9,5},{13,9},{2,14},{6,2},{... | collective-permute-start | bytes 159752 | tf_op jit(solution)/shard_map/ppermute | solution.py:282
  13.8 4.0 %collective-permute-start.3 = (bf16[64,256]{1,0:T(8,128)(2,1)S(1)}, bf16[64,256]{1,0:T(8,128)(2,1)S(1)}, u32[]{:S(2)}, u32[]{:S(2)}) collective-permute-start(bf16[64,256]{1,0:T(8,128)(2,1)S(1)} %target_others.1), channel_id=1, source_target_pairs={{0,2},{2,0},{1,3},{3,1},{4,6},{6,4},{5,7},{7,5},{8,10},{10,8},{9,1... | collective-permute-start | bytes 98312 | tf_op jit(solution)/shard_map/ppermute | solution.py:312

commit v4 on v2

--- a/solution.py
+++ b/solution.py
@@ -13,10 +13,15 @@
 PACK = 4
 BASE = 64
 LIMIT = 24 << 20
+SEND_LIMIT = 24 << 20
 VMEM = pl.BlockSpec(memory_space=pltpu.VMEM)
 SMEM = pl.BlockSpec(memory_space=pltpu.SMEM)
 HBM = pl.BlockSpec(memory_space=pltpu.HBM)
 PARAMS = pltpu.CompilerParams(vmem_limit_bytes=LIMIT)
+
+
+def in_hbm(array):
+    return pltpu.with_memory_space_constraint(array, pltpu.HBM)
 
 
 def div_by(value, size):
@@ -67,14 +72,19 @@
     row_in.wait()
     targets = tgt_row[0]
     position = lax.broadcasted_iota(jnp.int32, targets.shape, 1)
+    line = lax.broadcasted_iota(jnp.int32, (-(-2 * (owners - 1) // 8) * 8, 1), 0)
+    low_of = wrap(me + 1 + line // 2, owners) * clusters
+    aimed = (targets >= low_of) & (targets < low_of + clusters)
+    found = jnp.where(aimed, jnp.where(line % 2 == 0, count - 1 - position, position), -1).astype(jnp.float32)
+    found = jnp.max(found, axis=1, keepdims=True).astype(jnp.int32)
     chosen_near = []
     for k in range(1, owners):
         low = wrap(me + k, owners) * clusters
-        aimed = (targets >= low) & (targets < low + clusters)
-        first = jnp.min(jnp.where(aimed, position, count - 1))
-        last = jnp.max(jnp.where(aimed, position, -1))
+        last = found[2 * k - 1, 0]
         final = jnp.maximum(last, 0)
+        first = jnp.minimum(count - 1 - found[2 * k - 2, 0], count - 1)
         chosen_near.append((low, first, final, last >= 0, last > first))
+    for k, (_, first, final, _, _) in enumerate(chosen_near, 1):
         for i, at in enumerate((first, final)):
             pltpu.make_async_copy(
                 near_blocks.at[0, 0, at], picked.at[2 * (k - 1) + i], pick_sems.at[2 * (k - 1) + i]).start()
@@ -137,15 +147,19 @@
     tgt_in.wait()
     near_in.wait()
     near_labels = jnp.zeros((1, LANES), jnp.int32)
+    for k, (_, first, final, _, _) in enumerate(chosen_near, 1):
+        for i, at in enumerate((first, final)):
+            pltpu.make_async_copy(
+                near_blocks.at[0, 0, at], picked.at[2 * (k - 1) + i], pick_sems.at[2 * (k - 1) + i]).wait()
     for k, (low, first, final, any_, two) in enumerate(chosen_near, 1):
         near_labels = jnp.where(lane == k, jnp.where(any_, tgt_n[0, 0, first] - low + 1, 0), near_labels)
-        total = jnp.zeros((rows, PANEL), jnp.float32)
+        left, right = [], []
         for i, (at, used) in enumerate(((first, any_), (final, two))):
-            pltpu.make_async_copy(
-                near_blocks.at[0, 0, at], picked.at[2 * (k - 1) + i], pick_sems.at[2 * (k - 1) + i]).wait()
             source = pl.ds(pl.multiple_of(src_n[0, 0, at] * rows, rows), rows)
-            matrix = jnp.concatenate([picked[2 * (k - 1) + i, 0], picked[2 * (k - 1) + i, 1]], axis=1)
-            total = total + jnp.where(used, dot_nt(field[source, :], matrix), 0.0)
+            values = field[source, :]
+            left.append(jnp.where(used, values, jnp.zeros_like(values)))
+            right += [picked[2 * (k - 1) + i, c] for c in range(2)]
+        total = dot_nt(jnp.concatenate(left, axis=1), jnp.concatenate(right, axis=1))
         messages[k - 1][chunks * rows:(chunks + 1) * rows, :] = total.astype(jnp.bfloat16)
     near_tile = jnp.broadcast_to(near_labels, (8, LANES)).astype(jnp.float32)
     tile = jnp.concatenate([far_labels, near_tile], axis=0).astype(jnp.bfloat16)
@@ -186,19 +200,13 @@
 
 def own_kernel(depth, used, near_src, near_tgt, far_tgt, field, labels, own_coeffs, far_u, near_blocks,
                total, spread, sums):
+    count = near_blocks.shape[2]
     me = lax.axis_index("src")
     sharers, rows, width = total.shape
     clusters = sums.shape[0] - 1
     share = clusters // sharers
     blocks, rank = far_u.shape[2], far_u.shape[4]
     chunks = depth * rank // LANES
-    sums[...] = jnp.zeros_like(sums)
-    for b in range(near_blocks.shape[2]):
-        target = near_tgt[0, 0, b] - me * clusters
-        target = jnp.where((target >= 0) & (target < clusters), target, clusters)
-        source = pl.ds(pl.multiple_of(near_src[0, 0, b] * rows, rows), rows)
-        matrix = jnp.concatenate([near_blocks[0, 0, b, 0], near_blocks[0, 0, b, 1]], axis=1)
-        sums[target] += dot_nt(field[source, :], matrix)
     zero = jnp.zeros((rank, PANEL), jnp.bfloat16)
     for holder in range(sharers):
         for part in range(2):
@@ -213,8 +221,18 @@
     slots, _ = read_labels(depth, used, 0, labels[...], None)
     left = far_operands(depth, chunks, rows, own_coeffs)
     for holder in range(sharers):
-        near = jnp.concatenate([sums[holder * share + c] for c in range(share)], axis=1)
-        total[holder] = near + dot_nn(left, far_matrix(depth, holder, slots, spread))
+        far = dot_nn(left, far_matrix(depth, holder, slots, spread))
+        for c in range(share):
+            sums[holder * share + c] = far[:, c * PANEL:(c + 1) * PANEL]
+    for b in range(count):
+        target = near_tgt[0, 0, b] - me * clusters
+        target = jnp.where((target >= 0) & (target < clusters), target, clusters)
+        source = pl.ds(pl.multiple_of(near_src[0, 0, b] * rows, rows), rows)
+        matrix = jnp.concatenate([near_blocks[0, 0, b, 0], near_blocks[0, 0, b, 1]], axis=1)
+        sums[target] += dot_nt(field[source, :], matrix)
+    for holder in range(sharers):
+        for c in range(share):
+            total[holder, :, c * PANEL:(c + 1) * PANEL] = sums[holder * share + c]
 
 
 def target_kernel(owners, depth, used, steps, total, spread, *rest):
@@ -274,9 +292,9 @@
             pltpu.SemaphoreType.DMA((7,)),
             pltpu.SemaphoreType.DMA((2 * (owners - 1),)),
         ],
-        compiler_params=PARAMS,
+        compiler_params=pltpu.CompilerParams(vmem_limit_bytes=SEND_LIMIT),
         name="send",
-    )(far_src, far_dst, near_src, near_tgt, incident, far_v, near_blocks)
+    )(*map(in_hbm, (far_src, far_dst, near_src, near_tgt, incident, far_v, near_blocks)))
     arrived = [
         lax.ppermute(message, "src", [(s, (s + k) % owners) for s in range(owners)])
         for k, message in enumerate(messages, 1)

time: 24.7 us -> 17.9 us (0.72)
  local copies, waits for them, and re-layouts: 6.55 us -> 0.02 us
    unnamed x20 -> x10, local copies, waits for them, and re-layouts: 6.55 us -> 0.02 us
  transfers between devices with their start and end apart: 4 -> 4, of which waited for: 3 -> 2; matrix products, arithmetic and copies ran while one was open for 0% -> 0% of each run, Pallas kernels for 11% -> 16%
where the time goes in v4:
time: 17.9 us; the launch traced here: 17.8 us
  starting transfers between devices  8.73 us (49%)
  Pallas kernels  6 us (34%)
  waiting for transfers between devices  2.36 us (13%)
  other arithmetic  0.64 us (4%)
    ppermute x3, starting transfers between devices, body(): lax.ppermute(message, 'src', [(s, (s + k) % owners) for s in range(owners)])  7.04 us
    pallas_call x1, Pallas kernels, body(): pl.pallas_call(functools.partial(send_kernel, owners, depth), out_shape=[...  2.82 us
    pallas_call x1, Pallas kernels, body(): pl.pallas_call(functools.partial(own_kernel, depth, used), out_shape=[sha...  2.42 us
    ppermute x1, waiting for transfers between devices, body(): lax.ppermute(other, 'tgt', [(t, (t + k) % sharers) for t in range(sharers)])  1.9 us
    ppermute x1, starting transfers between devices, body(): lax.ppermute(other, 'tgt', [(t, (t + k) % sharers) for t in range(sharers)])  1.69 us
    pallas_call x2, Pallas kernels, target(): pl.pallas_call(functools.partial(target_kernel, owners, depth, used, step...  0.76 us
    add x1, other arithmetic, body(): result = result + other.astype(f32).reshape(result.shape)  0.64 us
    ppermute x3, waiting for transfers between devices, body(): lax.ppermute(message, 'src', [(s, (s + k) % owners) for s in range(owners)])  0.46 us
  transfers between devices with their start and end apart: 4, of which 2 were waited for; matrix products, arithmetic and copies ran while one was open for 0% of the time, Pallas kernels for 16%

profile of v4, /device:TPU:0, one launch (start us, length us, event | category | flops | bytes accessed | tf_op | source)
XLA Modules:
  0.0 17.8 jit_solution(11640023556278876257)
XLA Ops:
  0.0 0.0 copy-start.2
  0.0 0.0 copy-start.1
  0.0 0.0 copy-start
  0.0 0.0 copy-start.4
  0.0 0.0 copy-start.3
  0.0 2.8 %send.1 = (bf16[256,256]{1,0:T(8,128)(2,1)S(1)}, f32[8,128]{1,0:T(8,128)S(1)}, bf16[128,128]{1,0:T(8,128)(2,1)S(1)}, bf16[208,128]{1,0:T(8,128)(2,1)S(1)}, bf16[...) custom-call(s32[1,1,32]{2,1,0:T(1,128)} %far_src.1, s32[1,1,32]{2,1,0:T(1,128)} %far_dst.1, s32[1,1,56]{2,1,0:T(1,128)} %near_src.3, ...), custom_call_target="tpu_custom_call" | custom-call | tf_op jit(solution)/shard_map/send/pallas_call | solution.py:276
  2.8 3.1 %collective-permute-start = (bf16[208,128]{1,0:T(8,128)(2,1)S(1)}, bf16[208,128]{1,0:T(8,128)(2,1)S(1)}, u32[]{:S(2)}, u32[]{:S(2)}) collective-permute-start(bf16[208,128]{1,0:T(8,128)(2,1)S(1)} %get-tuple-element.18), channel_id=1, source_target_pairs={{0,4},{4,8},{8,12},{12,0},{1,5},{5,9},{9,13},{13,1},{2,6},{6,10},{... | collective-permute-start | bytes 159752 | tf_op jit(solution)/shard_map/ppermute | solution.py:299
  5.9 2.6 %collective-permute-start.1 = (bf16[208,128]{1,0:T(8,128)(2,1)S(1)}, bf16[208,128]{1,0:T(8,128)(2,1)S(1)}, u32[]{:S(2)}, u32[]{:S(2)}) collective-permute-start(bf16[208,128]{1,0:T(8,128)(2,1)S(1)} %get-tuple-element.19), channel_id=1, source_target_pairs={{0,8},{4,12},{8,0},{12,4},{1,9},{5,13},{9,1},{13,5},{2,10},{6,14},... | collective-permute-start | bytes 159752 | tf_op jit(solution)/shard_map/ppermute | solution.py:299
  8.5 1.3 %collective-permute-start.2 = (bf16[208,128]{1,0:T(8,128)(2,1)S(1)}, bf16[208,128]{1,0:T(8,128)(2,1)S(1)}, u32[]{:S(2)}, u32[]{:S(2)}) collective-permute-start(bf16[208,128]{1,0:T(8,128)(2,1)S(1)} %get-tuple-element.20), channel_id=1, source_target_pairs={{0,12},{4,0},{8,4},{12,8},{1,13},{5,1},{9,5},{13,9},{2,14},{6,2},{... | collective-permute-start | bytes 159752 | tf_op jit(solution)/shard_map/ppermute | solution.py:299
  9.9 0.0 copy-done.2
  9.9 0.0 copy-done.1
  9.9 0.0 copy-done
  9.9 0.0 copy-done.4
  9.9 0.0 copy-done.3
  9.9 2.4 %own.1 = (f32[2,64,256]{2,1,0:T(8,128)S(1)}, bf16[2,33,2,32,256]{4,3,2,1,0:T(8,128)(2,1)S(1)}) custom-call(s32[1,1,56]{2,1,0:T(1,128)S(1)} %copy-done.1, s32[1,1,56]{2,1,0:T(1,128)S(1)} %copy-done.2, s32[1,1,32]{2,1,0:T(1,128)S(1)} %copy-done.4, bf16[256,256]{1,0:T(8,128)(2,1)S(1)} %get-tuple-element.13.field, f32[8,128]{1,0:T(8,128)S(1)} %get-tuple-element.14.labels, ...), custom_call_target="tpu_custom_call" | custom-call | flops 3758096384 | bytes 3670016 | tf_op jit(solution)/shard_map/own/pallas_call | solution.py:303
  12.3 0.0 collective-permute-done.rest_0_
  12.3 0.0 collective-permute-done.1.rest_1_
  12.4 0.4 %collective-permute-done.2.rest_2_ = bf16[208,128]{1,0:T(8,128)(2,1)S(1)} collective-permute-done((bf16[208,128]{1,0:T(8,128)(2,1)S(1)}, bf16[208,128]{1,0:T(8,128)(2,1)S(1)}, u32[]{:S(2)}, u32[]{:S(2)}) %collective-permute-start.2) | collective-permute-done | bytes 53280 | tf_op jit(solution)/shard_map/ppermute | solution.py:299
  12.8 0.4 %target_others.1 = bf16[64,256]{1,0:T(8,128)(2,1)S(1)} custom-call(f32[2,64,256]{2,1,0:T(8,128)S(1)} %get-tuple-element.16.total, bf16[2,33,2,32,256]{4,3,2,1,0:T(8,128)(2,1)S(1)} %get-tuple-element.17.spread, bf16[208,128]{1,0:T(8,128)(2,1)S(1)} %collective-permute-done.rest_0_, bf16[208,128]{1,0:T(8,128)(2,1)S(1)} %collective-permute-done.1.rest_1_, ...), custom_call_target="tpu_custom_call" | custom-call | tf_op jit(solution)/shard_map/target_others/pallas_call | solution.py:316
  13.2 1.7 %collective-permute-start.3 = (bf16[64,256]{1,0:T(8,128)(2,1)S(1)}, bf16[64,256]{1,0:T(8,128)(2,1)S(1)}, u32[]{:S(2)}, u32[]{:S(2)}) collective-permute-start(bf16[64,256]{1,0:T(8,128)(2,1)S(1)} %target_others.1), channel_id=1, source_target_pairs={{0,2},{2,0},{1,3},{3,1},{4,6},{6,4},{5,7},{7,5},{8,10},{10,8},{9,1... | collective-permute-start | bytes 98312 | tf_op jit(solution)/shard_map/ppermute | solution.py:329
  14.9 0.4 %target_mine.1 = f32[2,32,256]{2,1,0:T(8,128)S(1)} custom-call(f32[2,64,256]{2,1,0:T(8,128)S(1)} %get-tuple-element.16.total, bf16[2,33,2,32,256]{4,3,2,1,0:T(8,128)(2,1)S(1)} %get-tuple-element.17.spread, bf16[208,128]{1,0:T(8,128)(2,1)S(1)} %collective-permute-done.rest_0_, bf16[208,128]{1,0:T(8,128)(2,1)S(1)} %collective-permute-done.1.rest_1_, ...), custom_call_target="tpu_custom_call" | custom-call | tf_op jit(solution)/shard_map/target_mine/pallas_call | solution.py:316
  15.3 1.9 %collective-permute-done.3 = bf16[64,256]{1,0:T(8,128)(2,1)S(1)} collective-permute-done((bf16[64,256]{1,0:T(8,128)(2,1)S(1)}, bf16[64,256]{1,0:T(8,128)(2,1)S(1)}, u32[]{:S(2)}, u32[]{:S(2)}) %collective-permute-start.3) | collective-permute-done | bytes 32800 | tf_op jit(solution)/shard_map/ppermute | solution.py:329
  17.2 0.6 %convert_add_fusion = f32[2,32,256]{2,1,0:T(8,128)} fusion(f32[2,32,256]{2,1,0:T(8,128)S(1)} %target_mine.1, bf16[2,32,256]{2,1,0:T(8,128)(2,1)S(1)} %bitcast.2), kind=kLoop, calls=%fused_computation | loop fusion | flops 32768 | bytes 163840 | tf_op jit(solution)/shard_map/add | solution.py:334
Async XLA Ops:
  0.0 9.9 %copy-start.2 = (s32[1,1,56]{2,1,0:T(1,128)S(1)}, s32[1,1,56]{2,1,0:T(1,128)}, u32[]{:S(2)}) copy-start(s32[1,1,56]{2,1,0:T(1,128)} %near_tgt.3) | copy-start | bytes 676
  0.0 9.9 %copy-start.1 = (s32[1,1,56]{2,1,0:T(1,128)S(1)}, s32[1,1,56]{2,1,0:T(1,128)}, u32[]{:S(2)}) copy-start(s32[1,1,56]{2,1,0:T(1,128)} %near_src.3) | copy-start | bytes 676
  0.0 9.9 %copy-start = (bf16[1,1,56,2,128,128]{5,4,3,2,1,0:T(8,128)(2,1)S(1)}, bf16[1,1,56,2,128,128]{5,4,3,2,1,0:T(8,128)(2,1)}, u32[]{:S(2)}) copy-start(bf16[1,1,56,2,128,128]{5,4,3,2,1,0:T(8,128)(2,1)} %near_blocks.3) | copy-start | bytes 11010052
  0.0 9.9 %copy-start.4 = (s32[1,1,32]{2,1,0:T(1,128)S(1)}, s32[1,1,32]{2,1,0:T(1,128)}, u32[]{:S(2)}) copy-start(s32[1,1,32]{2,1,0:T(1,128)} %far_tgt.1) | copy-start | bytes 388
  0.0 9.9 %copy-start.3 = (bf16[1,1,32,2,32,128]{5,4,3,2,1,0:T(8,128)(2,1)S(1)}, bf16[1,1,32,2,32,128]{5,4,3,2,1,0:T(8,128)(2,1)}, u32[]{:S(2)}) copy-start(bf16[1,1,32,2,32,128]{5,4,3,2,1,0:T(8,128)(2,1)} %far_u.1) | copy-start | bytes 1572868
  2.8 9.5 %collective-permute-start = (bf16[208,128]{1,0:T(8,128)(2,1)S(1)}, bf16[208,128]{1,0:T(8,128)(2,1)S(1)}, u32[]{:S(2)}, u32[]{:S(2)}) collective-permute-start(bf16[208,128]{1,0:T(8,128)(2,1)S(1)} %get-tuple-element.18), channel_id=1, source_target_pairs={{0,4},{4,8},{8,12},{12,0},{1,5},{5,9},{9,13},{13,1},{2,6},{6,10},{... | collective-permute-start | bytes 159752 | tf_op jit(solution)/shard_map/ppermute | solution.py:299
  5.9 6.4 %collective-permute-start.1 = (bf16[208,128]{1,0:T(8,128)(2,1)S(1)}, bf16[208,128]{1,0:T(8,128)(2,1)S(1)}, u32[]{:S(2)}, u32[]{:S(2)}) collective-permute-start(bf16[208,128]{1,0:T(8,128)(2,1)S(1)} %get-tuple-element.19), channel_id=1, source_target_pairs={{0,8},{4,12},{8,0},{12,4},{1,9},{5,13},{9,1},{13,5},{2,10},{6,14},... | collective-permute-start | bytes 159752 | tf_op jit(solution)/shard_map/ppermute | solution.py:299
  8.5 4.3 %collective-permute-start.2 = (bf16[208,128]{1,0:T(8,128)(2,1)S(1)}, bf16[208,128]{1,0:T(8,128)(2,1)S(1)}, u32[]{:S(2)}, u32[]{:S(2)}) collective-permute-start(bf16[208,128]{1,0:T(8,128)(2,1)S(1)} %get-tuple-element.20), channel_id=1, source_target_pairs={{0,12},{4,0},{8,4},{12,8},{1,13},{5,1},{9,5},{13,9},{2,14},{6,2},{... | collective-permute-start | bytes 159752 | tf_op jit(solution)/shard_map/ppermute | solution.py:299
  13.2 4.0 %collective-permute-start.3 = (bf16[64,256]{1,0:T(8,128)(2,1)S(1)}, bf16[64,256]{1,0:T(8,128)(2,1)S(1)}, u32[]{:S(2)}, u32[]{:S(2)}) collective-permute-start(bf16[64,256]{1,0:T(8,128)(2,1)S(1)} %target_others.1), channel_id=1, source_target_pairs={{0,2},{2,0},{1,3},{3,1},{4,6},{6,4},{5,7},{7,5},{8,10},{10,8},{9,1... | collective-permute-start | bytes 98312 | tf_op jit(solution)/shard_map/ppermute | solution.py:329

commit v5 on v4

--- a/solution.py
+++ b/solution.py
@@ -13,7 +13,7 @@
 PACK = 4
 BASE = 64
 LIMIT = 24 << 20
-SEND_LIMIT = 24 << 20
+MESSAGE_FLOPS = 2 * 10**9
 VMEM = pl.BlockSpec(memory_space=pltpu.VMEM)
 SMEM = pl.BlockSpec(memory_space=pltpu.SMEM)
 HBM = pl.BlockSpec(memory_space=pltpu.HBM)
@@ -44,11 +44,10 @@
     return jnp.dot(left, right, preferred_element_type=jnp.float32)
 
 
-def send_kernel(owners, depth, far_src, far_dst, near_src, near_tgt, incident, far_v, near_blocks,
-                field, labels, own_coeffs, *rest):
-    messages, rest = rest[:owners - 1], rest[owners - 1:]
-    (src_f, dst_f, src_n, tgt_n, tgt_row, waves, factors, picked, ordered, source_of, counts,
-     sems, pick_sems) = rest
+def coeff_kernel(owners, depth, far_src, far_dst, near_src, near_tgt, incident, far_v, near_blocks,
+                 field, labels, aimed_out, picked, *rest):
+    coeffs, rest = rest[:owners], rest[owners:]
+    src_f, dst_f, tgt_row, src_row, waves, factors, ordered, source_of, counts, sems, pick_sems = rest
     me = lax.axis_index("src")
     half = waves.shape[1]
     rows = 2 * half
@@ -62,32 +61,31 @@
     loads = [
         pltpu.make_async_copy(a, b, sems.at[i])
         for i, (a, b) in enumerate((
-            (near_tgt, tgt_row), (near_tgt, tgt_n), (near_src, src_n), (far_dst, dst_f), (far_src, src_f),
-            (incident, waves), (far_v, factors)))
+            (near_tgt, tgt_row), (near_src, src_row), (far_dst, dst_f), (far_src, src_f), (incident, waves), (far_v, factors)))
     ]
     for load in loads:
         load.start()
-    row_in, tgt_in, near_in, dst_in, far_in, waves_in, factors_in = loads
-
-    row_in.wait()
+    tgt_in, near_in, dst_in, far_in, waves_in, factors_in = loads
+
+    tgt_in.wait()
+    near_in.wait()
     targets = tgt_row[0]
     position = lax.broadcasted_iota(jnp.int32, targets.shape, 1)
-    line = lax.broadcasted_iota(jnp.int32, (-(-2 * (owners - 1) // 8) * 8, 1), 0)
-    low_of = wrap(me + 1 + line // 2, owners) * clusters
-    aimed = (targets >= low_of) & (targets < low_of + clusters)
-    found = jnp.where(aimed, jnp.where(line % 2 == 0, count - 1 - position, position), -1).astype(jnp.float32)
-    found = jnp.max(found, axis=1, keepdims=True).astype(jnp.int32)
-    chosen_near = []
-    for k in range(1, owners):
-        low = wrap(me + k, owners) * clusters
-        last = found[2 * k - 1, 0]
-        final = jnp.maximum(last, 0)
-        first = jnp.minimum(count - 1 - found[2 * k - 2, 0], count - 1)
-        chosen_near.append((low, first, final, last >= 0, last > first))
-    for k, (_, first, final, _, _) in enumerate(chosen_near, 1):
-        for i, at in enumerate((first, final)):
-            pltpu.make_async_copy(
-                near_blocks.at[0, 0, at], picked.at[2 * (k - 1) + i], pick_sems.at[2 * (k - 1) + i]).start()
+    line = lax.broadcasted_iota(jnp.int32, (aimed_out.shape[0], 1), 0)
+    low = wrap(me + 1 + line // 2, owners) * clusters
+    aimed = (targets >= low) & (targets < low + clusters)
+    found = jnp.where(line % 2 == 0, count - 1 - position, position)
+    found = (found * clusters + src_row[0]) * clusters + targets - low
+    found = jnp.max(jnp.where(aimed, found, -1).astype(jnp.float32), axis=1, keepdims=True)
+    aimed_out[...] = jnp.broadcast_to(found.astype(jnp.int32), aimed_out.shape)
+
+    picks = []
+    for at in range(2 * (owners - 1)):
+        where = div_by(jnp.maximum(found[at, 0].astype(jnp.int32), 0), clusters * clusters)
+        if at % 2 == 0:
+            where = count - 1 - where
+        picks.append(pltpu.make_async_copy(near_blocks.at[0, 0, where], picked.at[at], pick_sems.at[at]))
+        picks[-1].start()
 
     waves_in.wait()
     for s in range(clusters):
@@ -126,13 +124,11 @@
         ordered[at, PANEL:2 * PANEL] = factors[0, 0, f, 1]
         source_of[place] = src_f[0, 0, f]
         label_row = jnp.where(lane == place, slot + 1, label_row)
-    far_labels = jnp.broadcast_to(label_row, (8, LANES)).astype(jnp.float32)
-    labels[...] = far_labels
+    labels[...] = jnp.broadcast_to(label_row, (8, LANES)).astype(jnp.float32)
 
     group = lane // rank
     everything = field[...]
     for k in range(owners):
-        out = own_coeffs if k == 0 else messages[k - 1]
         product = dot_nt(everything, ordered[k * chunks * LANES:(k + 1) * chunks * LANES, :])
         for chunk in range(chunks):
             source = jnp.zeros((1, LANES), jnp.int32)
@@ -142,29 +138,41 @@
             chosen = part[0:rows]
             for s in range(1, clusters):
                 chosen = jnp.where(source == s, part[s * rows:(s + 1) * rows], chosen)
-            out[chunk * rows:(chunk + 1) * rows, :] = chosen.astype(jnp.bfloat16)
-
-    tgt_in.wait()
-    near_in.wait()
+            coeffs[k][chunk * rows:(chunk + 1) * rows, :] = chosen.astype(jnp.bfloat16)
+    for pick in picks:
+        pick.wait()
+
+
+def message_kernel(owners, count, field, labels, aimed, picked, *rest):
+    coeffs, messages = rest[:owners - 1], rest[owners - 1:]
+    depth_rows = coeffs[0].shape[0]
+    rows = messages[0].shape[0] - depth_rows - LABEL_ROWS
+    clusters = field.shape[0] // rows
+    lane = lax.broadcasted_iota(jnp.int32, (1, LANES), 1)
     near_labels = jnp.zeros((1, LANES), jnp.int32)
-    for k, (_, first, final, _, _) in enumerate(chosen_near, 1):
-        for i, at in enumerate((first, final)):
-            pltpu.make_async_copy(
-                near_blocks.at[0, 0, at], picked.at[2 * (k - 1) + i], pick_sems.at[2 * (k - 1) + i]).wait()
-    for k, (low, first, final, any_, two) in enumerate(chosen_near, 1):
-        near_labels = jnp.where(lane == k, jnp.where(any_, tgt_n[0, 0, first] - low + 1, 0), near_labels)
-        left, right = [], []
-        for i, (at, used) in enumerate(((first, any_), (final, two))):
-            source = pl.ds(pl.multiple_of(src_n[0, 0, at] * rows, rows), rows)
-            values = field[source, :]
-            left.append(jnp.where(used, values, jnp.zeros_like(values)))
+    every = aimed[...]
+    for k, (message, part) in enumerate(zip(messages, coeffs), 1):
+        first, last = every[2 * k - 2, 0], every[2 * k - 1, 0]
+        filled = first >= 0
+        positions, left, right = [], [], []
+        for number in (jnp.maximum(first, 0), jnp.maximum(last, 0)):
+            above = div_by(number, clusters)
+            positions.append(div_by(above, clusters))
+            source = above - positions[-1] * clusters
+            left.append(field[pl.ds(pl.multiple_of(source * rows, rows), rows), :])
+            target = number - above * clusters
+        positions[0] = count - 1 - positions[0]
+        near_labels = jnp.where(lane == k, jnp.where(filled, target + 1, 0), near_labels)
+        for i, used in enumerate((filled, positions[1] > positions[0])):
+            left[i] = jnp.where(used & filled, left[i], jnp.zeros_like(left[i]))
             right += [picked[2 * (k - 1) + i, c] for c in range(2)]
         total = dot_nt(jnp.concatenate(left, axis=1), jnp.concatenate(right, axis=1))
-        messages[k - 1][chunks * rows:(chunks + 1) * rows, :] = total.astype(jnp.bfloat16)
+        message[0:depth_rows, :] = part[...]
+        message[depth_rows:depth_rows + rows, :] = total.astype(jnp.bfloat16)
     near_tile = jnp.broadcast_to(near_labels, (8, LANES)).astype(jnp.float32)
-    tile = jnp.concatenate([far_labels, near_tile], axis=0).astype(jnp.bfloat16)
+    tile = jnp.concatenate([labels[...], near_tile], axis=0).astype(jnp.bfloat16)
     for message in messages:
-        message[(chunks + 1) * rows:, :] = tile
+        message[depth_rows + rows:, :] = tile
 
 
 def read_labels(depth, used, k, far_tile, near_tile):
@@ -273,33 +281,42 @@
     bf16, f32, i32 = jnp.bfloat16, jnp.float32, jnp.int32
     shape = jax.ShapeDtypeStruct
 
-    field, labels, own_coeffs, *messages = pl.pallas_call(
-        functools.partial(send_kernel, owners, depth),
-        out_shape=[shape((clusters * rows, 2 * PANEL), bf16), shape((8, LANES), f32), shape((chunks * rows, LANES), bf16)]
-        + [shape(((chunks + 1) * rows + LABEL_ROWS, LANES), bf16)] * (owners - 1),
+    lines = -(-2 * (owners - 1) // 8) * 8
+    near_count = near_blocks.shape[2]
+    field, labels, aimed, picked, own_coeffs, *coeffs = pl.pallas_call(
+        functools.partial(coeff_kernel, owners, depth),
+        out_shape=[shape((clusters * rows, 2 * PANEL), bf16), shape((8, LANES), f32), shape((lines, LANES), i32)]
+        + [shape((2 * (owners - 1),) + near_blocks.shape[3:], bf16)]
+        + [shape((chunks * rows, LANES), bf16)] * owners,
         in_specs=[HBM] * 7,
-        out_specs=[VMEM] * (2 + owners),
+        out_specs=[VMEM] * (4 + owners),
         scratch_shapes=[
             pltpu.SMEM(far_src.shape, i32), pltpu.SMEM(far_dst.shape, i32),
-            pltpu.SMEM(near_src.shape, i32), pltpu.SMEM(near_tgt.shape, i32),
-            pltpu.VMEM(near_tgt.shape, i32),
+            pltpu.VMEM(near_tgt.shape, i32), pltpu.VMEM(near_src.shape, i32),
             pltpu.VMEM(incident.shape, bf16),
             pltpu.VMEM(far_v.shape, bf16),
-            pltpu.VMEM((2 * (owners - 1),) + near_blocks.shape[3:], bf16),
             pltpu.VMEM((owners * depth * rank, 2 * PANEL), bf16),
             pltpu.SMEM((owners * depth,), i32),
             pltpu.SMEM((owners,), i32),
-            pltpu.SemaphoreType.DMA((7,)),
+            pltpu.SemaphoreType.DMA((6,)),
             pltpu.SemaphoreType.DMA((2 * (owners - 1),)),
         ],
-        compiler_params=pltpu.CompilerParams(vmem_limit_bytes=SEND_LIMIT),
-        name="send",
+        compiler_params=PARAMS,
+        name="coefficients",
     )(*map(in_hbm, (far_src, far_dst, near_src, near_tgt, incident, far_v, near_blocks)))
+    messages = pl.pallas_call(
+        functools.partial(message_kernel, owners, near_count),
+        out_shape=[shape(((chunks + 1) * rows + LABEL_ROWS, LANES), bf16)] * (owners - 1),
+        in_specs=[VMEM] * (3 + owners),
+        out_specs=[VMEM] * (owners - 1),
+        compiler_params=PARAMS,
+        cost_estimate=pl.CostEstimate(flops=MESSAGE_FLOPS, bytes_accessed=0, transcendentals=0),
+        name="messages",
+    )(field, labels, aimed, picked, *coeffs)
     arrived = [
         lax.ppermute(message, "src", [(s, (s + k) % owners) for s in range(owners)])
         for k, message in enumerate(messages, 1)
     ]
-    near_count = near_blocks.shape[2]
     total, spread = pl.pallas_call(
         functools.partial(own_kernel, depth, used),
         out_shape=[shape((sharers, rows, width), f32), shape((sharers, blocks + 1, 2, rank, width), bf16)],

time: 17.9 us -> 17.3 us (0.966)
  Pallas kernels: 6 us -> 5.35 us
    pallas_call x1 -> x2, Pallas kernels: 2.82 us -> 2.17 us  [the longest x1 1.89 us: body(): pl.pallas_call(functools.partial(coeff_kernel, owners, depth), out_shape=...]
where the time goes in v5:
time: 17.3 us; the launch traced here: 17.2 us
  starting transfers between devices  8.71 us (50%)
  Pallas kernels  5.35 us (31%)
  waiting for transfers between devices  2.36 us (14%)
  other arithmetic  0.64 us (4%)
    ppermute x3, starting transfers between devices, body(): lax.ppermute(message, 'src', [(s, (s + k) % owners) for s in range(owners)])  7.01 us
    pallas_call x1, Pallas kernels, body(): pl.pallas_call(functools.partial(own_kernel, depth, used), out_shape=[sha...  2.43 us
    ppermute x1, waiting for transfers between devices, body(): lax.ppermute(other, 'tgt', [(t, (t + k) % sharers) for t in range(sharers)])  1.9 us
    pallas_call x1, Pallas kernels, body(): pl.pallas_call(functools.partial(coeff_kernel, owners, depth), out_shape=...  1.89 us
    ppermute x1, starting transfers between devices, body(): lax.ppermute(other, 'tgt', [(t, (t + k) % sharers) for t in range(sharers)])  1.69 us
    pallas_call x2, Pallas kernels, target(): pl.pallas_call(functools.partial(target_kernel, owners, depth, used, step...  0.76 us
    add x1, other arithmetic, body(): result = result + other.astype(f32).reshape(result.shape)  0.64 us
    ppermute x3, waiting for transfers between devices, body(): lax.ppermute(message, 'src', [(s, (s + k) % owners) for s in range(owners)])  0.45 us
  transfers between devices with their start and end apart: 4, of which 2 were waited for; matrix products, arithmetic and copies ran while one was open for 0% of the time, Pallas kernels for 16%

profile of v5, /device:TPU:0, one launch (start us, length us, event | category | flops | bytes accessed | tf_op | source)
XLA Modules:
  0.0 17.2 jit_solution(6558745040194748553)
XLA Ops:
  0.0 1.9 %coefficients.1 = (bf16[256,256]{1,0:T(8,128)(2,1)S(1)}, f32[8,128]{1,0:T(8,128)S(1)}, s32[8,128]{1,0:T(8,128)S(1)}, bf16[6,2,128,128]{3,2,1,0:T(8,128)(2,1)S(1)...) custom-call(s32[1,1,32]{2,1,0:T(1,128)} %far_src.1, ...), custom_call_target="tpu_custom_call" | custom-call | tf_op jit(solution)/shard_map/coefficients/pallas_call | solution.py:286
  1.9 0.0 copy-start
  1.9 0.0 copy-start.1
  1.9 0.0 copy-start.2
  1.9 0.0 copy-start.3
  1.9 0.0 copy-start.4
  2.0 0.3 %messages.1 = (bf16[208,128]{1,0:T(8,128)(2,1)S(1)}, bf16[208,128]{1,0:T(8,128)(2,1)S(1)}, bf16[208,128]{1,0:T(8,128)(2,1)S(1)}) custom-call(bf16[256,256]{1,0:T(8,128)(2,1)S(1)} %get-tuple-element.18.field, f32[8,128]{1,0:T(8,128)S(1)} %get-tuple-element.19.labels, s32[8,128]{1,0:T(8,128)S(1)} %get-tuple-element.23.aimed, ...), custom_call_target="tpu_custom_call" | custom-call | flops 2000000000 | tf_op jit(solution)/shard_map/messages/pallas_call | solution.py:307
  2.2 3.1 %collective-permute-start = (bf16[208,128]{1,0:T(8,128)(2,1)S(1)}, bf16[208,128]{1,0:T(8,128)(2,1)S(1)}, u32[]{:S(2)}, u32[]{:S(2)}) collective-permute-start(bf16[208,128]{1,0:T(8,128)(2,1)S(1)} %get-tuple-element.28), channel_id=1, source_target_pairs={{0,4},{4,8},{8,12},{12,0},{1,5},{5,9},{9,13},{13,1},{2,6},{6,10},{... | collective-permute-start | bytes 159752 | tf_op jit(solution)/shard_map/ppermute | solution.py:317
  5.3 2.6 %collective-permute-start.1 = (bf16[208,128]{1,0:T(8,128)(2,1)S(1)}, bf16[208,128]{1,0:T(8,128)(2,1)S(1)}, u32[]{:S(2)}, u32[]{:S(2)}) collective-permute-start(bf16[208,128]{1,0:T(8,128)(2,1)S(1)} %get-tuple-element.29), channel_id=1, source_target_pairs={{0,8},{4,12},{8,0},{12,4},{1,9},{5,13},{9,1},{13,5},{2,10},{6,14},... | collective-permute-start | bytes 159752 | tf_op jit(solution)/shard_map/ppermute | solution.py:317
  7.9 1.3 %collective-permute-start.2 = (bf16[208,128]{1,0:T(8,128)(2,1)S(1)}, bf16[208,128]{1,0:T(8,128)(2,1)S(1)}, u32[]{:S(2)}, u32[]{:S(2)}) collective-permute-start(bf16[208,128]{1,0:T(8,128)(2,1)S(1)} %get-tuple-element.30), channel_id=1, source_target_pairs={{0,12},{4,0},{8,4},{12,8},{1,13},{5,1},{9,5},{13,9},{2,14},{6,2},{... | collective-permute-start | bytes 159752 | tf_op jit(solution)/shard_map/ppermute | solution.py:317
  9.3 0.0 copy-done
  9.3 0.0 copy-done.1
  9.3 0.0 copy-done.2
  9.3 0.0 copy-done.3
  9.3 0.0 copy-done.4
  9.3 2.4 %own.1 = (f32[2,64,256]{2,1,0:T(8,128)S(1)}, bf16[2,33,2,32,256]{4,3,2,1,0:T(8,128)(2,1)S(1)}) custom-call(s32[1,1,56]{2,1,0:T(1,128)S(1)} %copy-done.1, s32[1,1,56]{2,1,0:T(1,128)S(1)} %copy-done.2, s32[1,1,32]{2,1,0:T(1,128)S(1)} %copy-done.4, bf16[256,256]{1,0:T(8,128)(2,1)S(1)} %get-tuple-element.18.field, f32[8,128]{1,0:T(8,128)S(1)} %get-tuple-element.19.labels, ...), custom_call_target="tpu_custom_call" | custom-call | flops 3758096384 | bytes 3670016 | tf_op jit(solution)/shard_map/own/pallas_call | solution.py:320
  11.7 0.0 collective-permute-done.rest_0_
  11.7 0.0 collective-permute-done.1.rest_1_
  11.7 0.4 %collective-permute-done.2.rest_2_ = bf16[208,128]{1,0:T(8,128)(2,1)S(1)} collective-permute-done((bf16[208,128]{1,0:T(8,128)(2,1)S(1)}, bf16[208,128]{1,0:T(8,128)(2,1)S(1)}, u32[]{:S(2)}, u32[]{:S(2)}) %collective-permute-start.2) | collective-permute-done | bytes 53280 | tf_op jit(solution)/shard_map/ppermute | solution.py:317
  12.2 0.4 %target_others.1 = bf16[64,256]{1,0:T(8,128)(2,1)S(1)} custom-call(f32[2,64,256]{2,1,0:T(8,128)S(1)} %get-tuple-element.21.total, bf16[2,33,2,32,256]{4,3,2,1,0:T(8,128)(2,1)S(1)} %get-tuple-element.22.spread, bf16[208,128]{1,0:T(8,128)(2,1)S(1)} %collective-permute-done.rest_0_, bf16[208,128]{1,0:T(8,128)(2,1)S(1)} %collective-permute-done.1.rest_1_, ...), custom_call_target="tpu_custom_call" | custom-call | tf_op jit(solution)/shard_map/target_others/pallas_call | solution.py:333
  12.6 1.7 %collective-permute-start.3 = (bf16[64,256]{1,0:T(8,128)(2,1)S(1)}, bf16[64,256]{1,0:T(8,128)(2,1)S(1)}, u32[]{:S(2)}, u32[]{:S(2)}) collective-permute-start(bf16[64,256]{1,0:T(8,128)(2,1)S(1)} %target_others.1), channel_id=1, source_target_pairs={{0,2},{2,0},{1,3},{3,1},{4,6},{6,4},{5,7},{7,5},{8,10},{10,8},{9,1... | collective-permute-start | bytes 98312 | tf_op jit(solution)/shard_map/ppermute | solution.py:346
  14.3 0.4 %target_mine.1 = f32[2,32,256]{2,1,0:T(8,128)S(1)} custom-call(f32[2,64,256]{2,1,0:T(8,128)S(1)} %get-tuple-element.21.total, bf16[2,33,2,32,256]{4,3,2,1,0:T(8,128)(2,1)S(1)} %get-tuple-element.22.spread, bf16[208,128]{1,0:T(8,128)(2,1)S(1)} %collective-permute-done.rest_0_, bf16[208,128]{1,0:T(8,128)(2,1)S(1)} %collective-permute-done.1.rest_1_, ...), custom_call_target="tpu_custom_call" | custom-call | tf_op jit(solution)/shard_map/target_mine/pallas_call | solution.py:333
  14.6 1.9 %collective-permute-done.3 = bf16[64,256]{1,0:T(8,128)(2,1)S(1)} collective-permute-done((bf16[64,256]{1,0:T(8,128)(2,1)S(1)}, bf16[64,256]{1,0:T(8,128)(2,1)S(1)}, u32[]{:S(2)}, u32[]{:S(2)}) %collective-permute-start.3) | collective-permute-done | bytes 32800 | tf_op jit(solution)/shard_map/ppermute | solution.py:346
  16.5 0.6 %convert_add_fusion = f32[2,32,256]{2,1,0:T(8,128)} fusion(f32[2,32,256]{2,1,0:T(8,128)S(1)} %target_mine.1, bf16[2,32,256]{2,1,0:T(8,128)(2,1)S(1)} %bitcast.2), kind=kLoop, calls=%fused_computation | loop fusion | flops 32768 | bytes 163840 | tf_op jit(solution)/shard_map/add | solution.py:351
Async XLA Ops:
  1.9 7.4 %copy-start = (bf16[1,1,56,2,128,128]{5,4,3,2,1,0:T(8,128)(2,1)S(1)}, bf16[1,1,56,2,128,128]{5,4,3,2,1,0:T(8,128)(2,1)}, u32[]{:S(2)}) copy-start(bf16[1,1,56,2,128,128]{5,4,3,2,1,0:T(8,128)(2,1)} %near_blocks.3) | copy-start | bytes 11010052
  1.9 7.4 %copy-start.1 = (s32[1,1,56]{2,1,0:T(1,128)S(1)}, s32[1,1,56]{2,1,0:T(1,128)}, u32[]{:S(2)}) copy-start(s32[1,1,56]{2,1,0:T(1,128)} %near_src.3) | copy-start | bytes 676
  1.9 7.3 %copy-start.2 = (s32[1,1,56]{2,1,0:T(1,128)S(1)}, s32[1,1,56]{2,1,0:T(1,128)}, u32[]{:S(2)}) copy-start(s32[1,1,56]{2,1,0:T(1,128)} %near_tgt.3) | copy-start | bytes 676
  1.9 7.3 %copy-start.3 = (bf16[1,1,32,2,32,128]{5,4,3,2,1,0:T(8,128)(2,1)S(1)}, bf16[1,1,32,2,32,128]{5,4,3,2,1,0:T(8,128)(2,1)}, u32[]{:S(2)}) copy-start(bf16[1,1,32,2,32,128]{5,4,3,2,1,0:T(8,128)(2,1)} %far_u.1) | copy-start | bytes 1572868
  1.9 7.3 %copy-start.4 = (s32[1,1,32]{2,1,0:T(1,128)S(1)}, s32[1,1,32]{2,1,0:T(1,128)}, u32[]{:S(2)}) copy-start(s32[1,1,32]{2,1,0:T(1,128)} %far_tgt.1) | copy-start | bytes 388
  2.2 9.5 %collective-permute-start = (bf16[208,128]{1,0:T(8,128)(2,1)S(1)}, bf16[208,128]{1,0:T(8,128)(2,1)S(1)}, u32[]{:S(2)}, u32[]{:S(2)}) collective-permute-start(bf16[208,128]{1,0:T(8,128)(2,1)S(1)} %get-tuple-element.28), channel_id=1, source_target_pairs={{0,4},{4,8},{8,12},{12,0},{1,5},{5,9},{9,13},{13,1},{2,6},{6,10},{... | collective-permute-start | bytes 159752 | tf_op jit(solution)/shard_map/ppermute | solution.py:317
  5.3 6.4 %collective-permute-start.1 = (bf16[208,128]{1,0:T(8,128)(2,1)S(1)}, bf16[208,128]{1,0:T(8,128)(2,1)S(1)}, u32[]{:S(2)}, u32[]{:S(2)}) collective-permute-start(bf16[208,128]{1,0:T(8,128)(2,1)S(1)} %get-tuple-element.29), channel_id=1, source_target_pairs={{0,8},{4,12},{8,0},{12,4},{1,9},{5,13},{9,1},{13,5},{2,10},{6,14},... | collective-permute-start | bytes 159752 | tf_op jit(solution)/shard_map/ppermute | solution.py:317
  7.9 4.3 %collective-permute-start.2 = (bf16[208,128]{1,0:T(8,128)(2,1)S(1)}, bf16[208,128]{1,0:T(8,128)(2,1)S(1)}, u32[]{:S(2)}, u32[]{:S(2)}) collective-permute-start(bf16[208,128]{1,0:T(8,128)(2,1)S(1)} %get-tuple-element.30), channel_id=1, source_target_pairs={{0,12},{4,0},{8,4},{12,8},{1,13},{5,1},{9,5},{13,9},{2,14},{6,2},{... | collective-permute-start | bytes 159752 | tf_op jit(solution)/shard_map/ppermute | solution.py:317
  12.6 4.0 %collective-permute-start.3 = (bf16[64,256]{1,0:T(8,128)(2,1)S(1)}, bf16[64,256]{1,0:T(8,128)(2,1)S(1)}, u32[]{:S(2)}, u32[]{:S(2)}) collective-permute-start(bf16[64,256]{1,0:T(8,128)(2,1)S(1)} %target_others.1), channel_id=1, source_target_pairs={{0,2},{2,0},{1,3},{3,1},{4,6},{6,4},{5,7},{7,5},{8,10},{10,8},{9,1... | collective-permute-start | bytes 98312 | tf_op jit(solution)/shard_map/ppermute | solution.py:346

commit v6 on v5

--- a/solution.py
+++ b/solution.py
@@ -13,7 +13,7 @@
 PACK = 4
 BASE = 64
 LIMIT = 24 << 20
-MESSAGE_FLOPS = 2 * 10**9
+HAND_ON_FLOPS = 2 * 10**9
 VMEM = pl.BlockSpec(memory_space=pltpu.VMEM)
 SMEM = pl.BlockSpec(memory_space=pltpu.SMEM)
 HBM = pl.BlockSpec(memory_space=pltpu.HBM)
@@ -44,10 +44,11 @@
     return jnp.dot(left, right, preferred_element_type=jnp.float32)
 
 
-def coeff_kernel(owners, depth, far_src, far_dst, near_src, near_tgt, incident, far_v, near_blocks,
-                 field, labels, aimed_out, picked, *rest):
-    coeffs, rest = rest[:owners], rest[owners:]
-    src_f, dst_f, tgt_row, src_row, waves, factors, ordered, source_of, counts, sems, pick_sems = rest
+def send_kernel(owners, depth, far_src, far_dst, near_src, near_tgt, incident, far_v, near_blocks,
+                field, labels, own_coeffs, *rest):
+    messages, rest = rest[:owners - 1], rest[owners - 1:]
+    src_f, dst_f, tgt_row, src_row, waves, factors, picked, ordered, source_of, counts, sems, pick_sem = rest
+    coeffs = (own_coeffs,) + messages
     me = lax.axis_index("src")
     half = waves.shape[1]
     rows = 2 * half
@@ -71,21 +72,19 @@
     near_in.wait()
     targets = tgt_row[0]
     position = lax.broadcasted_iota(jnp.int32, targets.shape, 1)
-    line = lax.broadcasted_iota(jnp.int32, (aimed_out.shape[0], 1), 0)
+    line = lax.broadcasted_iota(jnp.int32, (-(-2 * (owners - 1) // 8) * 8, 1), 0)
     low = wrap(me + 1 + line // 2, owners) * clusters
     aimed = (targets >= low) & (targets < low + clusters)
     found = jnp.where(line % 2 == 0, count - 1 - position, position)
     found = (found * clusters + src_row[0]) * clusters + targets - low
     found = jnp.max(jnp.where(aimed, found, -1).astype(jnp.float32), axis=1, keepdims=True)
-    aimed_out[...] = jnp.broadcast_to(found.astype(jnp.int32), aimed_out.shape)
-
-    picks = []
+    found = found.astype(jnp.int32)
+    near_from = []
     for at in range(2 * (owners - 1)):
-        where = div_by(jnp.maximum(found[at, 0].astype(jnp.int32), 0), clusters * clusters)
-        if at % 2 == 0:
-            where = count - 1 - where
-        picks.append(pltpu.make_async_copy(near_blocks.at[0, 0, where], picked.at[at], pick_sems.at[at]))
-        picks[-1].start()
+        number = found[at, 0]
+        near_from.append((number, div_by(jnp.maximum(number, 0), clusters * clusters)))
+        where = near_from[-1][1] if at % 2 else count - 1 - near_from[-1][1]
+        pltpu.make_async_copy(near_blocks.at[0, 0, where], picked.at[at], pick_sem).start()
 
     waves_in.wait()
     for s in range(clusters):
@@ -139,40 +138,34 @@
             for s in range(1, clusters):
                 chosen = jnp.where(source == s, part[s * rows:(s + 1) * rows], chosen)
             coeffs[k][chunk * rows:(chunk + 1) * rows, :] = chosen.astype(jnp.bfloat16)
-    for pick in picks:
-        pick.wait()
-
-
-def message_kernel(owners, count, field, labels, aimed, picked, *rest):
-    coeffs, messages = rest[:owners - 1], rest[owners - 1:]
-    depth_rows = coeffs[0].shape[0]
-    rows = messages[0].shape[0] - depth_rows - LABEL_ROWS
-    clusters = field.shape[0] // rows
-    lane = lax.broadcasted_iota(jnp.int32, (1, LANES), 1)
     near_labels = jnp.zeros((1, LANES), jnp.int32)
-    every = aimed[...]
-    for k, (message, part) in enumerate(zip(messages, coeffs), 1):
-        first, last = every[2 * k - 2, 0], every[2 * k - 1, 0]
-        filled = first >= 0
-        positions, left, right = [], [], []
-        for number in (jnp.maximum(first, 0), jnp.maximum(last, 0)):
-            above = div_by(number, clusters)
-            positions.append(div_by(above, clusters))
-            source = above - positions[-1] * clusters
-            left.append(field[pl.ds(pl.multiple_of(source * rows, rows), rows), :])
-            target = number - above * clusters
-        positions[0] = count - 1 - positions[0]
+    lefts = []
+    for k in range(1, owners):
+        filled = near_from[2 * k - 2][0] >= 0
+        two = near_from[2 * k - 1][1] > count - 1 - near_from[2 * k - 2][1]
+        left = []
+        for at, used in ((2 * k - 2, filled), (2 * k - 1, filled & two)):
+            number, above = near_from[at]
+            number = jnp.maximum(number, 0) - above * (clusters * clusters)
+            source = div_by(number, clusters)
+            target = number - source * clusters
+            values = field[pl.ds(pl.multiple_of(source * rows, rows), rows), :]
+            left.append(jnp.where(used, values, jnp.zeros_like(values)))
+        lefts.append(jnp.concatenate(left, axis=1))
         near_labels = jnp.where(lane == k, jnp.where(filled, target + 1, 0), near_labels)
-        for i, used in enumerate((filled, positions[1] > positions[0])):
-            left[i] = jnp.where(used & filled, left[i], jnp.zeros_like(left[i]))
-            right += [picked[2 * (k - 1) + i, c] for c in range(2)]
-        total = dot_nt(jnp.concatenate(left, axis=1), jnp.concatenate(right, axis=1))
-        message[0:depth_rows, :] = part[...]
-        message[depth_rows:depth_rows + rows, :] = total.astype(jnp.bfloat16)
     near_tile = jnp.broadcast_to(near_labels, (8, LANES)).astype(jnp.float32)
     tile = jnp.concatenate([labels[...], near_tile], axis=0).astype(jnp.bfloat16)
     for message in messages:
-        message[depth_rows + rows:, :] = tile
+        message[(chunks + 1) * rows:, :] = tile
+    pltpu.make_async_copy(picked, picked, pick_sem).wait()
+    for k, message in enumerate(messages):
+        right = jnp.concatenate([picked[2 * k + i, c] for i in range(2) for c in range(2)], axis=1)
+        message[chunks * rows:(chunks + 1) * rows, :] = dot_nt(lefts[k], right).astype(jnp.bfloat16)
+
+
+def hand_on_kernel(*refs):
+    for a, b in zip(refs[:len(refs) // 2], refs[len(refs) // 2:]):
+        b[...] = a[...]
 
 
 def read_labels(depth, used, k, far_tile, near_tile):
@@ -243,16 +236,12 @@
             total[holder, :, c * PANEL:(c + 1) * PANEL] = sums[holder * share + c]
 
 
-def target_kernel(owners, depth, used, steps, total, spread, *rest):
-    messages, outs = rest[:owners - 1], rest[owners - 1:]
-    sharers, rows, width = total.shape
-    share = width // PANEL
+def add_messages(depth, used, first, messages, holders, sums, spread):
+    rows = sums[0].shape[0]
+    share = sums[0].shape[1] // PANEL
     chunks = depth * spread.shape[3] // LANES
-    me = lax.axis_index("tgt")
-    holders = [wrap(me + step, sharers) for step in steps]
-    sums = [total[holder] for holder in holders]
     read = []
-    for k, message in enumerate(messages, 1):
+    for k, message in enumerate(messages, first):
         tile = message[(chunks + 1) * rows:, :].astype(jnp.float32)
         read.append(read_labels(depth, used, k, tile[0:8], tile[8:16]))
     for message, (slots, label) in zip(messages, read):
@@ -262,6 +251,21 @@
             part = [jnp.where(label == holder * share + c + 1, near, 0.0) for c in range(share)]
             sums[i] = sums[i] + jnp.concatenate(part, axis=1)
             sums[i] = sums[i] + dot_nn(left, far_matrix(depth, holder, slots, spread))
+    return sums
+
+
+def first_target_kernel(depth, used, total, spread, *rest):
+    messages, out = rest[:-1], rest[-1]
+    holders = range(total.shape[0])
+    sums = add_messages(depth, used, 1, messages, holders, [total[holder] for holder in holders], spread)
+    for holder in holders:
+        out[holder] = sums[holder]
+
+
+def last_target_kernel(depth, used, last, steps, total, spread, message, *outs):
+    me = lax.axis_index("tgt")
+    holders = [wrap(me + step, total.shape[0]) for step in steps]
+    sums = add_messages(depth, used, last, [message], holders, [total[holder] for holder in holders], spread)
     for out, value in zip(outs, sums):
         out[...] = value.astype(out.dtype).reshape(out.shape)
 
@@ -281,38 +285,38 @@
     bf16, f32, i32 = jnp.bfloat16, jnp.float32, jnp.int32
     shape = jax.ShapeDtypeStruct
 
-    lines = -(-2 * (owners - 1) // 8) * 8
     near_count = near_blocks.shape[2]
-    field, labels, aimed, picked, own_coeffs, *coeffs = pl.pallas_call(
-        functools.partial(coeff_kernel, owners, depth),
-        out_shape=[shape((clusters * rows, 2 * PANEL), bf16), shape((8, LANES), f32), shape((lines, LANES), i32)]
-        + [shape((2 * (owners - 1),) + near_blocks.shape[3:], bf16)]
-        + [shape((chunks * rows, LANES), bf16)] * owners,
+    message_shape = shape(((chunks + 1) * rows + LABEL_ROWS, LANES), bf16)
+    field, labels, own_coeffs, *messages = pl.pallas_call(
+        functools.partial(send_kernel, owners, depth),
+        out_shape=[shape((clusters * rows, 2 * PANEL), bf16), shape((8, LANES), f32), shape((chunks * rows, LANES), bf16)]
+        + [message_shape] * (owners - 1),
         in_specs=[HBM] * 7,
-        out_specs=[VMEM] * (4 + owners),
+        out_specs=[VMEM] * (2 + owners),
         scratch_shapes=[
             pltpu.SMEM(far_src.shape, i32), pltpu.SMEM(far_dst.shape, i32),
             pltpu.VMEM(near_tgt.shape, i32), pltpu.VMEM(near_src.shape, i32),
             pltpu.VMEM(incident.shape, bf16),
             pltpu.VMEM(far_v.shape, bf16),
+            pltpu.VMEM((2 * (owners - 1),) + near_blocks.shape[3:], bf16),
             pltpu.VMEM((owners * depth * rank, 2 * PANEL), bf16),
             pltpu.SMEM((owners * depth,), i32),
             pltpu.SMEM((owners,), i32),
             pltpu.SemaphoreType.DMA((6,)),
-            pltpu.SemaphoreType.DMA((2 * (owners - 1),)),
+            pltpu.SemaphoreType.DMA,
         ],
         compiler_params=PARAMS,
-        name="coefficients",
+        name="send",
     )(*map(in_hbm, (far_src, far_dst, near_src, near_tgt, incident, far_v, near_blocks)))
     messages = pl.pallas_call(
-        functools.partial(message_kernel, owners, near_count),
-        out_shape=[shape(((chunks + 1) * rows + LABEL_ROWS, LANES), bf16)] * (owners - 1),
-        in_specs=[VMEM] * (3 + owners),
+        hand_on_kernel,
+        out_shape=[message_shape] * (owners - 1),
+        in_specs=[VMEM] * (owners - 1),
         out_specs=[VMEM] * (owners - 1),
         compiler_params=PARAMS,
-        cost_estimate=pl.CostEstimate(flops=MESSAGE_FLOPS, bytes_accessed=0, transcendentals=0),
-        name="messages",
-    )(field, labels, aimed, picked, *coeffs)
+        cost_estimate=pl.CostEstimate(flops=HAND_ON_FLOPS, bytes_accessed=0, transcendentals=0),
+        name="hand_on",
+    )(*messages)
     arrived = [
         lax.ppermute(message, "src", [(s, (s + k) % owners) for s in range(owners)])
         for k, message in enumerate(messages, 1)
@@ -329,15 +333,25 @@
         name="own",
     )(near_src, near_tgt, far_tgt, field, labels, own_coeffs, far_u, near_blocks)
 
+    if owners > 2:
+        total = pl.pallas_call(
+            functools.partial(first_target_kernel, depth, used),
+            out_shape=shape((sharers, rows, width), f32),
+            in_specs=[VMEM] * owners,
+            out_specs=VMEM,
+            compiler_params=PARAMS,
+            name="target_first",
+        )(total, spread, *arrived[:-1])
+
     def target(steps, dtype, dims, name):
         return pl.pallas_call(
-            functools.partial(target_kernel, owners, depth, used, steps),
+            functools.partial(last_target_kernel, depth, used, owners - 1, steps),
             out_shape=[shape(dims, dtype)] * len(steps),
-            in_specs=[VMEM] * (2 + owners - 1),
+            in_specs=[VMEM] * 3,
             out_specs=[VMEM] * len(steps),
             compiler_params=PARAMS,
             name=name,
-        )(total, spread, *arrived)
+        )(total, spread, arrived[-1])
 
     received = []
     if sharers > 1:

time: 17.3 us -> 17.2 us (level)
  waiting for transfers between devices: 2.36 us -> 1.78 us
  Pallas kernels: 5.35 us -> 5.61 us
  starting transfers between devices: 8.71 us -> 8.91 us
    ppermute x3, waiting for transfers between devices: 0.45 us -> 0.01 us  [body(): lax.ppermute(message, 'src', [(s, (s + k) % owners) for s in range(owners)])]
    pallas_call x4 -> x5, Pallas kernels: 2.93 us -> 3.15 us  [the longest x1 2.11 us: body(): pl.pallas_call(functools.partial(send_kernel, owners, depth), out_shape=[...]
    ppermute x1, starting transfers between devices: 1.69 us -> 1.91 us  [body(): lax.ppermute(other, 'tgt', [(t, (t + k) % sharers) for t in range(sharers)])]
  transfers between devices with their start and end apart: 4 -> 4, of which waited for: 2 -> 1; matrix products, arithmetic and copies ran while one was open for 0% -> 0% of each run, Pallas kernels for 16% -> 19%
where the time goes in v6:
time: 17.2 us; the launch traced here: 17.1 us
  starting transfers between devices  8.91 us (52%)
  Pallas kernels  5.61 us (33%)
  waiting for transfers between devices  1.78 us (10%)
  other arithmetic  0.64 us (4%)
    ppermute x3, starting transfers between devices, body(): lax.ppermute(message, 'src', [(s, (s + k) % owners) for s in range(owners)])  7 us
    pallas_call x1, Pallas kernels, body(): pl.pallas_call(functools.partial(own_kernel, depth, used), out_shape=[sha...  2.46 us
    pallas_call x1, Pallas kernels, body(): pl.pallas_call(functools.partial(send_kernel, owners, depth), out_shape=[...  2.11 us
    ppermute x1, starting transfers between devices, body(): lax.ppermute(other, 'tgt', [(t, (t + k) % sharers) for t in range(sharers)])  1.91 us
    ppermute x1, waiting for transfers between devices, body(): lax.ppermute(other, 'tgt', [(t, (t + k) % sharers) for t in range(sharers)])  1.77 us
    add x1, other arithmetic, body(): result = result + other.astype(f32).reshape(result.shape)  0.64 us
    pallas_call x2, Pallas kernels, target(): pl.pallas_call(functools.partial(last_target_kernel, depth, used, owners...  0.6 us
    pallas_call x1, Pallas kernels, body(): pl.pallas_call(functools.partial(first_target_kernel, depth, used), out_s...  0.43 us
  transfers between devices with their start and end apart: 4, of which 1 were waited for; matrix products, arithmetic and copies ran while one was open for 0% of the time, Pallas kernels for 19%

profile of v6, /device:TPU:0, one launch (start us, length us, event | category | flops | bytes accessed | tf_op | source)
XLA Modules:
  0.0 17.1 jit_solution(3774024884160916344)
XLA Ops:
  0.0 2.1 %send.1 = (bf16[256,256]{1,0:T(8,128)(2,1)S(1)}, f32[8,128]{1,0:T(8,128)S(1)}, bf16[128,128]{1,0:T(8,128)(2,1)S(1)}, bf16[208,128]{1,0:T(8,128)(2,1)S(1)}, bf16[...) custom-call(s32[1,1,32]{2,1,0:T(1,128)} %far_src.1, s32[1,1,32]{2,1,0:T(1,128)} %far_dst.1, s32[1,1,56]{2,1,0:T(1,128)} %near_src.3, ...), custom_call_target="tpu_custom_call" | custom-call | tf_op jit(solution)/shard_map/send/pallas_call | solution.py:290
  2.1 0.0 copy-start
  2.1 0.0 copy-start.1
  2.1 0.0 copy-start.2
  2.2 0.0 copy-start.3
  2.2 0.0 copy-start.4
  2.2 3.1 %collective-permute-start = (bf16[208,128]{1,0:T(8,128)(2,1)S(1)}, bf16[208,128]{1,0:T(8,128)(2,1)S(1)}, u32[]{:S(2)}, u32[]{:S(2)}) collective-permute-start(bf16[208,128]{1,0:T(8,128)(2,1)S(1)} %get-tuple-element.24), channel_id=1, source_target_pairs={{0,4},{4,8},{8,12},{12,0},{1,5},{5,9},{9,13},{13,1},{2,6},{6,10},{... | collective-permute-start | bytes 159752 | tf_op jit(solution)/shard_map/ppermute | solution.py:321
  5.3 2.6 %collective-permute-start.1 = (bf16[208,128]{1,0:T(8,128)(2,1)S(1)}, bf16[208,128]{1,0:T(8,128)(2,1)S(1)}, u32[]{:S(2)}, u32[]{:S(2)}) collective-permute-start(bf16[208,128]{1,0:T(8,128)(2,1)S(1)} %get-tuple-element.25), channel_id=1, source_target_pairs={{0,8},{4,12},{8,0},{12,4},{1,9},{5,13},{9,1},{13,5},{2,10},{6,14},... | collective-permute-start | bytes 159752 | tf_op jit(solution)/shard_map/ppermute | solution.py:321
  7.9 1.3 %collective-permute-start.2 = (bf16[208,128]{1,0:T(8,128)(2,1)S(1)}, bf16[208,128]{1,0:T(8,128)(2,1)S(1)}, u32[]{:S(2)}, u32[]{:S(2)}) collective-permute-start(bf16[208,128]{1,0:T(8,128)(2,1)S(1)} %get-tuple-element.26), channel_id=1, source_target_pairs={{0,12},{4,0},{8,4},{12,8},{1,13},{5,1},{9,5},{13,9},{2,14},{6,2},{... | collective-permute-start | bytes 159752 | tf_op jit(solution)/shard_map/ppermute | solution.py:321
  9.2 0.0 copy-done
  9.2 0.0 copy-done.1
  9.2 0.0 copy-done.2
  9.2 0.0 copy-done.3
  9.2 0.0 copy-done.4
  9.2 2.5 %own.1 = (f32[2,64,256]{2,1,0:T(8,128)S(1)}, bf16[2,33,2,32,256]{4,3,2,1,0:T(8,128)(2,1)S(1)}) custom-call(s32[1,1,56]{2,1,0:T(1,128)S(1)} %copy-done.1, s32[1,1,56]{2,1,0:T(1,128)S(1)} %copy-done.2, s32[1,1,32]{2,1,0:T(1,128)S(1)} %copy-done.4, bf16[256,256]{1,0:T(8,128)(2,1)S(1)} %get-tuple-element.16.field, f32[8,128]{1,0:T(8,128)S(1)} %get-tuple-element.17.labels, ...), custom_call_target="tpu_custom_call" | custom-call | flops 3758096384 | bytes 3670016 | tf_op jit(solution)/shard_map/own/pallas_call | solution.py:324
  11.7 0.0 collective-permute-done.rest_0_
  11.7 0.0 collective-permute-done.1.rest_1_
  11.7 0.4 %target_first.1.total = f32[2,64,256]{2,1,0:T(8,128)S(1)} custom-call(f32[2,64,256]{2,1,0:T(8,128)S(1)} %get-tuple-element.19.total, bf16[2,33,2,32,256]{4,3,2,1,0:T(8,128)(2,1)S(1)} %get-tuple-element.20.spread, bf16[208,128]{1,0:T(8,128)(2,1)S(1)} %collective-permute-done.rest_0_, bf16[208,128]{1,0:T(8,128)(2,1)S(1)} %collective-permute-done.1.rest_1_), custom_call_target="tpu_custom_call" | custom-call | tf_op jit(solution)/shard_map/target_first/pallas_call | solution.py:337
  12.2 0.0 collective-permute-done.2.message
  12.2 0.3 %target_others.1 = bf16[64,256]{1,0:T(8,128)(2,1)S(1)} custom-call(f32[2,64,256]{2,1,0:T(8,128)S(1)} %target_first.1.total, bf16[2,33,2,32,256]{4,3,2,1,0:T(8,128)(2,1)S(1)} %get-tuple-element.20.spread, bf16[208,128]{1,0:T(8,128)(2,1)S(1)} %collective-permute-done.2.message), custom_call_target="tpu_custom_call" | custom-call | tf_op jit(solution)/shard_map/target_others/pallas_call | solution.py:347
  12.5 1.9 %collective-permute-start.3 = (bf16[64,256]{1,0:T(8,128)(2,1)S(1)}, bf16[64,256]{1,0:T(8,128)(2,1)S(1)}, u32[]{:S(2)}, u32[]{:S(2)}) collective-permute-start(bf16[64,256]{1,0:T(8,128)(2,1)S(1)} %target_others.1), channel_id=1, source_target_pairs={{0,2},{2,0},{1,3},{3,1},{4,6},{6,4},{5,7},{7,5},{8,10},{10,8},{9,1... | collective-permute-start | bytes 98312 | tf_op jit(solution)/shard_map/ppermute | solution.py:360
  14.4 0.3 %target_mine.1 = f32[2,32,256]{2,1,0:T(8,128)S(1)} custom-call(f32[2,64,256]{2,1,0:T(8,128)S(1)} %target_first.1.total, bf16[2,33,2,32,256]{4,3,2,1,0:T(8,128)(2,1)S(1)} %get-tuple-element.20.spread, bf16[208,128]{1,0:T(8,128)(2,1)S(1)} %collective-permute-done.2.message), custom_call_target="tpu_custom_call" | custom-call | tf_op jit(solution)/shard_map/target_mine/pallas_call | solution.py:347
  14.7 1.8 %collective-permute-done.3 = bf16[64,256]{1,0:T(8,128)(2,1)S(1)} collective-permute-done((bf16[64,256]{1,0:T(8,128)(2,1)S(1)}, bf16[64,256]{1,0:T(8,128)(2,1)S(1)}, u32[]{:S(2)}, u32[]{:S(2)}) %collective-permute-start.3) | collective-permute-done | bytes 32800 | tf_op jit(solution)/shard_map/ppermute | solution.py:360
  16.4 0.6 %convert_add_fusion = f32[2,32,256]{2,1,0:T(8,128)} fusion(f32[2,32,256]{2,1,0:T(8,128)S(1)} %target_mine.1, bf16[2,32,256]{2,1,0:T(8,128)(2,1)S(1)} %bitcast.2), kind=kLoop, calls=%fused_computation | loop fusion | flops 32768 | bytes 163840 | tf_op jit(solution)/shard_map/add | solution.py:365
  (1 shorter events, 0.0 us)
Async XLA Ops:
  2.1 7.1 %copy-start = (bf16[1,1,56,2,128,128]{5,4,3,2,1,0:T(8,128)(2,1)S(1)}, bf16[1,1,56,2,128,128]{5,4,3,2,1,0:T(8,128)(2,1)}, u32[]{:S(2)}) copy-start(bf16[1,1,56,2,128,128]{5,4,3,2,1,0:T(8,128)(2,1)} %near_blocks.3) | copy-start | bytes 11010052
  2.1 7.1 %copy-start.1 = (s32[1,1,56]{2,1,0:T(1,128)S(1)}, s32[1,1,56]{2,1,0:T(1,128)}, u32[]{:S(2)}) copy-start(s32[1,1,56]{2,1,0:T(1,128)} %near_src.3) | copy-start | bytes 676
  2.1 7.1 %copy-start.2 = (s32[1,1,56]{2,1,0:T(1,128)S(1)}, s32[1,1,56]{2,1,0:T(1,128)}, u32[]{:S(2)}) copy-start(s32[1,1,56]{2,1,0:T(1,128)} %near_tgt.3) | copy-start | bytes 676
  2.2 7.1 %copy-start.3 = (bf16[1,1,32,2,32,128]{5,4,3,2,1,0:T(8,128)(2,1)S(1)}, bf16[1,1,32,2,32,128]{5,4,3,2,1,0:T(8,128)(2,1)}, u32[]{:S(2)}) copy-start(bf16[1,1,32,2,32,128]{5,4,3,2,1,0:T(8,128)(2,1)} %far_u.1) | copy-start | bytes 1572868
  2.2 7.1 %copy-start.4 = (s32[1,1,32]{2,1,0:T(1,128)S(1)}, s32[1,1,32]{2,1,0:T(1,128)}, u32[]{:S(2)}) copy-start(s32[1,1,32]{2,1,0:T(1,128)} %far_tgt.1) | copy-start | bytes 388
  2.2 9.5 %collective-permute-start = (bf16[208,128]{1,0:T(8,128)(2,1)S(1)}, bf16[208,128]{1,0:T(8,128)(2,1)S(1)}, u32[]{:S(2)}, u32[]{:S(2)}) collective-permute-start(bf16[208,128]{1,0:T(8,128)(2,1)S(1)} %get-tuple-element.24), channel_id=1, source_target_pairs={{0,4},{4,8},{8,12},{12,0},{1,5},{5,9},{9,13},{13,1},{2,6},{6,10},{... | collective-permute-start | bytes 159752 | tf_op jit(solution)/shard_map/ppermute | solution.py:321
  5.3 6.4 %collective-permute-start.1 = (bf16[208,128]{1,0:T(8,128)(2,1)S(1)}, bf16[208,128]{1,0:T(8,128)(2,1)S(1)}, u32[]{:S(2)}, u32[]{:S(2)}) collective-permute-start(bf16[208,128]{1,0:T(8,128)(2,1)S(1)} %get-tuple-element.25), channel_id=1, source_target_pairs={{0,8},{4,12},{8,0},{12,4},{1,9},{5,13},{9,1},{13,5},{2,10},{6,14},... | collective-permute-start | bytes 159752 | tf_op jit(solution)/shard_map/ppermute | solution.py:321
  7.9 4.3 %collective-permute-start.2 = (bf16[208,128]{1,0:T(8,128)(2,1)S(1)}, bf16[208,128]{1,0:T(8,128)(2,1)S(1)}, u32[]{:S(2)}, u32[]{:S(2)}) collective-permute-start(bf16[208,128]{1,0:T(8,128)(2,1)S(1)} %get-tuple-element.26), channel_id=1, source_target_pairs={{0,12},{4,0},{8,4},{12,8},{1,13},{5,1},{9,5},{13,9},{2,14},{6,2},{... | collective-permute-start | bytes 159752 | tf_op jit(solution)/shard_map/ppermute | solution.py:321
  12.5 4.0 %collective-permute-start.3 = (bf16[64,256]{1,0:T(8,128)(2,1)S(1)}, bf16[64,256]{1,0:T(8,128)(2,1)S(1)}, u32[]{:S(2)}, u32[]{:S(2)}) collective-permute-start(bf16[64,256]{1,0:T(8,128)(2,1)S(1)} %target_others.1), channel_id=1, source_target_pairs={{0,2},{2,0},{1,3},{3,1},{4,6},{6,4},{5,7},{7,5},{8,10},{10,8},{9,1... | collective-permute-start | bytes 98312 | tf_op jit(solution)/shard_map/ppermute | solution.py:360

commit v7 on v6

--- a/solution.py
+++ b/solution.py
@@ -9,10 +9,8 @@
 
 PANEL = 128
 LANES = 128
-LABEL_ROWS = 16
-PACK = 4
-BASE = 64
 LIMIT = 24 << 20
+LATE = 2
 HAND_ON_FLOPS = 2 * 10**9
 VMEM = pl.BlockSpec(memory_space=pltpu.VMEM)
 SMEM = pl.BlockSpec(memory_space=pltpu.SMEM)
@@ -28,6 +26,10 @@
     if size & (size - 1) == 0:
         return lax.shift_right_logical(value, jnp.int32(size.bit_length() - 1))
     return lax.div(value, jnp.int32(size))
+
+
+def label_count(depth):
+    return -(-(depth + 1) // 16) * 16
 
 
 def wrap(value, size):
@@ -103,7 +105,8 @@
         for k in range(owners):
             counts[k] = 0
     so_far = jnp.int32(0)
-    label_row = jnp.zeros((1, LANES), jnp.int32)
+    place_of = lax.broadcasted_iota(jnp.int32, labels.shape, 0)
+    label_rows = jnp.zeros(labels.shape, jnp.int32)
     factors_in.wait()
     for f in range(blocks):
         routed = dst_f[0, 0, f]
@@ -122,8 +125,8 @@
         ordered[at, 0:PANEL] = factors[0, 0, f, 0]
         ordered[at, PANEL:2 * PANEL] = factors[0, 0, f, 1]
         source_of[place] = src_f[0, 0, f]
-        label_row = jnp.where(lane == place, slot + 1, label_row)
-    labels[...] = jnp.broadcast_to(label_row, (8, LANES)).astype(jnp.float32)
+        label_rows = jnp.where(place_of == place, slot + 1, label_rows)
+    labels[...] = label_rows
 
     group = lane // rank
     everything = field[...]
@@ -138,9 +141,8 @@
             for s in range(1, clusters):
                 chosen = jnp.where(source == s, part[s * rows:(s + 1) * rows], chosen)
             coeffs[k][chunk * rows:(chunk + 1) * rows, :] = chosen.astype(jnp.bfloat16)
-    near_labels = jnp.zeros((1, LANES), jnp.int32)
     lefts = []
-    for k in range(1, owners):
+    for k, message in enumerate(messages, 1):
         filled = near_from[2 * k - 2][0] >= 0
         two = near_from[2 * k - 1][1] > count - 1 - near_from[2 * k - 2][1]
         left = []
@@ -152,11 +154,9 @@
             values = field[pl.ds(pl.multiple_of(source * rows, rows), rows), :]
             left.append(jnp.where(used, values, jnp.zeros_like(values)))
         lefts.append(jnp.concatenate(left, axis=1))
-        near_labels = jnp.where(lane == k, jnp.where(filled, target + 1, 0), near_labels)
-    near_tile = jnp.broadcast_to(near_labels, (8, LANES)).astype(jnp.float32)
-    tile = jnp.concatenate([labels[...], near_tile], axis=0).astype(jnp.bfloat16)
-    for message in messages:
-        message[(chunks + 1) * rows:, :] = tile
+        near_label = jnp.full((label_count(depth) - depth, LANES), jnp.where(filled, target + 1, 0), jnp.int32)
+        tile = jnp.concatenate([label_rows[k * depth:(k + 1) * depth], near_label], axis=0)
+        message[(chunks + 1) * rows:, :] = tile.astype(jnp.float32).astype(jnp.bfloat16)
     pltpu.make_async_copy(picked, picked, pick_sem).wait()
     for k, message in enumerate(messages):
         right = jnp.concatenate([picked[2 * k + i, c] for i in range(2) for c in range(2)], axis=1)
@@ -168,23 +168,8 @@
         b[...] = a[...]
 
 
-def read_labels(depth, used, k, far_tile, near_tile):
-    lane = lax.broadcasted_iota(jnp.int32, (8, LANES), 1) - k * depth
-    line = lax.broadcasted_iota(jnp.int32, (8, LANES), 0)
-    weight = jnp.zeros((8, LANES), jnp.float32)
-    for r in range(used):
-        weight = jnp.where((lane == r) & (line == r // PACK), float(BASE ** (r % PACK)), weight)
-    lines = -(-used // PACK)
-    values = far_tile * weight
-    if near_tile is not None:
-        values = values + jnp.where((lane == k - k * depth) & (line == lines), near_tile, 0.0)
-    sums = jnp.sum(values, axis=1, keepdims=True).astype(jnp.int32)
-    slots = []
-    for r in range(used):
-        if r % PACK == 0:
-            word = sums[r // PACK, 0]
-        slots.append(lax.shift_right_logical(word, jnp.int32((r % PACK) * (BASE.bit_length() - 1))) & (BASE - 1))
-    return slots, (sums[lines, 0] if near_tile is not None else None)
+def read_labels(used, tile):
+    return [tile[r, 0] for r in range(used)]
 
 
 def far_operands(depth, chunks, rows, coeffs):
@@ -219,7 +204,7 @@
             for c in range(clusters):
                 to = (c % share) * PANEL
                 spread[c // share, slot + 1, part, :, to:to + PANEL] = jnp.where(cluster == c, factor, zero)
-    slots, _ = read_labels(depth, used, 0, labels[...], None)
+    slots = read_labels(used, labels[0:depth, :])
     left = far_operands(depth, chunks, rows, own_coeffs)
     for holder in range(sharers):
         far = dot_nn(left, far_matrix(depth, holder, slots, spread))
@@ -236,14 +221,14 @@
             total[holder, :, c * PANEL:(c + 1) * PANEL] = sums[holder * share + c]
 
 
-def add_messages(depth, used, first, messages, holders, sums, spread):
+def add_messages(depth, used, messages, holders, sums, spread):
     rows = sums[0].shape[0]
     share = sums[0].shape[1] // PANEL
     chunks = depth * spread.shape[3] // LANES
     read = []
-    for k, message in enumerate(messages, first):
-        tile = message[(chunks + 1) * rows:, :].astype(jnp.float32)
-        read.append(read_labels(depth, used, k, tile[0:8], tile[8:16]))
+    for message in messages:
+        tile = message[(chunks + 1) * rows:, :].astype(jnp.float32).astype(jnp.int32)
+        read.append((read_labels(used, tile), tile[depth, 0]))
     for message, (slots, label) in zip(messages, read):
         near = message[chunks * rows:(chunks + 1) * rows, :].astype(jnp.float32)
         left = far_operands(depth, chunks, rows, message)
@@ -257,15 +242,16 @@
 def first_target_kernel(depth, used, total, spread, *rest):
     messages, out = rest[:-1], rest[-1]
     holders = range(total.shape[0])
-    sums = add_messages(depth, used, 1, messages, holders, [total[holder] for holder in holders], spread)
+    sums = add_messages(depth, used, messages, holders, [total[holder] for holder in holders], spread)
     for holder in holders:
         out[holder] = sums[holder]
 
 
-def last_target_kernel(depth, used, last, steps, total, spread, message, *outs):
+def last_target_kernel(depth, used, late, steps, total, spread, *rest):
+    messages, outs = rest[:late], rest[late:]
     me = lax.axis_index("tgt")
     holders = [wrap(me + step, total.shape[0]) for step in steps]
-    sums = add_messages(depth, used, last, [message], holders, [total[holder] for holder in holders], spread)
+    sums = add_messages(depth, used, messages, holders, [total[holder] for holder in holders], spread)
     for out, value in zip(outs, sums):
         out[...] = value.astype(out.dtype).reshape(out.shape)
 
@@ -286,10 +272,10 @@
     shape = jax.ShapeDtypeStruct
 
     near_count = near_blocks.shape[2]
-    message_shape = shape(((chunks + 1) * rows + LABEL_ROWS, LANES), bf16)
+    message_shape = shape(((chunks + 1) * rows + label_count(depth), LANES), bf16)
     field, labels, own_coeffs, *messages = pl.pallas_call(
         functools.partial(send_kernel, owners, depth),
-        out_shape=[shape((clusters * rows, 2 * PANEL), bf16), shape((8, LANES), f32), shape((chunks * rows, LANES), bf16)]
+        out_shape=[shape((clusters * rows, 2 * PANEL), bf16), shape((owners * depth, LANES), i32), shape((chunks * rows, LANES), bf16)]
         + [message_shape] * (owners - 1),
         in_specs=[HBM] * 7,
         out_specs=[VMEM] * (2 + owners),
@@ -333,25 +319,26 @@
         name="own",
     )(near_src, near_tgt, far_tgt, field, labels, own_coeffs, far_u, near_blocks)
 
-    if owners > 2:
+    late = min(LATE, len(arrived))
+    if late < len(arrived):
         total = pl.pallas_call(
             functools.partial(first_target_kernel, depth, used),
             out_shape=shape((sharers, rows, width), f32),
-            in_specs=[VMEM] * owners,
+            in_specs=[VMEM] * (2 + len(arrived) - late),
             out_specs=VMEM,
             compiler_params=PARAMS,
             name="target_first",
-        )(total, spread, *arrived[:-1])
+        )(total, spread, *arrived[:len(arrived) - late])
 
     def target(steps, dtype, dims, name):
         return pl.pallas_call(
-            functools.partial(last_target_kernel, depth, used, owners - 1, steps),
+            functools.partial(last_target_kernel, depth, used, late, steps),
             out_shape=[shape(dims, dtype)] * len(steps),
-            in_specs=[VMEM] * 3,
+            in_specs=[VMEM] * (2 + late),
             out_specs=[VMEM] * len(steps),
             compiler_params=PARAMS,
             name=name,
-        )(total, spread, arrived[-1])
+        )(total, spread, *arrived[len(arrived) - late:])
 
     received = []
     if sharers > 1:

time: 17.2 us -> 17.2 us (level)
  waiting for transfers between devices: 1.78 us -> 2.18 us
  Pallas kernels: 5.61 us -> 5.34 us
  starting transfers between devices: 8.91 us -> 8.71 us
    ppermute x1, waiting for transfers between devices: 1.77 us -> 2.01 us  [body(): lax.ppermute(other, 'tgt', [(t, (t + k) % sharers) for t in range(sharers)])]
    ppermute x1, starting transfers between devices: 1.91 us -> 1.7 us  [body(): lax.ppermute(other, 'tgt', [(t, (t + k) % sharers) for t in range(sharers)])]
    pallas_call x1, Pallas kernels: 0.43 us -> 0.25 us  [body(): pl.pallas_call(functools.partial(first_target_kernel, depth, used), out_s...]
  transfers between devices with their start and end apart: 4 -> 4, of which waited for: 1 -> 2; matrix products, arithmetic and copies ran while one was open for 0% -> 0% of each run, Pallas kernels for 19% -> 17%
where the time goes in v7:
time: 17.2 us; the launch traced here: 17 us
  starting transfers between devices  8.71 us (51%)
  Pallas kernels  5.34 us (31%)
  waiting for transfers between devices  2.18 us (13%)
  other arithmetic  0.64 us (4%)
    ppermute x3, starting transfers between devices, body(): lax.ppermute(message, 'src', [(s, (s + k) % owners) for s in range(owners)])  7 us
    pallas_call x1, Pallas kernels, body(): pl.pallas_call(functools.partial(own_kernel, depth, used), out_shape=[sha...  2.45 us
    pallas_call x1, Pallas kernels, body(): pl.pallas_call(functools.partial(send_kernel, owners, depth), out_shape=[...  2.11 us
    ppermute x1, waiting for transfers between devices, body(): lax.ppermute(other, 'tgt', [(t, (t + k) % sharers) for t in range(sharers)])  2.01 us
    ppermute x1, starting transfers between devices, body(): lax.ppermute(other, 'tgt', [(t, (t + k) % sharers) for t in range(sharers)])  1.7 us
    add x1, other arithmetic, body(): result = result + other.astype(f32).reshape(result.shape)  0.64 us
    pallas_call x2, Pallas kernels, target(): pl.pallas_call(functools.partial(last_target_kernel, depth, used, late, s...  0.51 us
  transfers between devices with their start and end apart: 4, of which 2 were waited for; matrix products, arithmetic and copies ran while one was open for 0% of the time, Pallas kernels for 17%

profile of v7, /device:TPU:0, one launch (start us, length us, event | category | flops | bytes accessed | tf_op | source)
XLA Modules:
  0.0 17.0 jit_solution(2576856743056503565)
XLA Ops:
  0.0 2.1 %send.1 = (bf16[256,256]{1,0:T(8,128)(2,1)S(1)}, s32[32,128]{1,0:T(8,128)S(1)}, bf16[128,128]{1,0:T(8,128)(2,1)S(1)}, bf16[208,128]{1,0:T(8,128)(2,1)S(1)}, bf16...) custom-call(s32[1,1,32]{2,1,0:T(1,128)} %far_src.1, s32[1,1,32]{2,1,0:T(1,128)} %far_dst.1, s32[1,1,56]{2,1,0:T(1,128)} %near_src.3, ...), custom_call_target="tpu_custom_call" | custom-call | tf_op jit(solution)/shard_map/send/pallas_call | solution.py:276
  2.1 0.0 copy-start
  2.1 0.0 copy-start.1
  2.1 0.0 copy-start.2
  2.2 0.0 copy-start.3
  2.2 0.0 copy-start.4
  2.2 3.1 %collective-permute-start = (bf16[208,128]{1,0:T(8,128)(2,1)S(1)}, bf16[208,128]{1,0:T(8,128)(2,1)S(1)}, u32[]{:S(2)}, u32[]{:S(2)}) collective-permute-start(bf16[208,128]{1,0:T(8,128)(2,1)S(1)} %get-tuple-element.24), channel_id=1, source_target_pairs={{0,4},{4,8},{8,12},{12,0},{1,5},{5,9},{9,13},{13,1},{2,6},{6,10},{... | collective-permute-start | bytes 159752 | tf_op jit(solution)/shard_map/ppermute | solution.py:307
  5.3 2.6 %collective-permute-start.1 = (bf16[208,128]{1,0:T(8,128)(2,1)S(1)}, bf16[208,128]{1,0:T(8,128)(2,1)S(1)}, u32[]{:S(2)}, u32[]{:S(2)}) collective-permute-start(bf16[208,128]{1,0:T(8,128)(2,1)S(1)} %get-tuple-element.25), channel_id=1, source_target_pairs={{0,8},{4,12},{8,0},{12,4},{1,9},{5,13},{9,1},{13,5},{2,10},{6,14},... | collective-permute-start | bytes 159752 | tf_op jit(solution)/shard_map/ppermute | solution.py:307
  7.9 1.3 %collective-permute-start.2 = (bf16[208,128]{1,0:T(8,128)(2,1)S(1)}, bf16[208,128]{1,0:T(8,128)(2,1)S(1)}, u32[]{:S(2)}, u32[]{:S(2)}) collective-permute-start(bf16[208,128]{1,0:T(8,128)(2,1)S(1)} %get-tuple-element.26), channel_id=1, source_target_pairs={{0,12},{4,0},{8,4},{12,8},{1,13},{5,1},{9,5},{13,9},{2,14},{6,2},{... | collective-permute-start | bytes 159752 | tf_op jit(solution)/shard_map/ppermute | solution.py:307
  9.2 0.0 copy-done
  9.2 0.0 copy-done.1
  9.2 0.0 copy-done.2
  9.2 0.0 copy-done.3
  9.2 0.0 copy-done.4
  9.2 2.5 %own.1 = (f32[2,64,256]{2,1,0:T(8,128)S(1)}, bf16[2,33,2,32,256]{4,3,2,1,0:T(8,128)(2,1)S(1)}) custom-call(s32[1,1,56]{2,1,0:T(1,128)S(1)} %copy-done.1, s32[1,1,56]{2,1,0:T(1,128)S(1)} %copy-done.2, s32[1,1,32]{2,1,0:T(1,128)S(1)} %copy-done.4, bf16[256,256]{1,0:T(8,128)(2,1)S(1)} %get-tuple-element.16.field, s32[32,128]{1,0:T(8,128)S(1)} %get-tuple-element.17.labels, ...), custom_call_target="tpu_custom_call" | custom-call | flops 3758096384 | bytes 3670016 | tf_op jit(solution)/shard_map/own/pallas_call | solution.py:310
  11.7 0.0 collective-permute-done.rest_0_
  11.7 0.2 %target_first.1.total = f32[2,64,256]{2,1,0:T(8,128)S(1)} custom-call(f32[2,64,256]{2,1,0:T(8,128)S(1)} %get-tuple-element.19.total, bf16[2,33,2,32,256]{4,3,2,1,0:T(8,128)(2,1)S(1)} %get-tuple-element.20.spread, bf16[208,128]{1,0:T(8,128)(2,1)S(1)} %collective-permute-done.rest_0_), custom_call_target="tpu_custom_call" | custom-call | tf_op jit(solution)/shard_map/target_first/pallas_call | solution.py:324
  12.0 0.0 collective-permute-done.1.rest_0_
  12.0 0.2 collective-permute-done.2.rest_1_
  12.1 0.3 %target_others.1 = bf16[64,256]{1,0:T(8,128)(2,1)S(1)} custom-call(f32[2,64,256]{2,1,0:T(8,128)S(1)} %target_first.1.total, bf16[2,33,2,32,256]{4,3,2,1,0:T(8,128)(2,1)S(1)} %get-tuple-element.20.spread, bf16[208,128]{1,0:T(8,128)(2,1)S(1)} %collective-permute-done.1.rest_0_, bf16[208,128]{1,0:T(8,128)(2,1)S(1)} %collective-permute-done.2.rest_1_), custom_call_target="tpu_custom_call" | custom-call | tf_op jit(solution)/shard_map/target_others/pallas_call | solution.py:334
  12.4 1.7 %collective-permute-start.3 = (bf16[64,256]{1,0:T(8,128)(2,1)S(1)}, bf16[64,256]{1,0:T(8,128)(2,1)S(1)}, u32[]{:S(2)}, u32[]{:S(2)}) collective-permute-start(bf16[64,256]{1,0:T(8,128)(2,1)S(1)} %target_others.1), channel_id=1, source_target_pairs={{0,2},{2,0},{1,3},{3,1},{4,6},{6,4},{5,7},{7,5},{8,10},{10,8},{9,1... | collective-permute-start | bytes 98312 | tf_op jit(solution)/shard_map/ppermute | solution.py:347
  14.1 0.3 %target_mine.1 = f32[2,32,256]{2,1,0:T(8,128)S(1)} custom-call(f32[2,64,256]{2,1,0:T(8,128)S(1)} %target_first.1.total, bf16[2,33,2,32,256]{4,3,2,1,0:T(8,128)(2,1)S(1)} %get-tuple-element.20.spread, bf16[208,128]{1,0:T(8,128)(2,1)S(1)} %collective-permute-done.1.rest_0_, bf16[208,128]{1,0:T(8,128)(2,1)S(1)} %collective-permute-done.2.rest_1_), custom_call_target="tpu_custom_call" | custom-call | tf_op jit(solution)/shard_map/target_mine/pallas_call | solution.py:334
  14.4 2.0 %collective-permute-done.3 = bf16[64,256]{1,0:T(8,128)(2,1)S(1)} collective-permute-done((bf16[64,256]{1,0:T(8,128)(2,1)S(1)}, bf16[64,256]{1,0:T(8,128)(2,1)S(1)}, u32[]{:S(2)}, u32[]{:S(2)}) %collective-permute-start.3) | collective-permute-done | bytes 32800 | tf_op jit(solution)/shard_map/ppermute | solution.py:347
  16.4 0.6 %convert_add_fusion = f32[2,32,256]{2,1,0:T(8,128)} fusion(f32[2,32,256]{2,1,0:T(8,128)S(1)} %target_mine.1, bf16[2,32,256]{2,1,0:T(8,128)(2,1)S(1)} %bitcast.2), kind=kLoop, calls=%fused_computation | loop fusion | flops 32768 | bytes 163840 | tf_op jit(solution)/shard_map/add | solution.py:352
  (1 shorter events, 0.0 us)
Async XLA Ops:
  2.1 7.1 %copy-start = (bf16[1,1,56,2,128,128]{5,4,3,2,1,0:T(8,128)(2,1)S(1)}, bf16[1,1,56,2,128,128]{5,4,3,2,1,0:T(8,128)(2,1)}, u32[]{:S(2)}) copy-start(bf16[1,1,56,2,128,128]{5,4,3,2,1,0:T(8,128)(2,1)} %near_blocks.3) | copy-start | bytes 11010052
  2.1 7.1 %copy-start.1 = (s32[1,1,56]{2,1,0:T(1,128)S(1)}, s32[1,1,56]{2,1,0:T(1,128)}, u32[]{:S(2)}) copy-start(s32[1,1,56]{2,1,0:T(1,128)} %near_src.3) | copy-start | bytes 676
  2.1 7.1 %copy-start.2 = (s32[1,1,56]{2,1,0:T(1,128)S(1)}, s32[1,1,56]{2,1,0:T(1,128)}, u32[]{:S(2)}) copy-start(s32[1,1,56]{2,1,0:T(1,128)} %near_tgt.3) | copy-start | bytes 676
  2.2 7.1 %copy-start.3 = (bf16[1,1,32,2,32,128]{5,4,3,2,1,0:T(8,128)(2,1)S(1)}, bf16[1,1,32,2,32,128]{5,4,3,2,1,0:T(8,128)(2,1)}, u32[]{:S(2)}) copy-start(bf16[1,1,32,2,32,128]{5,4,3,2,1,0:T(8,128)(2,1)} %far_u.1) | copy-start | bytes 1572868
  2.2 7.1 %copy-start.4 = (s32[1,1,32]{2,1,0:T(1,128)S(1)}, s32[1,1,32]{2,1,0:T(1,128)}, u32[]{:S(2)}) copy-start(s32[1,1,32]{2,1,0:T(1,128)} %far_tgt.1) | copy-start | bytes 388
  2.2 9.5 %collective-permute-start = (bf16[208,128]{1,0:T(8,128)(2,1)S(1)}, bf16[208,128]{1,0:T(8,128)(2,1)S(1)}, u32[]{:S(2)}, u32[]{:S(2)}) collective-permute-start(bf16[208,128]{1,0:T(8,128)(2,1)S(1)} %get-tuple-element.24), channel_id=1, source_target_pairs={{0,4},{4,8},{8,12},{12,0},{1,5},{5,9},{9,13},{13,1},{2,6},{6,10},{... | collective-permute-start | bytes 159752 | tf_op jit(solution)/shard_map/ppermute | solution.py:307
  5.3 6.7 %collective-permute-start.1 = (bf16[208,128]{1,0:T(8,128)(2,1)S(1)}, bf16[208,128]{1,0:T(8,128)(2,1)S(1)}, u32[]{:S(2)}, u32[]{:S(2)}) collective-permute-start(bf16[208,128]{1,0:T(8,128)(2,1)S(1)} %get-tuple-element.25), channel_id=1, source_target_pairs={{0,8},{4,12},{8,0},{12,4},{1,9},{5,13},{9,1},{13,5},{2,10},{6,14},... | collective-permute-start | bytes 159752 | tf_op jit(solution)/shard_map/ppermute | solution.py:307
  7.9 4.3 %collective-permute-start.2 = (bf16[208,128]{1,0:T(8,128)(2,1)S(1)}, bf16[208,128]{1,0:T(8,128)(2,1)S(1)}, u32[]{:S(2)}, u32[]{:S(2)}) collective-permute-start(bf16[208,128]{1,0:T(8,128)(2,1)S(1)} %get-tuple-element.26), channel_id=1, source_target_pairs={{0,12},{4,0},{8,4},{12,8},{1,13},{5,1},{9,5},{13,9},{2,14},{6,2},{... | collective-permute-start | bytes 159752 | tf_op jit(solution)/shard_map/ppermute | solution.py:307
  12.4 4.0 %collective-permute-start.3 = (bf16[64,256]{1,0:T(8,128)(2,1)S(1)}, bf16[64,256]{1,0:T(8,128)(2,1)S(1)}, u32[]{:S(2)}, u32[]{:S(2)}) collective-permute-start(bf16[64,256]{1,0:T(8,128)(2,1)S(1)} %target_others.1), channel_id=1, source_target_pairs={{0,2},{2,0},{1,3},{3,1},{4,6},{6,4},{5,7},{7,5},{8,10},{10,8},{9,1... | collective-permute-start | bytes 98312 | tf_op jit(solution)/shard_map/ppermute | solution.py:347

commit v8 on v7

--- a/solution.py
+++ b/solution.py
@@ -10,7 +10,7 @@
 PANEL = 128
 LANES = 128
 LIMIT = 24 << 20
-LATE = 2
+LATE = 1
 HAND_ON_FLOPS = 2 * 10**9
 VMEM = pl.BlockSpec(memory_space=pltpu.VMEM)
 SMEM = pl.BlockSpec(memory_space=pltpu.SMEM)
@@ -32,6 +32,12 @@
     return -(-(depth + 1) // 16) * 16
 
 
+def ring_place(owner, owners):
+    if owners != 4:
+        return owner
+    return (owner & 1) * 2 + (owner >= 2) * 1
+
+
 def wrap(value, size):
     if size & (size - 1) == 0:
         return value & (size - 1)
@@ -47,11 +53,11 @@
 
 
 def send_kernel(owners, depth, far_src, far_dst, near_src, near_tgt, incident, far_v, near_blocks,
-                field, labels, own_coeffs, *rest):
+                field, labels, own_coeffs, tgt_row, src_row, *rest):
     messages, rest = rest[:owners - 1], rest[owners - 1:]
-    src_f, dst_f, tgt_row, src_row, waves, factors, picked, ordered, source_of, counts, sems, pick_sem = rest
+    src_f, dst_f, waves, factors, picked, ordered, source_of, counts, sems, pick_sem = rest
     coeffs = (own_coeffs,) + messages
-    me = lax.axis_index("src")
+    my_place = ring_place(lax.axis_index("src"), owners)
     half = waves.shape[1]
     rows = 2 * half
     clusters = waves.shape[2] // PANEL
@@ -75,7 +81,7 @@
     targets = tgt_row[0]
     position = lax.broadcasted_iota(jnp.int32, targets.shape, 1)
     line = lax.broadcasted_iota(jnp.int32, (-(-2 * (owners - 1) // 8) * 8, 1), 0)
-    low = wrap(me + 1 + line // 2, owners) * clusters
+    low = ring_place(wrap(my_place + 1 + line // 2, owners), owners) * clusters
     aimed = (targets >= low) & (targets < low + clusters)
     found = jnp.where(line % 2 == 0, count - 1 - position, position)
     found = (found * clusters + src_row[0]) * clusters + targets - low
@@ -112,7 +118,7 @@
         routed = dst_f[0, 0, f]
         owner = div_by(routed, blocks)
         slot = routed - owner * blocks
-        ahead = wrap(owner - me, owners)
+        ahead = wrap(ring_place(owner, owners) - my_place, owners)
         if packed:
             shift = ahead * 8
             taken = lax.shift_right_logical(so_far, shift) & 255
@@ -273,15 +279,14 @@
 
     near_count = near_blocks.shape[2]
     message_shape = shape(((chunks + 1) * rows + label_count(depth), LANES), bf16)
-    field, labels, own_coeffs, *messages = pl.pallas_call(
+    field, labels, own_coeffs, tgt_row, src_row, *messages = pl.pallas_call(
         functools.partial(send_kernel, owners, depth),
         out_shape=[shape((clusters * rows, 2 * PANEL), bf16), shape((owners * depth, LANES), i32), shape((chunks * rows, LANES), bf16)]
-        + [message_shape] * (owners - 1),
+        + [shape(near_tgt.shape, i32), shape(near_src.shape, i32)] + [message_shape] * (owners - 1),
         in_specs=[HBM] * 7,
-        out_specs=[VMEM] * (2 + owners),
+        out_specs=[VMEM] * (4 + owners),
         scratch_shapes=[
             pltpu.SMEM(far_src.shape, i32), pltpu.SMEM(far_dst.shape, i32),
-            pltpu.VMEM(near_tgt.shape, i32), pltpu.VMEM(near_src.shape, i32),
             pltpu.VMEM(incident.shape, bf16),
             pltpu.VMEM(far_v.shape, bf16),
             pltpu.VMEM((2 * (owners - 1),) + near_blocks.shape[3:], bf16),
@@ -303,10 +308,10 @@
         cost_estimate=pl.CostEstimate(flops=HAND_ON_FLOPS, bytes_accessed=0, transcendentals=0),
         name="hand_on",
     )(*messages)
-    arrived = [
-        lax.ppermute(message, "src", [(s, (s + k) % owners) for s in range(owners)])
-        for k, message in enumerate(messages, 1)
-    ]
+    arrived = []
+    for k in (1, 3, 2) if owners == 4 else range(1, owners):
+        pairs = [(s, ring_place((ring_place(s, owners) + k) % owners, owners)) for s in range(owners)]
+        arrived.append(lax.ppermute(messages[k - 1], "src", pairs))
     total, spread = pl.pallas_call(
         functools.partial(own_kernel, depth, used),
         out_shape=[shape((sharers, rows, width), f32), shape((sharers, blocks + 1, 2, rank, width), bf16)],
@@ -317,7 +322,7 @@
         cost_estimate=pl.CostEstimate(
             flops=64 * near_count * rows * PANEL * PANEL, bytes_accessed=near_count * 4 * PANEL * PANEL, transcendentals=0),
         name="own",
-    )(near_src, near_tgt, far_tgt, field, labels, own_coeffs, far_u, near_blocks)
+    )(src_row, tgt_row, far_tgt, field, labels, own_coeffs, far_u, near_blocks)
 
     late = min(LATE, len(arrived))
     if late < len(arrived):

time: 17.2 us -> 17 us (0.988)
  starting transfers between devices: 8.71 us -> 7.23 us
  waiting for transfers between devices: 2.18 us -> 3.61 us
    ppermute x3, starting transfers between devices: 7 us -> 5.67 us  [body(): arrived.append(lax.ppermute(messages[k - 1], 'src', pairs))]
    ppermute x3, waiting for transfers between devices: 0.17 us -> 1.4 us  [body(): arrived.append(lax.ppermute(messages[k - 1], 'src', pairs))]
    ppermute x1, waiting for transfers between devices: 2.01 us -> 2.21 us  [body(): lax.ppermute(other, 'tgt', [(t, (t + k) % sharers) for t in range(sharers)])]
  transfers between devices with their start and end apart: 4 -> 4, of which waited for: 2 -> 3; matrix products, arithmetic and copies ran while one was open for 0% -> 0% of each run, Pallas kernels for 17% -> 18%
where the time goes in v8:
time: 17 us; the launch traced here: 16.9 us
  starting transfers between devices  7.23 us (43%)
  Pallas kernels  5.29 us (31%)
  waiting for transfers between devices  3.61 us (21%)
  other arithmetic  0.64 us (4%)
    ppermute x3, starting transfers between devices, body(): arrived.append(lax.ppermute(messages[k - 1], 'src', pairs))  5.67 us
    pallas_call x1, Pallas kernels, body(): pl.pallas_call(functools.partial(own_kernel, depth, used), out_shape=[sha...  2.42 us
    ppermute x1, waiting for transfers between devices, body(): lax.ppermute(other, 'tgt', [(t, (t + k) % sharers) for t in range(sharers)])  2.21 us
    pallas_call x1, Pallas kernels, body(): pl.pallas_call(functools.partial(send_kernel, owners, depth), out_shape=[...  2.11 us
    ppermute x1, starting transfers between devices, body(): lax.ppermute(other, 'tgt', [(t, (t + k) % sharers) for t in range(sharers)])  1.56 us
    ppermute x3, waiting for transfers between devices, body(): arrived.append(lax.ppermute(messages[k - 1], 'src', pairs))  1.4 us
    add x1, other arithmetic, body(): result = result + other.astype(f32).reshape(result.shape)  0.64 us
    pallas_call x2, Pallas kernels, target(): pl.pallas_call(functools.partial(last_target_kernel, depth, used, late, s...  0.42 us
  transfers between devices with their start and end apart: 4, of which 3 were waited for; matrix products, arithmetic and copies ran while one was open for 0% of the time, Pallas kernels for 18%

profile of v8, /device:TPU:0, one launch (start us, length us, event | category | flops | bytes accessed | tf_op | source)
XLA Modules:
  0.0 16.9 jit_solution(5953686926675549861)
XLA Ops:
  0.0 2.1 %send.1 = (bf16[256,256]{1,0:T(8,128)(2,1)S(1)}, s32[32,128]{1,0:T(8,128)S(1)}, bf16[128,128]{1,0:T(8,128)(2,1)S(1)}, s32[1,1,56]{2,1,0:T(1,128)S(1)}, s32[1,1,5...) custom-call(s32[1,1,32]{2,1,0:T(1,128)} %far_src.1, ...), custom_call_target="tpu_custom_call" | custom-call | tf_op jit(solution)/shard_map/send/pallas_call | solution.py:282
  2.1 0.0 copy-start
  2.1 0.0 copy-start.1
  2.1 0.0 copy-start.2
  2.2 4.1 %collective-permute-start = (bf16[208,128]{1,0:T(8,128)(2,1)S(1)}, bf16[208,128]{1,0:T(8,128)(2,1)S(1)}, u32[]{:S(2)}, u32[]{:S(2)}) collective-permute-start(bf16[208,128]{1,0:T(8,128)(2,1)S(1)} %get-tuple-element.28), channel_id=1, source_target_pairs={{0,8},{4,12},{8,4},{12,0},{1,9},{5,13},{9,5},{13,1},{2,10},{6,14},... | collective-permute-start | bytes 159752 | tf_op jit(solution)/shard_map/ppermute | solution.py:314
  6.3 1.1 %collective-permute-start.1 = (bf16[208,128]{1,0:T(8,128)(2,1)S(1)}, bf16[208,128]{1,0:T(8,128)(2,1)S(1)}, u32[]{:S(2)}, u32[]{:S(2)}) collective-permute-start(bf16[208,128]{1,0:T(8,128)(2,1)S(1)} %get-tuple-element.29), channel_id=1, source_target_pairs={{0,12},{4,8},{8,0},{12,4},{1,13},{5,9},{9,1},{13,5},{2,14},{6,10},... | collective-permute-start | bytes 159752 | tf_op jit(solution)/shard_map/ppermute | solution.py:314
  7.3 0.5 %collective-permute-start.2 = (bf16[208,128]{1,0:T(8,128)(2,1)S(1)}, bf16[208,128]{1,0:T(8,128)(2,1)S(1)}, u32[]{:S(2)}, u32[]{:S(2)}) collective-permute-start(bf16[208,128]{1,0:T(8,128)(2,1)S(1)} %get-tuple-element.30), channel_id=1, source_target_pairs={{0,4},{4,0},{8,12},{12,8},{1,5},{5,1},{9,13},{13,9},{2,6},{6,2},{1... | collective-permute-start | bytes 159752 | tf_op jit(solution)/shard_map/ppermute | solution.py:314
  7.8 0.0 copy-done
  7.9 0.0 copy-done.1
  7.9 0.0 copy-done.2
  7.9 2.4 %own.1 = (f32[2,64,256]{2,1,0:T(8,128)S(1)}, bf16[2,33,2,32,256]{4,3,2,1,0:T(8,128)(2,1)S(1)}) custom-call(s32[1,1,56]{2,1,0:T(1,128)S(1)} %get-tuple-element.18.near_src, s32[1,1,56]{2,1,0:T(1,128)S(1)} %get-tuple-element.19.near_tgt, s32[1,1,32]{2,1,0:T(1,128)S(1)} %copy-done.2, bf16[256,256]{1,0:T(8,128)(2,1)S(1)} %get-tuple-element.20.field, ...), custom_call_target="tpu_custom_call" | custom-call | flops 3758096384 | bytes 3670016 | tf_op jit(solution)/shard_map/own/pallas_call | solution.py:315
  10.3 0.0 collective-permute-done.rest_0_
  10.3 1.2 %collective-permute-done.1.rest_1_ = bf16[208,128]{1,0:T(8,128)(2,1)S(1)} collective-permute-done((bf16[208,128]{1,0:T(8,128)(2,1)S(1)}, bf16[208,128]{1,0:T(8,128)(2,1)S(1)}, u32[]{:S(2)}, u32[]{:S(2)}) %collective-permute-start.1) | collective-permute-done | bytes 53280 | tf_op jit(solution)/shard_map/ppermute | solution.py:314
  11.5 0.3 %target_first.1.total = f32[2,64,256]{2,1,0:T(8,128)S(1)} custom-call(f32[2,64,256]{2,1,0:T(8,128)S(1)} %get-tuple-element.23.total, bf16[2,33,2,32,256]{4,3,2,1,0:T(8,128)(2,1)S(1)} %get-tuple-element.24.spread, bf16[208,128]{1,0:T(8,128)(2,1)S(1)} %collective-permute-done.rest_0_, bf16[208,128]{1,0:T(8,128)(2,1)S(1)} %collective-permute-done.1.rest_1_), custom_call_target="tpu_custom_call" | custom-call | tf_op jit(solution)/shard_map/target_first/pallas_call | solution.py:329
  11.9 0.2 %collective-permute-done.2.rest_0_ = bf16[208,128]{1,0:T(8,128)(2,1)S(1)} collective-permute-done((bf16[208,128]{1,0:T(8,128)(2,1)S(1)}, bf16[208,128]{1,0:T(8,128)(2,1)S(1)}, u32[]{:S(2)}, u32[]{:S(2)}) %collective-permute-start.2) | collective-permute-done | bytes 53280 | tf_op jit(solution)/shard_map/ppermute | solution.py:314
  12.0 0.2 %target_others.1 = bf16[64,256]{1,0:T(8,128)(2,1)S(1)} custom-call(f32[2,64,256]{2,1,0:T(8,128)S(1)} %target_first.1.total, bf16[2,33,2,32,256]{4,3,2,1,0:T(8,128)(2,1)S(1)} %get-tuple-element.24.spread, bf16[208,128]{1,0:T(8,128)(2,1)S(1)} %collective-permute-done.2.rest_0_), custom_call_target="tpu_custom_call" | custom-call | tf_op jit(solution)/shard_map/target_others/pallas_call | solution.py:339
  12.2 1.6 %collective-permute-start.3 = (bf16[64,256]{1,0:T(8,128)(2,1)S(1)}, bf16[64,256]{1,0:T(8,128)(2,1)S(1)}, u32[]{:S(2)}, u32[]{:S(2)}) collective-permute-start(bf16[64,256]{1,0:T(8,128)(2,1)S(1)} %target_others.1), channel_id=1, source_target_pairs={{0,2},{2,0},{1,3},{3,1},{4,6},{6,4},{5,7},{7,5},{8,10},{10,8},{9,1... | collective-permute-start | bytes 98312 | tf_op jit(solution)/shard_map/ppermute | solution.py:352
  13.8 0.2 %target_mine.1 = f32[2,32,256]{2,1,0:T(8,128)S(1)} custom-call(f32[2,64,256]{2,1,0:T(8,128)S(1)} %target_first.1.total, bf16[2,33,2,32,256]{4,3,2,1,0:T(8,128)(2,1)S(1)} %get-tuple-element.24.spread, bf16[208,128]{1,0:T(8,128)(2,1)S(1)} %collective-permute-done.2.rest_0_), custom_call_target="tpu_custom_call" | custom-call | tf_op jit(solution)/shard_map/target_mine/pallas_call | solution.py:339
  14.0 2.2 %collective-permute-done.3 = bf16[64,256]{1,0:T(8,128)(2,1)S(1)} collective-permute-done((bf16[64,256]{1,0:T(8,128)(2,1)S(1)}, bf16[64,256]{1,0:T(8,128)(2,1)S(1)}, u32[]{:S(2)}, u32[]{:S(2)}) %collective-permute-start.3) | collective-permute-done | bytes 32800 | tf_op jit(solution)/shard_map/ppermute | solution.py:352
  16.2 0.6 %convert_add_fusion = f32[2,32,256]{2,1,0:T(8,128)} fusion(f32[2,32,256]{2,1,0:T(8,128)S(1)} %target_mine.1, bf16[2,32,256]{2,1,0:T(8,128)(2,1)S(1)} %bitcast.2), kind=kLoop, calls=%fused_computation | loop fusion | flops 32768 | bytes 163840 | tf_op jit(solution)/shard_map/add | solution.py:357
  (1 shorter events, 0.0 us)
Async XLA Ops:
  2.1 5.7 %copy-start = (bf16[1,1,56,2,128,128]{5,4,3,2,1,0:T(8,128)(2,1)S(1)}, bf16[1,1,56,2,128,128]{5,4,3,2,1,0:T(8,128)(2,1)}, u32[]{:S(2)}) copy-start(bf16[1,1,56,2,128,128]{5,4,3,2,1,0:T(8,128)(2,1)} %near_blocks.3) | copy-start | bytes 11010052
  2.1 5.7 %copy-start.1 = (bf16[1,1,32,2,32,128]{5,4,3,2,1,0:T(8,128)(2,1)S(1)}, bf16[1,1,32,2,32,128]{5,4,3,2,1,0:T(8,128)(2,1)}, u32[]{:S(2)}) copy-start(bf16[1,1,32,2,32,128]{5,4,3,2,1,0:T(8,128)(2,1)} %far_u.1) | copy-start | bytes 1572868
  2.1 5.7 %copy-start.2 = (s32[1,1,32]{2,1,0:T(1,128)S(1)}, s32[1,1,32]{2,1,0:T(1,128)}, u32[]{:S(2)}) copy-start(s32[1,1,32]{2,1,0:T(1,128)} %far_tgt.1) | copy-start | bytes 388
  2.2 8.1 %collective-permute-start = (bf16[208,128]{1,0:T(8,128)(2,1)S(1)}, bf16[208,128]{1,0:T(8,128)(2,1)S(1)}, u32[]{:S(2)}, u32[]{:S(2)}) collective-permute-start(bf16[208,128]{1,0:T(8,128)(2,1)S(1)} %get-tuple-element.28), channel_id=1, source_target_pairs={{0,8},{4,12},{8,4},{12,0},{1,9},{5,13},{9,5},{13,1},{2,10},{6,14},... | collective-permute-start | bytes 159752 | tf_op jit(solution)/shard_map/ppermute | solution.py:314
  6.3 5.2 %collective-permute-start.1 = (bf16[208,128]{1,0:T(8,128)(2,1)S(1)}, bf16[208,128]{1,0:T(8,128)(2,1)S(1)}, u32[]{:S(2)}, u32[]{:S(2)}) collective-permute-start(bf16[208,128]{1,0:T(8,128)(2,1)S(1)} %get-tuple-element.29), channel_id=1, source_target_pairs={{0,12},{4,8},{8,0},{12,4},{1,13},{5,9},{9,1},{13,5},{2,14},{6,10},... | collective-permute-start | bytes 159752 | tf_op jit(solution)/shard_map/ppermute | solution.py:314
  7.3 4.7 %collective-permute-start.2 = (bf16[208,128]{1,0:T(8,128)(2,1)S(1)}, bf16[208,128]{1,0:T(8,128)(2,1)S(1)}, u32[]{:S(2)}, u32[]{:S(2)}) collective-permute-start(bf16[208,128]{1,0:T(8,128)(2,1)S(1)} %get-tuple-element.30), channel_id=1, source_target_pairs={{0,4},{4,0},{8,12},{12,8},{1,5},{5,1},{9,13},{13,9},{2,6},{6,2},{1... | collective-permute-start | bytes 159752 | tf_op jit(solution)/shard_map/ppermute | solution.py:314
  12.2 4.0 %collective-permute-start.3 = (bf16[64,256]{1,0:T(8,128)(2,1)S(1)}, bf16[64,256]{1,0:T(8,128)(2,1)S(1)}, u32[]{:S(2)}, u32[]{:S(2)}) collective-permute-start(bf16[64,256]{1,0:T(8,128)(2,1)S(1)} %target_others.1), channel_id=1, source_target_pairs={{0,2},{2,0},{1,3},{3,1},{4,6},{6,4},{5,7},{7,5},{8,10},{10,8},{9,1... | collective-permute-start | bytes 98312 | tf_op jit(solution)/shard_map/ppermute | solution.py:352
